TPU v7x, 512 devices: a whole 4x4x16 slice. The times are simulated.
512 devices in a mesh: blk: 32 (over x_lo, z), grp: 16 (over x_hi, y, core).
Axes of the slice: x: 4 (x_hi: 2, x_lo: 2; x = x_hi * 2 + x_lo), y: 4, z: 16, core: 2. Of those that a mesh axis runs over, the one named last changes fastest.
Arguments:
- image_emb: bfloat16 [57344, 1152], P(('blk', 'grp')), may hold values from -0.625 to 0.625
- text_held: bfloat16 [57344, 1152], P(('blk', 'grp')), may hold values from -0.625 to 0.625
- text_grad_acc: float32 [57344, 1152], P(('blk', 'grp')), may hold values from -6 to 6
- text_loss_acc: float32 [57344], P(('blk', 'grp')), may hold values from 0 to 2
- match: int32 [57344], P('blk'), may hold values from 0 to 57343, each once
- step: int32 [1], replicated, may hold values from 0 to 999999
- scale: float32 [1], replicated, may hold values from 6 to 14
- bias: float32 [1], replicated, may hold values from -6 to -3
Outputs:
- image_grad: float32 [57344, 1152], P(('blk', 'grp'))
- text_grad_out: float32 [57344, 1152], P(('blk', 'grp'))
- text_loss_out: float32 [57344], P(('blk', 'grp'))
Inputs may be any that keep to these rules, and one draw needn't show every extreme that they name: match holds every text index exactly once.
All inputs are finite; a program needn't handle non-finite values.
Results may differ from a plain program's by a relative error of at most 0.014.
Values may be sent and summed in bfloat16 or wider, within the bound.
No kernel may reach another device: no remote copies, remote signals or barrier semaphores. Data moves between devices by JAX's collectives and lax.ppermute only.
A program may use at most 64 MiB of HBM per device.

v0:
```python
import jax
import jax.numpy as jnp
from jax import lax
from jax.sharding import PartitionSpec as P


def from_behind(block, axis, distance):
    devices = range(lax.axis_size(axis))
    route = [((i - distance) % len(devices), i) for i in devices]
    return lax.ppermute(block, axis, route)


def pair_terms(texts, columns, images, labels, factor, offset):
    product = lax.dot_general(
        texts, images, (((1,), (1,)), ((), ())), preferred_element_type=jnp.float32
    )
    logits = factor * product + offset
    paired = columns[:, None] == labels[None, :]
    signs = jnp.where(paired, 1.0, -1.0)
    lost = jnp.sum(jax.nn.softplus(-signs * logits), axis=1)
    weights = (jax.nn.sigmoid(logits) - paired.astype(jnp.float32)).astype(jnp.bfloat16)
    return (weights, lost)


def image_part_of(weights, texts):
    return lax.dot_general(
        weights, texts, (((0,), (0,)), ((), ())), preferred_element_type=jnp.float32
    )


def on_device(image_emb, text_held, text_grad_acc, text_loss_acc, match, step, scale, bias):
    rows = text_held.shape[0]
    nblk = lax.axis_size("blk")
    ngrp = lax.axis_size("grp")
    span = ngrp * rows
    here = lax.axis_index("blk")
    member = lax.axis_index("grp")
    factor = scale[0]
    offset = bias[0]
    offsets = jnp.arange(rows, dtype=jnp.int32)
    first_cols = jnp.mod(here - step[0], nblk) * span + member * rows + offsets
    second_cols = jnp.mod(here - step[0] - 1, nblk) * span + member * rows + offsets
    arrived = from_behind(text_held, "blk", 1)
    piece = lax.all_gather(image_emb, "grp", axis=0, tiled=True)
    weights_first, lost_first = pair_terms(text_held, first_cols, piece, match, factor, offset)
    weights_second, lost_second = pair_terms(arrived, second_cols, piece, match, factor, offset)
    grad_first = factor * jnp.dot(weights_first, piece, preferred_element_type=jnp.float32)
    grad_second = factor * jnp.dot(weights_second, piece, preferred_element_type=jnp.float32)
    partial_rows = factor * image_part_of(weights_first, text_held) + factor * image_part_of(
        weights_second, arrived
    )
    image_part = partial_rows
    image_part, grad_first, grad_second, loss_first, loss_second = (
        image_part,
        grad_first,
        grad_second,
        lost_first,
        lost_second,
    )
    image_grad = lax.psum_scatter(
        image_part.astype(jnp.bfloat16), "grp", scatter_dimension=0, tiled=True
    ).astype(jnp.float32)
    middle = text_grad_acc + grad_first
    middle_loss = text_loss_acc + loss_first / span
    sent_grad, sent_loss = (
        from_behind(middle.astype(jnp.bfloat16), "blk", 1).astype(middle.dtype),
        from_behind(middle_loss.astype(jnp.bfloat16), "blk", 1).astype(middle_loss.dtype),
    )
    text_grad_out = sent_grad + grad_second
    text_loss_out = sent_loss + loss_second / span
    return (image_grad, text_grad_out, text_loss_out)


def solution(mesh):
    placed = (
        P(("blk", "grp"), None),
        P(("blk", "grp"), None),
        P(("blk", "grp"), None),
        P(("blk", "grp")),
        P("blk"),
        P(),
        P(),
        P(),
    )
    return jax.shard_map(
        on_device,
        mesh=mesh,
        in_specs=placed,
        out_specs=(P(("blk", "grp"), None), P(("blk", "grp"), None), P(("blk", "grp"))),
        check_vma=False,
    )
```

profile of v0, /device:TPU:32, one launch (start us, length us, event | category | flops | bytes accessed | tf_op | source)
XLA Modules:
  0.0 206.0 jit_solution(693919743287472552)
XLA Ops:
  7.2 0.0 copy-start.2
  7.2 0.0 copy-start.3
  7.2 0.0 all-gather.2.cloned.1.call-start
  7.2 0.7 all-gather.2.cloned.1.call-update
  7.9 0.0 reduce-scatter.2.cloned.1.call-start
  8.0 3.8 %collective-permute-start = (bf16[112,1152]{1,0:T(8,128)(2,1)}, bf16[112,1152]{1,0:T(8,128)(2,1)S(1)}, u32[]{:S(2)}, u32[]{:S(2)}) collective-permute-start(bf16[112,1152]{1,0:T(8,128)(2,1)} %param.9), channel_id=1, source_target_pairs={{496,0},{0,16},{16,32},{32,48},{48,64},{64,80},{80,96},{96,112},{1... | collective-permute-start | bytes 774152 | tf_op jit(solution)/shard_map/ppermute | solution.py:10
  13.8 6.1 %collective-permute-done = bf16[112,1152]{1,0:T(8,128)(2,1)S(1)} collective-permute-done((bf16[112,1152]{1,0:T(8,128)(2,1)}, bf16[112,1152]{1,0:T(8,128)(2,1)S(1)}, u32[]{:S(2)}, u32[]{:S(2)}) %collective-permute-start) | collective-permute-done | bytes 258080 | tf_op jit(solution)/shard_map/ppermute | solution.py:10
  19.9 65.9 %all-gather.2.cloned.1.call-done = bf16[1792,1152]{1,0:T(8,128)(2,1)} async-done(((bf16[112,1152]{1,0:T(8,128)(2,1)}), bf16[1792,1152]{1,0:T(8,128)(2,1)}) %all-gather.2.cloned.1.call-update) | async-done | bytes 4128784 | tf_op jit(solution)/shard_map/all_gather | solution.py:44
  85.8 0.0 copy-start
  85.8 3.6 %fusion.3 = f32[112,1792]{1,0:T(8,128)S(1)} fusion(bf16[112,1152]{1,0:T(8,128)(2,1)S(1)} %collective-permute-done, bf16[1792,1152]{1,0:T(8,128)(2,1)} %all-gather.2.cloned.1.call-done, f32[]{:T(128)} %bitcast.18, f32[]{:T(128)} %bitcast.15), kind=kOutput, calls=%fused_computation.7 | convolution fusion | flops 462823424 | bytes 5189640 | tf_op jit(solution)/shard_map/dot_general | solution.py:14
  89.4 0.0 copy-done.2
  89.4 0.0 copy-done.3
  89.4 0.0 copy-done
  89.4 2.1 %fusion.14 = (f32[112]{0:T(128)S(1)}, f32[112]{0:T(128)S(1)}, f32[112,1792]{1,0:T(8,128)S(1)}) fusion(s32[1792]{0:T(1024)S(1)} %copy-done.3, s32[112]{0:T(128)S(1)} %get-tuple-element.7, f32[112,1792]{1,0:T(8,128)S(1)} %fusion.3, s32[112]{0:T(128)S(1)} %get-tuple-element.6, f32[]{:T(128)} %bitcast.17, bf16[112,1152]{1,0:T(8,128)(2,1)S(1)} %copy-done.2, ...), kind=kOutput, calls=%fused_computation.25 | convolution fusion | flops 467238656 | bytes 6001416 | tf_op jit(solution)/shard_map/dot_general | solution.py:14
  91.5 1.4 fusion.19
  92.8 3.3 %fusion.1 = bf16[1792,1152]{1,0:T(8,128)(2,1)} fusion(f32[1792,1152]{1,0:T(8,128)S(1)} %fusion.19, bf16[112,1152]{1,0:T(8,128)(2,1)S(1)} %collective-permute-done, f32[]{:T(128)} %bitcast.12, f32[112,1792]{1,0:T(8,128)S(1)} %fusion.3, s32[1792]{0:T(1024)S(1)} %copy-done.3, s32[112]{0:T(128)S(1)} %get-tuple-element.6), kind=kOutput, calls=%fused_computation.2 | convolution fusion | flops 470020096 | bytes 13454788 | tf_op jit(solution)/shard_map/dot_general | solution.py:26
  96.2 0.0 copy-start.4
  96.2 0.0 reduce-scatter.2.cloned.1.call-update
  96.2 0.0 copy-start.5
  96.2 0.0 copy-start.1
  96.2 1.0 copy-done.4
  97.2 3.4 %fusion.5 = bf16[112,1152]{1,0:T(8,128)(2,1)S(1)} fusion(f32[112,1152]{1,0:T(8,128)S(1)} %copy-done.4, bf16[1792,1152]{1,0:T(8,128)(2,1)} %all-gather.2.cloned.1.call-done, f32[]{:T(128)} %bitcast.14, f32[112,1792]{1,0:T(8,128)S(1)} %get-tuple-element.5, s32[1792]{0:T(1024)S(1)} %copy-done.3, s32[112]{0:T(128)S(1)} %get-tuple-element.7), kind=kOutput, calls=%fused_computation.12 | convolution fusion | flops 464214016 | bytes 5713348 | tf_op jit(solution)/shard_map/dot_general | solution.py:47
  100.6 3.5 %collective-permute-start.1 = (bf16[112,1152]{1,0:T(8,128)(2,1)S(1)}, bf16[112,1152]{1,0:T(8,128)(2,1)S(1)}, u32[]{:S(2)}, u32[]{:S(2)}) collective-permute-start(bf16[112,1152]{1,0:T(8,128)(2,1)S(1)} %fusion.5), channel_id=1, source_target_pairs={{496,0},{0,16},{16,32},{32,48},{48,64},{64,80},{80,96},{96,112},{1... | collective-permute-start | bytes 774152 | tf_op jit(solution)/shard_map/ppermute | solution.py:10
  104.1 0.0 copy-done.5
  104.1 3.5 %collective-permute-start.2 = (bf16[112]{0:T(256)(128)(2,1)S(1)}, bf16[112]{0:T(256)(128)(2,1)S(1)}, u32[]{:S(2)}, u32[]{:S(2)}) collective-permute-start(bf16[112]{0:T(256)(128)(2,1)S(1)} %add_convert_fusion), channel_id=1, source_target_pairs={{496,0},{0,16},{16,32},{32,48},{48,64},{64,80},{80,96},{96,112},{1... | collective-permute-start | bytes 680 | tf_op jit(solution)/shard_map/ppermute | solution.py:10
  107.6 3.4 %collective-permute-done.2 = bf16[112]{0:T(256)(128)(2,1)S(1)} collective-permute-done((bf16[112]{0:T(256)(128)(2,1)S(1)}, bf16[112]{0:T(256)(128)(2,1)S(1)}, u32[]{:S(2)}, u32[]{:S(2)}) %collective-permute-start.2) | collective-permute-done | bytes 256 | tf_op jit(solution)/shard_map/ppermute | solution.py:10
  111.0 0.5 multiply_add_fusion
  111.5 0.0 collective-permute-done.1
  111.5 0.0 copy-done.1
  111.5 1.7 convert_add_fusion
  113.2 84.2 %reduce-scatter.2.cloned.1.call-done = bf16[112,1152]{1,0:T(8,128)(2,1)} async-done(((bf16[1792,1152]{1,0:T(8,128)(2,1)}), bf16[112,1152]{1,0:T(8,128)(2,1)}) %reduce-scatter.2.cloned.1.call-update) | async-done | bytes 258064 | tf_op jit(solution)/shard_map/reduce_scatter | solution.py:60
  197.4 1.8 convert_element_type.35
  (2 shorter events, 0.0 us)
Async XLA Ops:
  7.2 82.2 %copy-start.2 = (bf16[112,1152]{1,0:T(8,128)(2,1)S(1)}, bf16[112,1152]{1,0:T(8,128)(2,1)}, u32[]{:S(2)}) copy-start(bf16[112,1152]{1,0:T(8,128)(2,1)} %param.9) | copy-start | bytes 774148
  7.2 82.2 %copy-start.3 = (s32[1792]{0:T(1024)S(1)}, s32[1792]{0:T(1024)}, u32[]{:S(2)}) copy-start(s32[1792]{0:T(1024)} %param.12) | copy-start | bytes 21508
  7.2 78.6 %all-gather.2.cloned.1.call-start = ((), (), s32[]{:S(2)}) async-start(), calls=%async_computation.1 | async-start | bytes 4386816 | tf_op jit(solution)/shard_map/all_gather | solution.py:44
  7.9 189.5 %reduce-scatter.2.cloned.1.call-start = ((), (), s32[]{:S(2)}) async-start(), calls=%async_computation.2 | async-start | bytes 4386816 | tf_op jit(solution)/shard_map/reduce_scatter | solution.py:60
  8.0 11.9 %collective-permute-start = (bf16[112,1152]{1,0:T(8,128)(2,1)}, bf16[112,1152]{1,0:T(8,128)(2,1)S(1)}, u32[]{:S(2)}, u32[]{:S(2)}) collective-permute-start(bf16[112,1152]{1,0:T(8,128)(2,1)} %param.9), channel_id=1, source_target_pairs={{496,0},{0,16},{16,32},{32,48},{48,64},{64,80},{80,96},{96,112},{1... | collective-permute-start | bytes 774152 | tf_op jit(solution)/shard_map/ppermute | solution.py:10
  85.8 3.6 %copy-start = (bf16[1792,1152]{1,0:T(8,128)(2,1)S(1)}, bf16[1792,1152]{1,0:T(8,128)(2,1)}, u32[]{:S(2)}) copy-start(bf16[1792,1152]{1,0:T(8,128)(2,1)} %all-gather.2.cloned.1.call-done) | copy-start | bytes 12386308
  96.2 1.0 copy-start.4
  96.2 7.9 %copy-start.5 = (f32[112]{0:T(128)S(1)}, f32[112]{0:T(128)}, u32[]{:S(2)}) copy-start(f32[112]{0:T(128)} %param.11) | copy-start | bytes 1348
  96.2 15.3 %copy-start.1 = (bf16[1792,1152]{1,0:T(8,128)(2,1)S(1)}, bf16[1792,1152]{1,0:T(8,128)(2,1)}, u32[]{:S(2)}) copy-start(bf16[1792,1152]{1,0:T(8,128)(2,1)} %all-gather.2.cloned.1.call-done) | copy-start | bytes 12386308
  100.6 10.9 %collective-permute-start.1 = (bf16[112,1152]{1,0:T(8,128)(2,1)S(1)}, bf16[112,1152]{1,0:T(8,128)(2,1)S(1)}, u32[]{:S(2)}, u32[]{:S(2)}) collective-permute-start(bf16[112,1152]{1,0:T(8,128)(2,1)S(1)} %fusion.5), channel_id=1, source_target_pairs={{496,0},{0,16},{16,32},{32,48},{48,64},{64,80},{80,96},{96,112},{1... | collective-permute-start | bytes 774152 | tf_op jit(solution)/shard_map/ppermute | solution.py:10
  104.1 6.8 %collective-permute-start.2 = (bf16[112]{0:T(256)(128)(2,1)S(1)}, bf16[112]{0:T(256)(128)(2,1)S(1)}, u32[]{:S(2)}, u32[]{:S(2)}) collective-permute-start(bf16[112]{0:T(256)(128)(2,1)S(1)} %add_convert_fusion), channel_id=1, source_target_pairs={{496,0},{0,16},{16,32},{32,48},{48,64},{64,80},{80,96},{96,112},{1... | collective-permute-start | bytes 680 | tf_op jit(solution)/shard_map/ppermute | solution.py:10
Sparse Core Ops, SparseCore 0:
  11.3 74.4 all-gather.1
  96.3 101.0 reduce-scatter.1
where the time goes:
time: 206 us
  waiting for transfers between devices  160 us (78%)
  between operations  16.1 us (8%)
  matrix products  15.5 us (8%)
  starting transfers between devices  10.8 us (5%)
  other arithmetic  2.29 us (1%)
    reduce_scatter x1, waiting for transfers between devices, on_device(): lax.psum_scatter(image_part.astype(jnp.bfloat16), 'grp', scatter_dimensio...  84.2 us
    all_gather x1, waiting for transfers between devices, on_device(): piece = lax.all_gather(image_emb, 'grp', axis=0, tiled=True)  65.9 us
    ppermute x3, starting transfers between devices, from_behind(): return lax.ppermute(block, axis, route)  10.7 us
    ppermute x3, waiting for transfers between devices, from_behind(): return lax.ppermute(block, axis, route)  9.47 us
    dot_general x2, matrix products, pair_terms(): lax.dot_general(texts, images, (((1,), (1,)), ((), ())), preferred_elemen...  5.67 us
    dot_general x2, matrix products, image_part_of(): lax.dot_general(weights, texts, (((0,), (0,)), ((), ())), preferred_eleme...  4.68 us
  transfers between devices with their start and end apart: 5, of which 4 were waited for; matrix products, arithmetic and copies ran while one was open for 3% of the time, Pallas kernels for 0%

commit v1 on v0

v1 whole, which is shorter than its diff:
```python
import jax
import jax.numpy as jnp
from jax import lax
from jax.sharding import PartitionSpec as P


NBLK = 32
XH, Y, CORE = 2, 4, 2


def spot(xh, y, core):
    return (xh * Y + y) * CORE + core


def member_route(move):
    return [
        (spot(xh, y, c), spot(*move(xh, y, c)))
        for xh in range(XH)
        for y in range(Y)
        for c in range(CORE)
    ]


def across_x(xh, y, c):
    return (1 - xh, y, c)


def across_core(xh, y, c):
    return (xh, y, 1 - c)


def along_y(steps):
    return lambda xh, y, c: (xh, (y + steps) % Y, c)


def stay(xh, y, c):
    return (xh, y, c)


def to_member(block, move):
    return lax.ppermute(block, "grp", member_route(move))


def to_next_group(block, move):
    ngrp = XH * Y * CORE
    route = [
        (b * ngrp + s, ((b + 1) % NBLK) * ngrp + t)
        for b in range(NBLK)
        for s, t in member_route(move)
    ]
    return lax.ppermute(block, ("blk", "grp"), route)


def gather_y(block):
    groups = [[spot(xh, y, c) for y in range(Y)] for xh in range(XH) for c in range(CORE)]
    return lax.all_gather(block, "grp", axis_index_groups=groups, tiled=True)


def tile(texts, columns, images, labels, factor, offset):
    product = lax.dot_general(
        texts, images, (((1,), (1,)), ((), ())), preferred_element_type=jnp.float32
    )
    logits = factor * product + offset
    paired = columns[:, None] == labels[None, :]
    turned = jnp.where(paired, -logits, logits)
    lost = jnp.sum(jax.nn.softplus(turned), axis=1)
    sig = jax.nn.sigmoid(turned)
    weights = jnp.where(paired, -sig, sig).astype(jnp.bfloat16)
    return weights, lost


def on_device(image_emb, text_held, text_grad_acc, text_loss_acc, match, step, scale, bias):
    rows, width = text_held.shape
    ngrp = XH * Y * CORE
    span = ngrp * rows
    here = lax.axis_index("blk")
    member = lax.axis_index("grp")
    xh = member // (Y * CORE)
    y = (member // CORE) % Y
    core = member % CORE
    factor = scale[0]
    offset = bias[0]

    text_z = to_next_group(text_held, stay)
    text_d = to_next_group(text_held, across_x)
    text_x = to_member(text_held, across_x)
    images_own = gather_y(image_emb)
    images_other = to_member(images_own, across_core)

    texts = jnp.concatenate([text_held, text_x, text_z, text_d], axis=0)
    ids = jnp.arange(rows, dtype=jnp.int32)
    partner = member ^ (Y * CORE)
    first = jnp.mod(here - step[0], NBLK) * span
    second = jnp.mod(here - step[0] - 1, NBLK) * span
    columns = jnp.concatenate(
        [
            first + member * rows + ids,
            first + partner * rows + ids,
            second + member * rows + ids,
            second + partner * rows + ids,
        ]
    )
    labels = match.reshape(XH, Y, CORE, rows)
    labels = lax.dynamic_index_in_dim(labels, xh, 0, keepdims=False)
    labels_own = lax.dynamic_index_in_dim(labels, core, 1, keepdims=False).reshape(-1)
    labels_other = lax.dynamic_index_in_dim(labels, 1 - core, 1, keepdims=False).reshape(-1)

    w_own, lost_own = tile(texts, columns, images_own, labels_own, factor, offset)
    w_other, lost_other = tile(texts, columns, images_other, labels_other, factor, offset)
    lost = (lost_own + lost_other) / span

    def image_part(w):
        return factor * lax.dot_general(
            w, texts, (((0,), (0,)), ((), ())), preferred_element_type=jnp.float32
        )

    sent = to_member(image_part(w_other).astype(jnp.bfloat16), across_core)
    text_term = factor * (
        jnp.dot(w_own, images_own, preferred_element_type=jnp.float32)
        + jnp.dot(w_other, images_other, preferred_element_type=jnp.float32)
    )

    def packed(grad, loss):
        tail = jnp.zeros((16, width), jnp.bfloat16)
        tail = tail.at[0, :rows].set(loss.astype(jnp.bfloat16))
        return jnp.concatenate([grad.astype(jnp.bfloat16), tail], axis=0)

    def part(i):
        return text_term[i * rows : (i + 1) * rows], lost[i * rows : (i + 1) * rows]

    grad0, loss0 = part(0)
    from_z = to_next_group(packed(text_grad_acc + grad0, text_loss_acc + loss0), stay)
    from_d = to_next_group(packed(*part(1)), across_x)
    from_x = to_member(packed(*part(3)), across_x)

    image_sum = image_part(w_own) + sent.astype(jnp.float32)
    image_sum = image_sum.reshape(Y, rows, width)

    def block_for(steps):
        return lax.dynamic_index_in_dim(image_sum, (y + steps) % Y, 0, keepdims=False)

    image_grad = block_for(0)
    for steps in (1, 2, 3):
        moved = to_member(block_for(steps).astype(jnp.bfloat16), along_y(steps))
        image_grad = image_grad + moved.astype(jnp.float32)

    grad2, loss2 = part(2)
    text_grad_out = grad2
    text_loss_out = loss2
    for arrived in (from_z, from_d, from_x):
        text_grad_out = text_grad_out + arrived[:rows].astype(jnp.float32)
        text_loss_out = text_loss_out + arrived[rows, :rows].astype(jnp.float32)
    return (image_grad, text_grad_out, text_loss_out)


def solution(mesh):
    placed = (
        P(("blk", "grp"), None),
        P(("blk", "grp"), None),
        P(("blk", "grp"), None),
        P(("blk", "grp")),
        P("blk"),
        P(),
        P(),
        P(),
    )
    return jax.shard_map(
        on_device,
        mesh=mesh,
        in_specs=placed,
        out_specs=(P(("blk", "grp"), None), P(("blk", "grp"), None), P(("blk", "grp"))),
        check_vma=False,
    )
```

time: 206 us -> 79.8 us (0.39)
  the two profiles are of different devices: /device:TPU:32 before, /device:TPU:8 now
where the time goes in v1:
time: 79.8 us; the launch traced here: 79.1 us
  starting transfers between devices  40.9 us (51%)
  blocking collectives  15.4 us (19%)
  matrix products  8.82 us (11%)
  waiting for transfers between devices  6.78 us (8%)
  between operations  3.02 us (4%)
  other arithmetic  2.62 us (3%)
  local copies, waits for them, and re-layouts  1.58 us (2%)
    ppermute x7, starting transfers between devices, to_member(): return lax.ppermute(block, 'grp', member_route(move))  21.8 us
    ppermute x4, starting transfers between devices, to_next_group(): return lax.ppermute(block, ('blk', 'grp'), route)  19.1 us
    all_gather x1, blocking collectives, gather_y(): return lax.all_gather(block, 'grp', axis_index_groups=groups, tiled=True)  15.4 us
    ppermute x7, waiting for transfers between devices, to_member(): return lax.ppermute(block, 'grp', member_route(move))  6.77 us
    dot_general x2, matrix products, tile(): lax.dot_general(texts, images, (((1,), (1,)), ((), ())), preferred_elemen...  3.88 us
    dot_general x1, matrix products, on_device(): jnp.dot(w_other, images_other, preferred_element_type=jnp.float32)  2.19 us
    dot_general x2, matrix products, image_part(): lax.dot_general(w, texts, (((0,), (0,)), ((), ())), preferred_element_typ...  1.85 us
  transfers between devices with their start and end apart: 11, of which 3 were waited for; matrix products, arithmetic and copies ran while one was open for 9% of the time, Pallas kernels for 0%

profile of v1, /device:TPU:8, one launch (start us, length us, event | category | flops | bytes accessed | tf_op | source)
XLA Modules:
  0.0 79.1 jit_solution(9098088641596397267)
XLA Ops:
  0.6 4.9 %collective-permute-start = (bf16[112,1152]{1,0:T(8,128)(2,1)}, bf16[112,1152]{1,0:T(8,128)(2,1)S(1)}, u32[]{:S(2)}, u32[]{:S(2)}) collective-permute-start(bf16[112,1152]{1,0:T(8,128)(2,1)} %param.15), channel_id=1, source_target_pairs={{0,8},{1,9},{2,10},{3,11},{4,12},{5,13},{6,14},{7,15},{8,0},{9,1},... | collective-permute-start | bytes 774152 | tf_op jit(solution)/shard_map/ppermute | solution.py:41
  5.6 3.8 %collective-permute-start.1 = (bf16[112,1152]{1,0:T(8,128)(2,1)}, bf16[112,1152]{1,0:T(8,128)(2,1)S(1)}, u32[]{:S(2)}, u32[]{:S(2)}) collective-permute-start(bf16[112,1152]{1,0:T(8,128)(2,1)} %param.15), channel_id=1, source_target_pairs={{0,16},{1,17},{2,18},{3,19},{4,20},{5,21},{6,22},{7,23},{8,24},{9,... | collective-permute-start | bytes 774152 | tf_op jit(solution)/shard_map/ppermute | solution.py:51
  9.4 3.8 %collective-permute-start.2 = (bf16[112,1152]{1,0:T(8,128)(2,1)}, bf16[112,1152]{1,0:T(8,128)(2,1)S(1)}, u32[]{:S(2)}, u32[]{:S(2)}) collective-permute-start(bf16[112,1152]{1,0:T(8,128)(2,1)} %param.15), channel_id=1, source_target_pairs={{0,24},{1,25},{2,26},{3,27},{4,28},{5,29},{6,30},{7,31},{8,16},{9,... | collective-permute-start | bytes 774152 | tf_op jit(solution)/shard_map/ppermute | solution.py:51
  13.2 15.4 %all_gather.3 = bf16[448,1152]{1,0:T(8,128)(2,1)S(1)} all-gather(bf16[112,1152]{1,0:T(8,128)(2,1)} %param.14), channel_id=1, replica_groups={{0,2,4,6},{1,3,5,7},{8,10,12,14},{9,11,13,15},{16,18,20,22},{17,19,21,2..., dimensions={0}, use_global_device_ids=true | all-gather | bytes 1290240 | tf_op jit(solution)/shard_map/all_gather | solution.py:56
  28.6 1.9 %collective-permute-start.3 = (bf16[448,1152]{1,0:T(8,128)(2,1)S(1)}, bf16[448,1152]{1,0:T(8,128)(2,1)}, u32[]{:S(2)}, u32[]{:S(2)}) collective-permute-start(bf16[448,1152]{1,0:T(8,128)(2,1)S(1)} %all_gather.3), channel_id=1, source_target_pairs={{0,1},{1,0},{2,3},{3,2},{4,5},{5,4},{6,7},{7,6},{8,9},{9,8},{10,11... | collective-permute-start | bytes 3096584 | tf_op jit(solution)/shard_map/ppermute | solution.py:41
  31.2 1.0 %constant_dynamic-update-slice_fusion.3 = bf16[448,1152]{1,0:T(8,128)(2,1)S(1)} fusion(bf16[112,1152]{1,0:T(8,128)(2,1)} %param.15), kind=kLoop, calls=%fused_computation.44 | loop fusion | bytes 516096
  32.2 0.1 pad_add_fusion
  32.4 0.1 reshape.112
  32.5 0.1 eq.38
  33.9 0.1 eq.41
  34.1 1.3 %fusion.7 = (f32[448]{0:T(512)S(1)}, f32[448,448]{0,1:T(8,128)S(1)}) fusion(f32[]{:T(128)} %bitcast.61, bf16[448,1152]{1,0:T(8,128)(2,1)S(1)} %constant_dynamic-update-slice_fusion, bf16[448,1152]{1,0:T(8,128)(2,1)S(1)} %all_gather.3, f32[]{:T(128)} %bitcast.57, s32[448]{0:T(512)S(1)} %eq.38, s32[448]{0:T(512)S(1)} %pad_add_fusion), kind=kOutput, calls=%fused_computation.18 | convolution fusion | flops 464830016 | bytes 2872584 | tf_op jit(solution)/shard_map/dot_general | solution.py:60
  35.4 0.9 %fusion.31 = f32[448,1152]{1,0:T(8,128)S(1)} fusion(bf16[448,1152]{1,0:T(8,128)(2,1)S(1)} %all_gather.3, f32[448,448]{0,1:T(8,128)S(1)} %get-tuple-element.51, s32[448]{0:T(512)S(1)} %pad_add_fusion, s32[448]{0:T(512)S(1)} %eq.38), kind=kOutput, calls=%fused_computation.65 | convolution fusion | flops 463826944 | bytes 3902976 | tf_op jit(solution)/shard_map/dot_general | solution.py:119
  36.4 2.5 %fusion.8 = (f32[448]{0:T(512)S(1)}, f32[448,448]{0,1:T(8,128)S(1)}) fusion(f32[]{:T(128)} %bitcast.62, bf16[448,1152]{1,0:T(8,128)(2,1)S(1)} %constant_dynamic-update-slice_fusion, bf16[448,1152]{1,0:T(8,128)(2,1)} %collective-permute-done.3, f32[]{:T(128)} %bitcast.60, s32[448]{0:T(512)S(1)} %eq.41, s32[448]{0:T(512)S(1)} %pad_add_fusion), kind=kOutput, calls=%fused_computation.19 | convolution fusion | flops 464830016 | bytes 2872584 | tf_op jit(solution)/shard_map/dot_general | solution.py:60
  38.9 2.2 %fusion.36 = (bf16[448,1152]{1,0:T(8,128)(2,1)S(1)}, f32[448,1152]{1,0:T(8,128)S(1)}) fusion(f32[448,1152]{1,0:T(8,128)S(1)} %fusion.31, bf16[448,1152]{1,0:T(8,128)(2,1)} %collective-permute-done.3, f32[448,448]{0,1:T(8,128)S(1)} %get-tuple-element.53, s32[448]{0:T(512)S(1)} %pad_add_fusion, s32[448]{0:T(512)S(1)} %eq.41, f32[]{:T(128)} %bitcast.58), kind=kOutput, calls=%fused_computation.68 | convolution fusion | flops 465375232 | bytes 6999556 | tf_op jit(solution)/shard_map/dot_general | solution.py:120
  41.1 0.1 fusion.12
  41.3 3.8 %collective-permute-start.8 = (bf16[128,1152]{1,0:T(8,128)(2,1)S(1)}, bf16[128,1152]{1,0:T(8,128)(2,1)S(1)}, u32[]{:S(2)}, u32[]{:S(2)}) collective-permute-start(bf16[128,1152]{1,0:T(8,128)(2,1)S(1)} %fusion.17), channel_id=1, source_target_pairs={{0,16},{1,17},{2,18},{3,19},{4,20},{5,21},{6,22},{7,23},{8,24},{9,... | collective-permute-start | bytes 884744 | tf_op jit(solution)/shard_map/ppermute | solution.py:51
  45.1 0.9 %fusion.2 = bf16[448,1152]{1,0:T(8,128)(2,1)S(1)} fusion(bf16[448,1152]{1,0:T(8,128)(2,1)S(1)} %constant_dynamic-update-slice_fusion, f32[]{:T(128)} %bitcast.59, f32[448,448]{0,1:T(8,128)S(1)} %get-tuple-element.53, s32[448]{0:T(512)S(1)} %pad_add_fusion, s32[448]{0:T(512)S(1)} %eq.41), kind=kOutput, calls=%fused_computation.5 | convolution fusion | flops 464859136 | bytes 2870788 | tf_op jit(solution)/shard_map/dot_general | solution.py:113
  46.0 2.1 %collective-permute-start.4 = (bf16[448,1152]{1,0:T(8,128)(2,1)S(1)}, bf16[448,1152]{1,0:T(8,128)(2,1)S(1)}, u32[]{:S(2)}, u32[]{:S(2)}) collective-permute-start(bf16[448,1152]{1,0:T(8,128)(2,1)S(1)} %fusion.2), channel_id=1, source_target_pairs={{0,1},{1,0},{2,3},{3,2},{4,5},{5,4},{6,7},{7,6},{8,9},{9,8},{10,11... | collective-permute-start | bytes 3096584 | tf_op jit(solution)/shard_map/ppermute | solution.py:41
  48.2 0.1 slice_bitcast_fusion.4
  48.3 7.6 %collective-permute-start.9 = (bf16[128,1152]{1,0:T(8,128)(2,1)S(1)}, bf16[128,1152]{1,0:T(8,128)(2,1)S(1)}, u32[]{:S(2)}, u32[]{:S(2)}) collective-permute-start(bf16[128,1152]{1,0:T(8,128)(2,1)S(1)} %fusion.18), channel_id=1, source_target_pairs={{0,24},{1,25},{2,26},{3,27},{4,28},{5,29},{6,30},{7,31},{8,16},{9,... | collective-permute-start | bytes 884744 | tf_op jit(solution)/shard_map/ppermute | solution.py:51
  56.0 2.4 %collective-permute-start.10 = (bf16[128,1152]{1,0:T(8,128)(2,1)S(1)}, bf16[128,1152]{1,0:T(8,128)(2,1)S(1)}, u32[]{:S(2)}, u32[]{:S(2)}) collective-permute-start(bf16[128,1152]{1,0:T(8,128)(2,1)S(1)} %fusion.19), channel_id=1, source_target_pairs={{0,8},{1,9},{2,10},{3,11},{4,12},{5,13},{6,14},{7,15},{8,0},{9,1},... | collective-permute-start | bytes 884744 | tf_op jit(solution)/shard_map/ppermute | solution.py:41
  58.4 0.9 %fusion.1 = f32[448,1152]{1,0:T(8,128)S(1)} fusion(bf16[448,1152]{1,0:T(8,128)(2,1)S(1)} %constant_dynamic-update-slice_fusion, bf16[448,1152]{1,0:T(8,128)(2,1)S(1)} %collective-permute-done.4, f32[]{:T(128)} %bitcast.56, f32[448,448]{0,1:T(8,128)S(1)} %get-tuple-element.51, s32[448]{0:T(512)S(1)} %pad_add_fusion, s32[448]{0:T(512)S(1)} %eq.38), kind=kOutput, calls=%fused_computation.4 | convolution fusion | flops 465375232 | bytes 4935172 | tf_op jit(solution)/shard_map/dot_general | solution.py:113
  59.4 0.1 fusion.20
  59.5 1.9 %collective-permute-start.5 = (bf16[112,1152]{1,0:T(8,128)(2,1)S(1)}, bf16[112,1152]{1,0:T(8,128)(2,1)S(1)}, u32[]{:S(2)}, u32[]{:S(2)}) collective-permute-start(bf16[112,1152]{1,0:T(8,128)(2,1)S(1)} %get-tuple-element.43), channel_id=1, source_target_pairs={{0,2},{1,3},{2,4},{3,5},{4,6},{5,7},{6,0},{7,1},{8,10},{9,11},{10,... | collective-permute-start | bytes 774152 | tf_op jit(solution)/shard_map/ppermute | solution.py:41
  61.4 4.0 %collective-permute-start.6 = (bf16[112,1152]{1,0:T(8,128)(2,1)S(1)}, bf16[112,1152]{1,0:T(8,128)(2,1)S(1)}, u32[]{:S(2)}, u32[]{:S(2)}) collective-permute-start(bf16[112,1152]{1,0:T(8,128)(2,1)S(1)} %get-tuple-element.45), channel_id=1, source_target_pairs={{0,4},{1,5},{2,6},{3,7},{4,0},{5,1},{6,2},{7,3},{8,12},{9,13},{10,... | collective-permute-start | bytes 774152 | tf_op jit(solution)/shard_map/ppermute | solution.py:41
  65.5 4.5 %collective-permute-start.7 = (bf16[112,1152]{1,0:T(8,128)(2,1)S(1)}, bf16[112,1152]{1,0:T(8,128)(2,1)S(1)}, u32[]{:S(2)}, u32[]{:S(2)}) collective-permute-start(bf16[112,1152]{1,0:T(8,128)(2,1)S(1)} %get-tuple-element.44), channel_id=1, source_target_pairs={{0,6},{1,7},{2,0},{3,1},{4,2},{5,3},{6,4},{7,5},{8,14},{9,15},{10,... | collective-permute-start | bytes 774152 | tf_op jit(solution)/shard_map/ppermute | solution.py:41
  69.9 0.1 collective-permute-done.10
  70.0 0.9 %fusion.14 = f32[112,1152]{1,0:T(8,128)} fusion(f32[448,1152]{1,0:T(8,128)S(1)} %get-tuple-element.55, bf16[128,1152]{1,0:T(8,128)(2,1)S(1)} %collective-permute-done.10, bf16[128,1152]{1,0:T(8,128)(2,1)S(1)} %collective-permute-done.9, bf16[128,1152]{1,0:T(8,128)(2,1)S(1)} %collective-permute-done.8), kind=kLoop, calls=%fused_computation.28 | loop fusion | flops 774144 | bytes 1806336 | tf_op jit(solution)/shard_map/add | solution.py:151
  70.9 0.6 fusion.24
  71.5 2.5 %collective-permute-done.6 = bf16[112,1152]{1,0:T(8,128)(2,1)S(1)} collective-permute-done((bf16[112,1152]{1,0:T(8,128)(2,1)S(1)}, bf16[112,1152]{1,0:T(8,128)(2,1)S(1)}, u32[]{:S(2)}, u32[]{:S(2)}) %collective-permute-start.6) | collective-permute-done | bytes 258080 | tf_op jit(solution)/shard_map/ppermute | solution.py:41
  74.0 4.2 %collective-permute-done.7 = bf16[112,1152]{1,0:T(8,128)(2,1)S(1)} collective-permute-done((bf16[112,1152]{1,0:T(8,128)(2,1)S(1)}, bf16[112,1152]{1,0:T(8,128)(2,1)S(1)}, u32[]{:S(2)}, u32[]{:S(2)}) %collective-permute-start.7) | collective-permute-done | bytes 258080 | tf_op jit(solution)/shard_map/ppermute | solution.py:41
  78.2 0.9 %fusion.16 = f32[112,1152]{1,0:T(8,128)} fusion(bf16[112,1152]{1,0:T(8,128)(2,1)S(1)} %collective-permute-done.7, bf16[112,1152]{1,0:T(8,128)(2,1)S(1)} %collective-permute-done.6, bf16[112,1152]{1,0:T(8,128)(2,1)S(1)} %collective-permute-done.5, f32[4,112,1152]{2,1,0:T(8,128)S(1)} %bitcast.64, s32[]{:T(128)S(6)} %select_n.109), kind=kLoop, calls=%fused_computation.31 | loop fusion | flops 774144 | bytes 1806340 | tf_op jit(solution)/shard_map/add | solution.py:145
  (26 shorter events, 0.3 us)
Async XLA Ops:
  0.6 31.8 %copy-start.1 = (s32[1792]{0:T(1024)S(1)}, s32[1792]{0:T(1024)}, u32[]{:S(2)}) copy-start(s32[1792]{0:T(1024)} %param.18) | copy-start | bytes 21508
  0.6 33.3 %collective-permute-start = (bf16[112,1152]{1,0:T(8,128)(2,1)}, bf16[112,1152]{1,0:T(8,128)(2,1)S(1)}, u32[]{:S(2)}, u32[]{:S(2)}) collective-permute-start(bf16[112,1152]{1,0:T(8,128)(2,1)} %param.15), channel_id=1, source_target_pairs={{0,8},{1,9},{2,10},{3,11},{4,12},{5,13},{6,14},{7,15},{8,0},{9,1},... | collective-permute-start | bytes 774152 | tf_op jit(solution)/shard_map/ppermute | solution.py:41
  5.6 28.4 %collective-permute-start.1 = (bf16[112,1152]{1,0:T(8,128)(2,1)}, bf16[112,1152]{1,0:T(8,128)(2,1)S(1)}, u32[]{:S(2)}, u32[]{:S(2)}) collective-permute-start(bf16[112,1152]{1,0:T(8,128)(2,1)} %param.15), channel_id=1, source_target_pairs={{0,16},{1,17},{2,18},{3,19},{4,20},{5,21},{6,22},{7,23},{8,24},{9,... | collective-permute-start | bytes 774152 | tf_op jit(solution)/shard_map/ppermute | solution.py:51
  9.4 24.6 %collective-permute-start.2 = (bf16[112,1152]{1,0:T(8,128)(2,1)}, bf16[112,1152]{1,0:T(8,128)(2,1)S(1)}, u32[]{:S(2)}, u32[]{:S(2)}) collective-permute-start(bf16[112,1152]{1,0:T(8,128)(2,1)} %param.15), channel_id=1, source_target_pairs={{0,24},{1,25},{2,26},{3,27},{4,28},{5,29},{6,30},{7,31},{8,16},{9,... | collective-permute-start | bytes 774152 | tf_op jit(solution)/shard_map/ppermute | solution.py:51
  28.6 7.7 %collective-permute-start.3 = (bf16[448,1152]{1,0:T(8,128)(2,1)S(1)}, bf16[448,1152]{1,0:T(8,128)(2,1)}, u32[]{:S(2)}, u32[]{:S(2)}) collective-permute-start(bf16[448,1152]{1,0:T(8,128)(2,1)S(1)} %all_gather.3), channel_id=1, source_target_pairs={{0,1},{1,0},{2,3},{3,2},{4,5},{5,4},{6,7},{7,6},{8,9},{9,8},{10,11... | collective-permute-start | bytes 3096584 | tf_op jit(solution)/shard_map/ppermute | solution.py:41
  38.9 2.2 %copy-start = (f32[112,1152]{1,0:T(8,128)S(1)}, f32[112,1152]{1,0:T(8,128)}, u32[]{:S(2)}) copy-start(f32[112,1152]{1,0:T(8,128)} %param.16) | copy-start | bytes 1548292
  38.9 2.3 %copy-start.2 = (f32[112]{0:T(128)S(1)}, f32[112]{0:T(128)}, u32[]{:S(2)}) copy-start(f32[112]{0:T(128)} %param.17) | copy-start | bytes 1348
  41.3 24.2 %collective-permute-start.8 = (bf16[128,1152]{1,0:T(8,128)(2,1)S(1)}, bf16[128,1152]{1,0:T(8,128)(2,1)S(1)}, u32[]{:S(2)}, u32[]{:S(2)}) collective-permute-start(bf16[128,1152]{1,0:T(8,128)(2,1)S(1)} %fusion.17), channel_id=1, source_target_pairs={{0,16},{1,17},{2,18},{3,19},{4,20},{5,21},{6,22},{7,23},{8,24},{9,... | collective-permute-start | bytes 884744 | tf_op jit(solution)/shard_map/ppermute | solution.py:51
  46.0 12.4 %collective-permute-start.4 = (bf16[448,1152]{1,0:T(8,128)(2,1)S(1)}, bf16[448,1152]{1,0:T(8,128)(2,1)S(1)}, u32[]{:S(2)}, u32[]{:S(2)}) collective-permute-start(bf16[448,1152]{1,0:T(8,128)(2,1)S(1)} %fusion.2), channel_id=1, source_target_pairs={{0,1},{1,0},{2,3},{3,2},{4,5},{5,4},{6,7},{7,6},{8,9},{9,8},{10,11... | collective-permute-start | bytes 3096584 | tf_op jit(solution)/shard_map/ppermute | solution.py:41
  48.3 21.6 %collective-permute-start.9 = (bf16[128,1152]{1,0:T(8,128)(2,1)S(1)}, bf16[128,1152]{1,0:T(8,128)(2,1)S(1)}, u32[]{:S(2)}, u32[]{:S(2)}) collective-permute-start(bf16[128,1152]{1,0:T(8,128)(2,1)S(1)} %fusion.18), channel_id=1, source_target_pairs={{0,24},{1,25},{2,26},{3,27},{4,28},{5,29},{6,30},{7,31},{8,16},{9,... | collective-permute-start | bytes 884744 | tf_op jit(solution)/shard_map/ppermute | solution.py:51
  56.0 14.0 %collective-permute-start.10 = (bf16[128,1152]{1,0:T(8,128)(2,1)S(1)}, bf16[128,1152]{1,0:T(8,128)(2,1)S(1)}, u32[]{:S(2)}, u32[]{:S(2)}) collective-permute-start(bf16[128,1152]{1,0:T(8,128)(2,1)S(1)} %fusion.19), channel_id=1, source_target_pairs={{0,8},{1,9},{2,10},{3,11},{4,12},{5,13},{6,14},{7,15},{8,0},{9,1},... | collective-permute-start | bytes 884744 | tf_op jit(solution)/shard_map/ppermute | solution.py:41
  59.5 12.0 %collective-permute-start.5 = (bf16[112,1152]{1,0:T(8,128)(2,1)S(1)}, bf16[112,1152]{1,0:T(8,128)(2,1)S(1)}, u32[]{:S(2)}, u32[]{:S(2)}) collective-permute-start(bf16[112,1152]{1,0:T(8,128)(2,1)S(1)} %get-tuple-element.43), channel_id=1, source_target_pairs={{0,2},{1,3},{2,4},{3,5},{4,6},{5,7},{6,0},{7,1},{8,10},{9,11},{10,... | collective-permute-start | bytes 774152 | tf_op jit(solution)/shard_map/ppermute | solution.py:41
  61.4 12.6 %collective-permute-start.6 = (bf16[112,1152]{1,0:T(8,128)(2,1)S(1)}, bf16[112,1152]{1,0:T(8,128)(2,1)S(1)}, u32[]{:S(2)}, u32[]{:S(2)}) collective-permute-start(bf16[112,1152]{1,0:T(8,128)(2,1)S(1)} %get-tuple-element.45), channel_id=1, source_target_pairs={{0,4},{1,5},{2,6},{3,7},{4,0},{5,1},{6,2},{7,3},{8,12},{9,13},{10,... | collective-permute-start | bytes 774152 | tf_op jit(solution)/shard_map/ppermute | solution.py:41
  65.5 12.7 %collective-permute-start.7 = (bf16[112,1152]{1,0:T(8,128)(2,1)S(1)}, bf16[112,1152]{1,0:T(8,128)(2,1)S(1)}, u32[]{:S(2)}, u32[]{:S(2)}) collective-permute-start(bf16[112,1152]{1,0:T(8,128)(2,1)S(1)} %get-tuple-element.44), channel_id=1, source_target_pairs={{0,6},{1,7},{2,0},{3,1},{4,2},{5,3},{6,4},{7,5},{8,14},{9,15},{10,... | collective-permute-start | bytes 774152 | tf_op jit(solution)/shard_map/ppermute | solution.py:41

commit v2 on v1

v2 whole, which is shorter than its diff:
```python
import functools

import jax
import jax.numpy as jnp
from jax import lax
from jax.experimental import pallas as pl
from jax.experimental.pallas import tpu as pltpu
from jax.sharding import PartitionSpec as P


NBLK = 32
XH, Y, CORE = 2, 4, 2
ROWS = 112
SETS = Y * ROWS
SPAN = XH * Y * CORE * ROWS
TAIL = 16
LOG2E = 1.4426950408889634
LN2 = 0.6931471805599453
CHUNK = 32
Y_ORDER = (1, 2, 3)
F32 = jnp.float32
BF16 = jnp.bfloat16


def spot(xh, y, core):
    return (xh * Y + y) * CORE + core


def member_route(move):
    return [
        (spot(xh, y, c), spot(*move(xh, y, c)))
        for xh in range(XH)
        for y in range(Y)
        for c in range(CORE)
    ]


def across_x(xh, y, c):
    return (1 - xh, y, c)


def across_core(xh, y, c):
    return (xh, y, 1 - c)


def along_y(steps):
    return lambda xh, y, c: (xh, (y + steps) % Y, c)


def stay(xh, y, c):
    return (xh, y, c)


def to_member(block, move):
    return lax.ppermute(block, "grp", member_route(move))


def to_next_group(block, move):
    ngrp = XH * Y * CORE
    route = [
        (b * ngrp + s, ((b + 1) % NBLK) * ngrp + t)
        for b in range(NBLK)
        for s, t in member_route(move)
    ]
    return lax.ppermute(block, ("blk", "grp"), route)


def gather_y(block):
    groups = [[spot(xh, y, c) for y in range(Y)] for xh in range(XH) for c in range(CORE)]
    return lax.all_gather(block, "grp", axis_index_groups=groups, tiled=True)


VMEM = pl.BlockSpec(memory_space=pltpu.VMEM)
HBM = pl.BlockSpec(memory_space=pltpu.HBM)


def call(body, outs, ins, flops, scratch=(), far=0):
    size = sum(x.size * x.dtype.itemsize for x in [*ins, *outs])
    return pl.pallas_call(
        body,
        out_shape=outs,
        in_specs=[HBM] * far + [VMEM] * (len(ins) - far),
        out_specs=[VMEM] * len(outs),
        scratch_shapes=list(scratch),
        cost_estimate=pl.CostEstimate(flops=flops, bytes_accessed=size, transcendentals=0),
        compiler_params=pltpu.CompilerParams(vmem_limit_bytes=12 * 1024 * 1024),
    )(*ins)


def shape(rows, cols, dtype):
    return jax.ShapeDtypeStruct((rows, cols), dtype)


def labels_of(match_ref, member, other):
    core = (member ^ other) & (CORE - 1)
    xh = member // (Y * CORE)
    lane = lax.broadcasted_iota(jnp.int32, (8, 128), 1)
    last = match_ref.shape[0] - 1
    tiles = []
    for q in range(-(-SETS // 128)):
        tile = jnp.zeros((8, 128), jnp.int32)
        for y in range(q * 128 // ROWS, min(Y - 1, (q * 128 + 127) // ROWS) + 1):
            shift = ROWS * (xh * Y * CORE + core + y)
            row = q + shift // 128
            turn = shift % 128
            pieces = []
            for r in (row, row + 1):
                piece = match_ref[pl.ds(jnp.minimum(r, last), 1), :]
                piece = jnp.broadcast_to(piece, (8, 128))
                pieces.append(pltpu.roll(piece, (128 - turn) % 128, 1))
            found = jnp.where(lane < 128 - turn, pieces[0], pieces[1])
            here = q * 128 + lane
            tile = jnp.where((here >= y * ROWS) & (here < (y + 1) * ROWS), found, tile)
        tiles.append(tile)
    return jnp.concatenate(tiles, axis=1)[0:1, :SETS]


def weigh(s_ref, labels, place, step, scale, bias, w_ref, lost_ref, first):
    here, member = place
    factor, offset = scale * LOG2E, bias * LOG2E
    turned = (here - step) & (NBLK - 1)
    behind = (turned - 1) & (NBLK - 1)
    partner = member ^ (Y * CORE)
    bases = [
        turned * SPAN + member * ROWS,
        turned * SPAN + partner * ROWS - ROWS,
        behind * SPAN + member * ROWS - 2 * ROWS,
        behind * SPAN + partner * ROWS - 3 * ROWS,
    ]

    def chunk(i, carry):
        start = pl.multiple_of(i * CHUNK, CHUNK)
        rows = start + lax.broadcasted_iota(jnp.int32, (CHUNK, 1), 0)
        base = jnp.where(
            rows < 2 * ROWS,
            jnp.where(rows < ROWS, bases[0], bases[1]),
            jnp.where(rows < 3 * ROWS, bases[2], bases[3]),
        )
        logits = factor * s_ref[pl.ds(start, CHUNK), :] + offset
        paired = (rows + base) == labels
        t = jnp.where(paired, -logits, logits)
        e = jnp.exp2(-jnp.abs(t))
        more = jnp.where(e < 1e-4, LOG2E * e, jnp.log2(1.0 + e))
        lost = jnp.maximum(t, 0.0) + more
        sig = jnp.exp2(t - lost)
        w_ref[pl.ds(start, CHUNK), :] = jnp.where(paired, -sig, sig).astype(BF16)
        total = jnp.sum(lost, axis=1, keepdims=True)
        if not first:
            total = total + lost_ref[pl.ds(start, CHUNK), :]
        lost_ref[pl.ds(start, CHUNK), :] = total
        return carry

    lax.fori_loop(0, 2 * XH * ROWS // CHUNK, chunk, 0, unroll=True)


def logits_of(texts, images):
    return lax.dot_general(texts, images, (((1,), (1,)), ((), ())), preferred_element_type=F32)


def image_part(weights, texts):
    return lax.dot_general(weights, texts, (((0,), (0,)), ((), ())), preferred_element_type=F32)


def here_and_member():
    return lax.axis_index("blk"), lax.axis_index("grp")


def fetch(pairs, sems):
    copies = [pltpu.make_async_copy(a, b, sems.at[i]) for i, (a, b) in enumerate(pairs)]
    for copy in copies:
        copy.start()
    return copies


def first_half(
    step, scale, bias, match, t0, t1, t2, t3, images, texts, w, part, lost,
    s, match_v, step_s, scale_s, bias_s, sems,
):
    copies = fetch(
        [(t0, texts.at[:ROWS, :]), (match, match_v), (step, step_s), (scale, scale_s), (bias, bias_s)],
        sems,
    )
    for i, t in enumerate((t1, t2, t3)):
        texts[(i + 1) * ROWS : (i + 2) * ROWS, :] = t[...]
    copies[0].wait()
    s[...] = logits_of(texts[...], images[...])
    for copy in copies[1:]:
        copy.wait()
    place = here_and_member()
    labels = labels_of(match_v, place[1], 0)
    weigh(s, labels, place, step_s[0], scale_s[0], bias_s[0], w, lost, True)
    part[...] = jnp.dot(w[...], images[...], preferred_element_type=F32)


def row_of(column):
    r = lax.broadcasted_iota(jnp.int32, (ROWS, 128), 0)
    c = lax.broadcasted_iota(jnp.int32, (ROWS, 128), 1)
    return jnp.sum(jnp.where(r == c, column, 0.0), axis=0, keepdims=True)


def second_half(
    step, scale, bias, match, texts, images, part, lost, acc, loss_acc,
    w, sent, late_rows, s, lost_all, match_v, step_s, scale_s, bias_s, sems,
):
    copies = fetch([(match, match_v), (step, step_s), (scale, scale_s), (bias, bias_s)], sems)
    s[...] = logits_of(texts[...], images[...])
    lost_all[...] = lost[...]
    for copy in copies:
        copy.wait()
    place = here_and_member()
    factor = scale_s[0]
    labels = labels_of(match_v, place[1], 1)
    weigh(s, labels, place, step_s[0], factor, bias_s[0], w, lost_all, False)
    grad = jnp.dot(w[: 2 * ROWS, :], images[...], preferred_element_type=F32)
    grad = factor * (grad + part[: 2 * ROWS, :])
    sent[:ROWS, :] = (acc[...] + grad[:ROWS]).astype(BF16)
    sent[ROWS : 2 * ROWS, :] = grad[ROWS:].astype(BF16)
    rows = [row_of(lost_all[i * ROWS : (i + 1) * ROWS, :]) * (LN2 / SPAN) for i in range(4)]
    at = lax.broadcasted_iota(jnp.int32, (TAIL, 128), 0)
    tail = jnp.where(at == 0, rows[0], jnp.where(at == 1, rows[1], 0.0))
    at = lax.broadcasted_iota(jnp.int32, (TAIL, ROWS), 0)
    tail = tail[:, :ROWS] + jnp.where(at == 0, loss_acc[...], 0.0)
    sent[2 * ROWS :, :] = jnp.zeros((TAIL, sent.shape[1]), BF16)
    sent[2 * ROWS :, :ROWS] = tail.astype(BF16)
    at = lax.broadcasted_iota(jnp.int32, (8, 128), 0)
    late_rows[...] = jnp.where(at == 0, rows[2], jnp.where(at == 1, rows[3], factor))


def image_other(late_rows, w, texts, out):
    out[...] = (late_rows[2:3, 0:1] * image_part(w[...], texts[...])).astype(BF16)


def rest(late_rows, w_own, w_other, texts, images, part, image_own, late):
    factor = late_rows[2:3, 0:1]
    image_own[...] = factor * image_part(w_own[...], texts[...])
    grad = jnp.dot(w_other[2 * ROWS :, :], images[...], preferred_element_type=F32)
    late[...] = factor * (grad + part[2 * ROWS :, :])


def image_sum(steps, own, came, *refs):
    y = (lax.axis_index("grp") // CORE) & (Y - 1)
    for step, out in zip(steps, refs[-len(steps) :]):
        start = pl.multiple_of(((y + step) & (Y - 1)) * ROWS, 16)
        rows = pl.ds(start, ROWS)
        out[...] = (own[rows, :] + came[rows, :].astype(F32)).astype(out.dtype)


def across(late, late_rows, came, token, sent):
    sent[:ROWS, :] = (late[ROWS:, :] + came[ROWS : 2 * ROWS, :].astype(F32)).astype(BF16)
    sent[ROWS:, :] = jnp.zeros((TAIL, sent.shape[1]), BF16)
    tail = came[2 * ROWS :, :128].astype(F32)
    sent[ROWS:, :128] = (tail[1:2, :] + late_rows[1:2, :] + jnp.zeros((TAIL, 128), F32)).astype(BF16)


def image_end(kept, one, two, three, out):
    out[...] = kept[...] + one[...].astype(F32) + two[...].astype(F32) + three[...].astype(F32)


def text_end(late, late_rows, came, crossed, grad, loss):
    grad[...] = late[:ROWS, :] + came[:ROWS, :].astype(F32) + crossed[:ROWS, :].astype(F32)
    ahead = came[2 * ROWS :, :128].astype(F32)
    beside = crossed[ROWS:, :128].astype(F32)
    loss[...] = (late_rows[0:1, :] + ahead[0:1, :] + beside[0:1, :])[:, :ROWS]


def on_device(image_emb, text_held, text_grad_acc, text_loss_acc, match, step, scale, bias):
    width = text_held.shape[1]

    text_z = to_next_group(text_held, stay)
    text_d = to_next_group(text_held, across_x)
    text_x = to_member(text_held, across_x)
    images = gather_y(image_emb)
    images_other = to_member(images, across_core)

    match = match.reshape(-1, 128)
    count = 2 * XH * ROWS
    big = 2 * count * SETS * width
    scratch = [
        pltpu.VMEM(match.shape, jnp.int32),
        pltpu.SMEM((1,), jnp.int32),
        pltpu.SMEM((1,), F32),
        pltpu.SMEM((1,), F32),
        pltpu.SemaphoreType.DMA((5,)),
    ]
    texts, w_own, part, lost = call(
        first_half,
        [shape(count, width, BF16), shape(count, SETS, BF16), shape(count, width, F32), shape(count, 1, F32)],
        [step, scale, bias, match, text_held, text_x, text_z, text_d, images],
        40 * big,
        [pltpu.VMEM((count, SETS), F32), *scratch],
        far=5,
    )
    w_other, ahead, late_rows = call(
        second_half,
        [shape(count, SETS, BF16), shape(2 * ROWS + TAIL, width, BF16), shape(8, 128, F32)],
        [step, scale, bias, match, texts, images_other, part, lost, text_grad_acc, text_loss_acc.reshape(1, ROWS)],
        2 * big,
        [pltpu.VMEM((count, SETS), F32), pltpu.VMEM((count, 1), F32), *scratch],
        far=4,
    )
    came = to_next_group(ahead, stay)
    (other,) = call(image_other, [shape(SETS, width, BF16)], [late_rows, w_other, texts], 20 * big)
    other_came = to_member(other, across_core)
    image_own, late = call(
        rest,
        [shape(SETS, width, F32), shape(2 * ROWS, width, F32)],
        [late_rows, w_own, w_other, texts, images_other, part],
        20 * big,
    )
    block = shape(ROWS, width, BF16)
    arrived = []
    token = ()
    for step_y in Y_ORDER:
        steps = (step_y,) if step_y != Y_ORDER[-1] else (step_y, 0)
        outs = [block, shape(ROWS, width, F32)][: len(steps)]
        sums = call(functools.partial(image_sum, steps), outs, [image_own, other_came, *token], 20 * big)
        arrived.append(to_member(sums[0], along_y(step_y)))
        token = sums[-1:]
    kept = token[0]
    (crossing,) = call(across, [shape(ROWS + TAIL, width, BF16)], [late, late_rows, came, kept], ROWS * width)
    crossed = to_member(crossing, across_x)
    (image_grad,) = call(image_end, [shape(ROWS, width, F32)], [kept, *arrived], ROWS * width)
    text_grad_out, loss = call(
        text_end,
        [shape(ROWS, width, F32), shape(1, ROWS, F32)],
        [late, late_rows, came, crossed],
        ROWS * width,
    )
    return (image_grad, text_grad_out, loss.reshape(ROWS))


def solution(mesh):
    placed = (
        P(("blk", "grp"), None),
        P(("blk", "grp"), None),
        P(("blk", "grp"), None),
        P(("blk", "grp")),
        P("blk"),
        P(),
        P(),
        P(),
    )
    return jax.shard_map(
        on_device,
        mesh=mesh,
        in_specs=placed,
        out_specs=(P(("blk", "grp"), None), P(("blk", "grp"), None), P(("blk", "grp"))),
        check_vma=False,
    )
```

time: 79.8 us -> 90 us (1.13)
  the two profiles are of different devices: /device:TPU:8 before, /device:TPU:1 now
where the time goes in v2:
time: 90 us; the launch traced here: 89.6 us
  starting transfers between devices  35.6 us (40%)
  waiting for transfers between devices  26.7 us (30%)
  blocking collectives  14 us (16%)
  Pallas kernels  8.92 us (10%)
  between operations  2.76 us (3%)
  local copies, waits for them, and re-layouts  1.65 us (2%)
    ppermute x7, starting transfers between devices, to_member(): return lax.ppermute(block, 'grp', member_route(move))  23.9 us
    ppermute x3, waiting for transfers between devices, to_next_group(): return lax.ppermute(block, ('blk', 'grp'), route)  14.5 us
    all_gather x1, blocking collectives, gather_y(): return lax.all_gather(block, 'grp', axis_index_groups=groups, tiled=True)  14 us
    ppermute x7, waiting for transfers between devices, to_member(): return lax.ppermute(block, 'grp', member_route(move))  12.1 us
    ppermute x3, starting transfers between devices, to_next_group(): return lax.ppermute(block, ('blk', 'grp'), route)  11.7 us
    pallas_call x10, Pallas kernels, call(): pl.pallas_call(body, out_shape=outs, in_specs=[HBM] * far + [VMEM] * (len...  8.92 us
  transfers between devices with their start and end apart: 10, of which 4 were waited for; matrix products, arithmetic and copies ran while one was open for 0% of the time, Pallas kernels for 6%

profile of v2, /device:TPU:1, one launch (start us, length us, event | category | flops | bytes accessed | tf_op | source)
XLA Modules:
  0.0 89.6 jit_solution(4239477650006497794)
XLA Ops:
  0.6 4.4 %collective-permute-start.1 = (bf16[112,1152]{1,0:T(8,128)(2,1)}, bf16[112,1152]{1,0:T(8,128)(2,1)S(1)}, u32[]{:S(2)}, u32[]{:S(2)}) collective-permute-start(bf16[112,1152]{1,0:T(8,128)(2,1)} %t0.1), channel_id=1, source_target_pairs={{0,16},{1,17},{2,18},{3,19},{4,20},{5,21},{6,22},{7,23},{8,24},{9,... | collective-permute-start | bytes 774152 | tf_op jit(solution)/shard_map/ppermute | solution.py:65
  5.0 4.7 %collective-permute-start = (bf16[112,1152]{1,0:T(8,128)(2,1)}, bf16[112,1152]{1,0:T(8,128)(2,1)S(1)}, u32[]{:S(2)}, u32[]{:S(2)}) collective-permute-start(bf16[112,1152]{1,0:T(8,128)(2,1)} %t0.1), channel_id=1, source_target_pairs={{0,8},{1,9},{2,10},{3,11},{4,12},{5,13},{6,14},{7,15},{8,0},{9,1},... | collective-permute-start | bytes 774152 | tf_op jit(solution)/shard_map/ppermute | solution.py:55
  9.7 3.5 %collective-permute-start.2 = (bf16[112,1152]{1,0:T(8,128)(2,1)}, bf16[112,1152]{1,0:T(8,128)(2,1)S(1)}, u32[]{:S(2)}, u32[]{:S(2)}) collective-permute-start(bf16[112,1152]{1,0:T(8,128)(2,1)} %t0.1), channel_id=1, source_target_pairs={{0,24},{1,25},{2,26},{3,27},{4,28},{5,29},{6,30},{7,31},{8,16},{9,... | collective-permute-start | bytes 774152 | tf_op jit(solution)/shard_map/ppermute | solution.py:65
  13.2 14.0 %all_gather.3.images = bf16[448,1152]{1,0:T(8,128)(2,1)S(1)} all-gather(bf16[112,1152]{1,0:T(8,128)(2,1)} %param.8), channel_id=1, replica_groups={{0,2,4,6},{1,3,5,7},{8,10,12,14},{9,11,13,15},{16,18,20,22},{17,19,21,2..., dimensions={0}, use_global_device_ids=true | all-gather | bytes 1290240 | tf_op jit(solution)/shard_map/all_gather | solution.py:70
  27.2 4.3 %collective-permute-start.3 = (bf16[448,1152]{1,0:T(8,128)(2,1)S(1)}, bf16[448,1152]{1,0:T(8,128)(2,1)S(1)}, u32[]{:S(2)}, u32[]{:S(2)}) collective-permute-start(bf16[448,1152]{1,0:T(8,128)(2,1)S(1)} %all_gather.3.images), channel_id=1, source_target_pairs={{0,1},{1,0},{2,3},{3,2},{4,5},{5,4},{6,7},{7,6},{8,9},{9,8},{10,11... | collective-permute-start | bytes 3096584 | tf_op jit(solution)/shard_map/ppermute | solution.py:55
  33.4 0.0 collective-permute-done.1.t2
  33.4 0.0 collective-permute-done.t1
  33.4 0.0 copy-start.1
  33.5 0.7 copy-done.1
  34.1 0.9 %copy-done.3 = bf16[112,1152]{1,0:T(8,128)(2,1)S(1)} copy-done((bf16[112,1152]{1,0:T(8,128)(2,1)S(1)}, bf16[112,1152]{1,0:T(8,128)(2,1)}, u32[]{:S(2)}) %copy-start.3) | copy-done | bytes 258072
  35.1 2.7 %shard_map.103 = (bf16[448,1152]{1,0:T(8,128)(2,1)S(1)}, bf16[448,448]{1,0:T(8,128)(2,1)S(1)}, f32[448,1152]{1,0:T(8,128)S(1)}, f32[448,1]{1,0:T(8,128)S(1)}) custom-call(s32[1]{0:T(128)S(6)} %copy.11.step, f32[1]{0:T(128)S(6)} %copy.12.scale, f32[1]{0:T(128)S(6)} %copy.13.bias, s32[14,128]{1,0:T(8,128)S(1)} %bitcast.3, bf16[112,1152]{1,0:T(8,128)(2,1)S(1)} %copy-done.3, ...), custom_call_target="tpu_custom_call" | custom-call | flops 18496880640 | bytes 5571340 | tf_op jit(solution)/shard_map/pallas_call | solution.py:79
  37.8 0.0 collective-permute-done.3.images
  37.8 2.2 %shard_map.104 = (bf16[448,448]{1,0:T(8,128)(2,1)S(1)}, bf16[240,1152]{1,0:T(8,128)(2,1)S(1)}, f32[8,128]{1,0:T(8,128)S(1)}) custom-call(s32[1]{0:T(128)S(6)} %copy.11.step, f32[1]{0:T(128)S(6)} %copy.12.scale, f32[1]{0:T(128)S(6)} %copy.13.bias, s32[14,128]{1,0:T(8,128)S(1)} %bitcast.4, bf16[448,1152]{1,0:T(8,128)(2,1)S(1)} %get-tuple-element.16.texts, ...), custom_call_target="tpu_custom_call" | custom-call | flops 924844032 | bytes 5612748 | tf_op jit(solution)/shard_map/pallas_call | solution.py:79
  40.0 0.8 shard_map.106
  40.8 1.9 %collective-permute-start.4 = (bf16[448,1152]{1,0:T(8,128)(2,1)S(1)}, bf16[448,1152]{1,0:T(8,128)(2,1)S(1)}, u32[]{:S(2)}, u32[]{:S(2)}) collective-permute-start(bf16[448,1152]{1,0:T(8,128)(2,1)S(1)} %shard_map.106), channel_id=1, source_target_pairs={{0,1},{1,0},{2,3},{3,2},{4,5},{5,4},{6,7},{7,6},{8,9},{9,8},{10,11... | collective-permute-start | bytes 3096584 | tf_op jit(solution)/shard_map/ppermute | solution.py:55
  42.8 3.8 %collective-permute-start.8 = (bf16[240,1152]{1,0:T(8,128)(2,1)S(1)}, bf16[240,1152]{1,0:T(8,128)(2,1)S(1)}, u32[]{:S(2)}, u32[]{:S(2)}) collective-permute-start(bf16[240,1152]{1,0:T(8,128)(2,1)S(1)} %get-tuple-element.26), channel_id=1, source_target_pairs={{0,16},{1,17},{2,18},{3,19},{4,20},{5,21},{6,22},{7,23},{8,24},{9,... | collective-permute-start | bytes 1658888 | tf_op jit(solution)/shard_map/ppermute | solution.py:65
  46.6 1.1 %shard_map.105 = (f32[448,1152]{1,0:T(8,128)S(1)}, f32[224,1152]{1,0:T(8,128)S(1)}) custom-call(f32[8,128]{1,0:T(8,128)S(1)} %get-tuple-element.19.late_rows, bf16[448,448]{1,0:T(8,128)(2,1)S(1)} %get-tuple-element.20.w_own, bf16[448,448]{1,0:T(8,128)(2,1)S(1)} %get-tuple-element.21.w_other.w, bf16[448,1152]{1,0:T(8,128)(2,1)S(1)} %get-tuple-element.16.texts, ...), custom_call_target="tpu_custom_call" | custom-call | flops 9248440320 | bytes 8032256 | tf_op jit(solution)/shard_map/pallas_call | solution.py:79
  47.7 0.0 collective-permute-done.4.came
  47.7 0.1 shard_map.107.refs_0_
  47.8 0.1 shard_map.108.refs_0_
  47.9 0.1 shard_map.109
  48.0 14.5 %collective-permute-done.8.came = bf16[240,1152]{1,0:T(8,128)(2,1)S(1)} collective-permute-done((bf16[240,1152]{1,0:T(8,128)(2,1)S(1)}, bf16[240,1152]{1,0:T(8,128)(2,1)S(1)}, u32[]{:S(2)}, u32[]{:S(2)}) %collective-permute-start.8) | collective-permute-done | bytes 552992 | tf_op jit(solution)/shard_map/ppermute | solution.py:65
  62.6 0.1 shard_map.111
  62.6 3.5 %collective-permute-start.9 = (bf16[128,1152]{1,0:T(8,128)(2,1)S(1)}, bf16[128,1152]{1,0:T(8,128)(2,1)S(1)}, u32[]{:S(2)}, u32[]{:S(2)}) collective-permute-start(bf16[128,1152]{1,0:T(8,128)(2,1)S(1)} %shard_map.111), channel_id=1, source_target_pairs={{0,8},{1,9},{2,10},{3,11},{4,12},{5,13},{6,14},{7,15},{8,0},{9,1},... | collective-permute-start | bytes 884744 | tf_op jit(solution)/shard_map/ppermute | solution.py:55
  66.1 5.1 %collective-permute-start.7 = (bf16[112,1152]{1,0:T(8,128)(2,1)S(1)}, bf16[112,1152]{1,0:T(8,128)(2,1)S(1)}, u32[]{:S(2)}, u32[]{:S(2)}) collective-permute-start(bf16[112,1152]{1,0:T(8,128)(2,1)S(1)} %get-tuple-element.24), channel_id=1, source_target_pairs={{0,6},{1,7},{2,0},{3,1},{4,2},{5,3},{6,4},{7,5},{8,14},{9,15},{10,... | collective-permute-start | bytes 774152 | tf_op jit(solution)/shard_map/ppermute | solution.py:55
  71.2 2.5 %collective-permute-start.6 = (bf16[112,1152]{1,0:T(8,128)(2,1)S(1)}, bf16[112,1152]{1,0:T(8,128)(2,1)S(1)}, u32[]{:S(2)}, u32[]{:S(2)}) collective-permute-start(bf16[112,1152]{1,0:T(8,128)(2,1)S(1)} %shard_map.108.refs_0_), channel_id=1, source_target_pairs={{0,4},{1,5},{2,6},{3,7},{4,0},{5,1},{6,2},{7,3},{8,12},{9,13},{10,... | collective-permute-start | bytes 774152 | tf_op jit(solution)/shard_map/ppermute | solution.py:55
  73.7 1.9 %collective-permute-start.5 = (bf16[112,1152]{1,0:T(8,128)(2,1)S(1)}, bf16[112,1152]{1,0:T(8,128)(2,1)S(1)}, u32[]{:S(2)}, u32[]{:S(2)}) collective-permute-start(bf16[112,1152]{1,0:T(8,128)(2,1)S(1)} %shard_map.107.refs_0_), channel_id=1, source_target_pairs={{0,2},{1,3},{2,4},{3,5},{4,6},{5,7},{6,0},{7,1},{8,10},{9,11},{10,... | collective-permute-start | bytes 774152 | tf_op jit(solution)/shard_map/ppermute | solution.py:55
  75.6 0.5 collective-permute-done.7.three
  76.1 4.6 %collective-permute-done.6.two = bf16[112,1152]{1,0:T(8,128)(2,1)S(1)} collective-permute-done((bf16[112,1152]{1,0:T(8,128)(2,1)S(1)}, bf16[112,1152]{1,0:T(8,128)(2,1)S(1)}, u32[]{:S(2)}, u32[]{:S(2)}) %collective-permute-start.6) | collective-permute-done | bytes 258080 | tf_op jit(solution)/shard_map/ppermute | solution.py:55
  80.7 7.0 %collective-permute-done.5.one = bf16[112,1152]{1,0:T(8,128)(2,1)S(1)} collective-permute-done((bf16[112,1152]{1,0:T(8,128)(2,1)S(1)}, bf16[112,1152]{1,0:T(8,128)(2,1)S(1)}, u32[]{:S(2)}, u32[]{:S(2)}) %collective-permute-start.5) | collective-permute-done | bytes 258080 | tf_op jit(solution)/shard_map/ppermute | solution.py:55
  87.8 0.9 %shard_map.110 = f32[112,1152]{1,0:T(8,128)} custom-call(f32[112,1152]{1,0:T(8,128)S(1)} %get-tuple-element.23.kept.token, bf16[112,1152]{1,0:T(8,128)(2,1)S(1)} %collective-permute-done.5.one, bf16[112,1152]{1,0:T(8,128)(2,1)S(1)} %collective-permute-done.6.two, bf16[112,1152]{1,0:T(8,128)(2,1)S(1)} %collective-permute-done.7.three), custom_call_target="tpu_custom_call" | custom-call | flops 129024 | bytes 1806336 | tf_op jit(solution)/shard_map/pallas_call | solution.py:79
  88.7 0.9 shard_map.112
  (7 shorter events, 0.0 us)
Async XLA Ops:
  0.6 32.8 %collective-permute-start.1 = (bf16[112,1152]{1,0:T(8,128)(2,1)}, bf16[112,1152]{1,0:T(8,128)(2,1)S(1)}, u32[]{:S(2)}, u32[]{:S(2)}) collective-permute-start(bf16[112,1152]{1,0:T(8,128)(2,1)} %t0.1), channel_id=1, source_target_pairs={{0,16},{1,17},{2,18},{3,19},{4,20},{5,21},{6,22},{7,23},{8,24},{9,... | collective-permute-start | bytes 774152 | tf_op jit(solution)/shard_map/ppermute | solution.py:65
  5.0 28.4 %collective-permute-start = (bf16[112,1152]{1,0:T(8,128)(2,1)}, bf16[112,1152]{1,0:T(8,128)(2,1)S(1)}, u32[]{:S(2)}, u32[]{:S(2)}) collective-permute-start(bf16[112,1152]{1,0:T(8,128)(2,1)} %t0.1), channel_id=1, source_target_pairs={{0,8},{1,9},{2,10},{3,11},{4,12},{5,13},{6,14},{7,15},{8,0},{9,1},... | collective-permute-start | bytes 774152 | tf_op jit(solution)/shard_map/ppermute | solution.py:55
  9.7 23.8 %collective-permute-start.2 = (bf16[112,1152]{1,0:T(8,128)(2,1)}, bf16[112,1152]{1,0:T(8,128)(2,1)S(1)}, u32[]{:S(2)}, u32[]{:S(2)}) collective-permute-start(bf16[112,1152]{1,0:T(8,128)(2,1)} %t0.1), channel_id=1, source_target_pairs={{0,24},{1,25},{2,26},{3,27},{4,28},{5,29},{6,30},{7,31},{8,16},{9,... | collective-permute-start | bytes 774152 | tf_op jit(solution)/shard_map/ppermute | solution.py:65
  27.2 10.6 %collective-permute-start.3 = (bf16[448,1152]{1,0:T(8,128)(2,1)S(1)}, bf16[448,1152]{1,0:T(8,128)(2,1)S(1)}, u32[]{:S(2)}, u32[]{:S(2)}) collective-permute-start(bf16[448,1152]{1,0:T(8,128)(2,1)S(1)} %all_gather.3.images), channel_id=1, source_target_pairs={{0,1},{1,0},{2,3},{3,2},{4,5},{5,4},{6,7},{7,6},{8,9},{9,8},{10,11... | collective-permute-start | bytes 3096584 | tf_op jit(solution)/shard_map/ppermute | solution.py:55
  33.4 0.7 copy-start.1
  34.1 0.9 %copy-start.3 = (bf16[112,1152]{1,0:T(8,128)(2,1)S(1)}, bf16[112,1152]{1,0:T(8,128)(2,1)}, u32[]{:S(2)}) copy-start(bf16[112,1152]{1,0:T(8,128)(2,1)} %t0.1) | copy-start | bytes 774148
  35.1 2.7 %copy-start = (f32[112,1152]{1,0:T(8,128)S(1)}, f32[112,1152]{1,0:T(8,128)}, u32[]{:S(2)}) copy-start(f32[112,1152]{1,0:T(8,128)} %acc.1) | copy-start | bytes 1548292
  35.1 2.7 %copy-start.2 = (f32[112]{0:T(128)S(1)}, f32[112]{0:T(128)}, u32[]{:S(2)}) copy-start(f32[112]{0:T(128)} %param.11) | copy-start | bytes 1348
  40.8 6.9 %collective-permute-start.4 = (bf16[448,1152]{1,0:T(8,128)(2,1)S(1)}, bf16[448,1152]{1,0:T(8,128)(2,1)S(1)}, u32[]{:S(2)}, u32[]{:S(2)}) collective-permute-start(bf16[448,1152]{1,0:T(8,128)(2,1)S(1)} %shard_map.106), channel_id=1, source_target_pairs={{0,1},{1,0},{2,3},{3,2},{4,5},{5,4},{6,7},{7,6},{8,9},{9,8},{10,11... | collective-permute-start | bytes 3096584 | tf_op jit(solution)/shard_map/ppermute | solution.py:55
  42.8 19.8 %collective-permute-start.8 = (bf16[240,1152]{1,0:T(8,128)(2,1)S(1)}, bf16[240,1152]{1,0:T(8,128)(2,1)S(1)}, u32[]{:S(2)}, u32[]{:S(2)}) collective-permute-start(bf16[240,1152]{1,0:T(8,128)(2,1)S(1)} %get-tuple-element.26), channel_id=1, source_target_pairs={{0,16},{1,17},{2,18},{3,19},{4,20},{5,21},{6,22},{7,23},{8,24},{9,... | collective-permute-start | bytes 1658888 | tf_op jit(solution)/shard_map/ppermute | solution.py:65
  62.6 26.1 %collective-permute-start.9 = (bf16[128,1152]{1,0:T(8,128)(2,1)S(1)}, bf16[128,1152]{1,0:T(8,128)(2,1)S(1)}, u32[]{:S(2)}, u32[]{:S(2)}) collective-permute-start(bf16[128,1152]{1,0:T(8,128)(2,1)S(1)} %shard_map.111), channel_id=1, source_target_pairs={{0,8},{1,9},{2,10},{3,11},{4,12},{5,13},{6,14},{7,15},{8,0},{9,1},... | collective-permute-start | bytes 884744 | tf_op jit(solution)/shard_map/ppermute | solution.py:55
  66.1 10.0 %collective-permute-start.7 = (bf16[112,1152]{1,0:T(8,128)(2,1)S(1)}, bf16[112,1152]{1,0:T(8,128)(2,1)S(1)}, u32[]{:S(2)}, u32[]{:S(2)}) collective-permute-start(bf16[112,1152]{1,0:T(8,128)(2,1)S(1)} %get-tuple-element.24), channel_id=1, source_target_pairs={{0,6},{1,7},{2,0},{3,1},{4,2},{5,3},{6,4},{7,5},{8,14},{9,15},{10,... | collective-permute-start | bytes 774152 | tf_op jit(solution)/shard_map/ppermute | solution.py:55
  71.2 9.5 %collective-permute-start.6 = (bf16[112,1152]{1,0:T(8,128)(2,1)S(1)}, bf16[112,1152]{1,0:T(8,128)(2,1)S(1)}, u32[]{:S(2)}, u32[]{:S(2)}) collective-permute-start(bf16[112,1152]{1,0:T(8,128)(2,1)S(1)} %shard_map.108.refs_0_), channel_id=1, source_target_pairs={{0,4},{1,5},{2,6},{3,7},{4,0},{5,1},{6,2},{7,3},{8,12},{9,13},{10,... | collective-permute-start | bytes 774152 | tf_op jit(solution)/shard_map/ppermute | solution.py:55
  73.7 14.1 %collective-permute-start.5 = (bf16[112,1152]{1,0:T(8,128)(2,1)S(1)}, bf16[112,1152]{1,0:T(8,128)(2,1)S(1)}, u32[]{:S(2)}, u32[]{:S(2)}) collective-permute-start(bf16[112,1152]{1,0:T(8,128)(2,1)S(1)} %shard_map.107.refs_0_), channel_id=1, source_target_pairs={{0,2},{1,3},{2,4},{3,5},{4,6},{5,7},{6,0},{7,1},{8,10},{9,11},{10,... | collective-permute-start | bytes 774152 | tf_op jit(solution)/shard_map/ppermute | solution.py:55

commit v3 on v2

--- a/solution.py
+++ b/solution.py
@@ -17,7 +17,7 @@
 LOG2E = 1.4426950408889634
 LN2 = 0.6931471805599453
 CHUNK = 32
-Y_ORDER = (1, 2, 3)
+Y_ORDER = (1, 3, 2)
 F32 = jnp.float32
 BF16 = jnp.bfloat16
 
@@ -71,15 +71,20 @@
 
 
 VMEM = pl.BlockSpec(memory_space=pltpu.VMEM)
+SMEM = pl.BlockSpec(memory_space=pltpu.SMEM)
 HBM = pl.BlockSpec(memory_space=pltpu.HBM)
 
 
 def call(body, outs, ins, flops, scratch=(), far=0):
     size = sum(x.size * x.dtype.itemsize for x in [*ins, *outs])
+    ins = [
+        pltpu.with_memory_space_constraint(x, pltpu.HBM) if i < far else x
+        for i, x in enumerate(ins)
+    ]
     return pl.pallas_call(
         body,
         out_shape=outs,
-        in_specs=[HBM] * far + [VMEM] * (len(ins) - far),
+        in_specs=[HBM if i < far else SMEM if x.size == 1 else VMEM for i, x in enumerate(ins)],
         out_specs=[VMEM] * len(outs),
         scratch_shapes=list(scratch),
         cost_estimate=pl.CostEstimate(flops=flops, bytes_accessed=size, transcendentals=0),
@@ -173,12 +178,11 @@
 
 
 def first_half(
-    step, scale, bias, match, t0, t1, t2, t3, images, texts, w, part, lost,
-    s, match_v, step_s, scale_s, bias_s, sems,
+    match, t0, step, scale, bias, t1, t2, t3, images, texts, w, part, lost,
+    s, match_v, sems,
 ):
     copies = fetch(
-        [(t0, texts.at[:ROWS, :]), (match, match_v), (step, step_s), (scale, scale_s), (bias, bias_s)],
-        sems,
+        [(t0, texts.at[:ROWS, :]), (match, match_v)], sems
     )
     for i, t in enumerate((t1, t2, t3)):
         texts[(i + 1) * ROWS : (i + 2) * ROWS, :] = t[...]
@@ -188,7 +192,7 @@
         copy.wait()
     place = here_and_member()
     labels = labels_of(match_v, place[1], 0)
-    weigh(s, labels, place, step_s[0], scale_s[0], bias_s[0], w, lost, True)
+    weigh(s, labels, place, step[0], scale[0], bias[0], w, lost, True)
     part[...] = jnp.dot(w[...], images[...], preferred_element_type=F32)
 
 
@@ -199,18 +203,18 @@
 
 
 def second_half(
-    step, scale, bias, match, texts, images, part, lost, acc, loss_acc,
-    w, sent, late_rows, s, lost_all, match_v, step_s, scale_s, bias_s, sems,
+    match, step, scale, bias, texts, images, part, lost, acc, loss_acc,
+    w, sent, late_rows, s, lost_all, match_v, sems,
 ):
-    copies = fetch([(match, match_v), (step, step_s), (scale, scale_s), (bias, bias_s)], sems)
+    copies = fetch([(match, match_v)], sems)
     s[...] = logits_of(texts[...], images[...])
     lost_all[...] = lost[...]
     for copy in copies:
         copy.wait()
     place = here_and_member()
-    factor = scale_s[0]
+    factor = scale[0]
     labels = labels_of(match_v, place[1], 1)
-    weigh(s, labels, place, step_s[0], factor, bias_s[0], w, lost_all, False)
+    weigh(s, labels, place, step[0], factor, bias[0], w, lost_all, False)
     grad = jnp.dot(w[: 2 * ROWS, :], images[...], preferred_element_type=F32)
     grad = factor * (grad + part[: 2 * ROWS, :])
     sent[:ROWS, :] = (acc[...] + grad[:ROWS]).astype(BF16)
@@ -252,11 +256,12 @@
     sent[ROWS:, :128] = (tail[1:2, :] + late_rows[1:2, :] + jnp.zeros((TAIL, 128), F32)).astype(BF16)
 
 
-def image_end(kept, one, two, three, out):
+def image_end(kept, one, two, three, out, token):
+    token[...] = kept[:8, :128]
     out[...] = kept[...] + one[...].astype(F32) + two[...].astype(F32) + three[...].astype(F32)
 
 
-def text_end(late, late_rows, came, crossed, grad, loss):
+def text_end(late, late_rows, came, crossed, token, grad, loss):
     grad[...] = late[:ROWS, :] + came[:ROWS, :].astype(F32) + crossed[:ROWS, :].astype(F32)
     ahead = came[2 * ROWS :, :128].astype(F32)
     beside = crossed[ROWS:, :128].astype(F32)
@@ -277,26 +282,23 @@
     big = 2 * count * SETS * width
     scratch = [
         pltpu.VMEM(match.shape, jnp.int32),
-        pltpu.SMEM((1,), jnp.int32),
-        pltpu.SMEM((1,), F32),
-        pltpu.SMEM((1,), F32),
-        pltpu.SemaphoreType.DMA((5,)),
+        pltpu.SemaphoreType.DMA((2,)),
     ]
     texts, w_own, part, lost = call(
         first_half,
         [shape(count, width, BF16), shape(count, SETS, BF16), shape(count, width, F32), shape(count, 1, F32)],
-        [step, scale, bias, match, text_held, text_x, text_z, text_d, images],
+        [match, text_held, step, scale, bias, text_x, text_z, text_d, images],
         40 * big,
         [pltpu.VMEM((count, SETS), F32), *scratch],
-        far=5,
+        far=2,
     )
     w_other, ahead, late_rows = call(
         second_half,
         [shape(count, SETS, BF16), shape(2 * ROWS + TAIL, width, BF16), shape(8, 128, F32)],
-        [step, scale, bias, match, texts, images_other, part, lost, text_grad_acc, text_loss_acc.reshape(1, ROWS)],
+        [match, step, scale, bias, texts, images_other, part, lost, text_grad_acc, text_loss_acc.reshape(1, ROWS)],
         2 * big,
         [pltpu.VMEM((count, SETS), F32), pltpu.VMEM((count, 1), F32), *scratch],
-        far=4,
+        far=1,
     )
     came = to_next_group(ahead, stay)
     (other,) = call(image_other, [shape(SETS, width, BF16)], [late_rows, w_other, texts], 20 * big)
@@ -319,11 +321,13 @@
     kept = token[0]
     (crossing,) = call(across, [shape(ROWS + TAIL, width, BF16)], [late, late_rows, came, kept], ROWS * width)
     crossed = to_member(crossing, across_x)
-    (image_grad,) = call(image_end, [shape(ROWS, width, F32)], [kept, *arrived], ROWS * width)
+    image_grad, token = call(
+        image_end, [shape(ROWS, width, F32), shape(8, 128, F32)], [kept, *arrived], 40 * big
+    )
     text_grad_out, loss = call(
         text_end,
         [shape(ROWS, width, F32), shape(1, ROWS, F32)],
-        [late, late_rows, came, crossed],
+        [late, late_rows, came, crossed, token],
         ROWS * width,
     )
     return (image_grad, text_grad_out, loss.reshape(ROWS))

time: 90 us -> 75.1 us (0.83)
  the two profiles are of different devices: /device:TPU:1 before, /device:TPU:8 now
where the time goes in v3:
time: 75.1 us; the launch traced here: 74.6 us
  starting transfers between devices  34.2 us (46%)
  blocking collectives  15.5 us (21%)
  waiting for transfers between devices  12.5 us (17%)
  Pallas kernels  9.58 us (13%)
  between operations  2.78 us (4%)
    ppermute x7, starting transfers between devices, to_member(): return lax.ppermute(block, 'grp', member_route(move))  22.8 us
    all_gather x1, blocking collectives, gather_y(): return lax.all_gather(block, 'grp', axis_index_groups=groups, tiled=True)  15.5 us
    ppermute x3, starting transfers between devices, to_next_group(): return lax.ppermute(block, ('blk', 'grp'), route)  11.4 us
    pallas_call x10, Pallas kernels, call(): pl.pallas_call(body, out_shape=outs, in_specs=[HBM if i < far else SMEM i...  9.58 us
    ppermute x7, waiting for transfers between devices, to_member(): return lax.ppermute(block, 'grp', member_route(move))  7.16 us
    ppermute x3, waiting for transfers between devices, to_next_group(): return lax.ppermute(block, ('blk', 'grp'), route)  5.32 us
  transfers between devices with their start and end apart: 10, of which 2 were waited for; matrix products, arithmetic and copies ran while one was open for 0% of the time, Pallas kernels for 7%

profile of v3, /device:TPU:8, one launch (start us, length us, event | category | flops | bytes accessed | tf_op | source)
XLA Modules:
  0.0 74.6 jit_solution(17775547390641254051)
XLA Ops:
  0.6 3.8 %collective-permute-start.1 = (bf16[112,1152]{1,0:T(8,128)(2,1)}, bf16[112,1152]{1,0:T(8,128)(2,1)S(1)}, u32[]{:S(2)}, u32[]{:S(2)}) collective-permute-start(bf16[112,1152]{1,0:T(8,128)(2,1)} %t0.1), channel_id=1, source_target_pairs={{0,16},{1,17},{2,18},{3,19},{4,20},{5,21},{6,22},{7,23},{8,24},{9,... | collective-permute-start | bytes 774152 | tf_op jit(solution)/shard_map/ppermute | solution.py:65
  4.5 4.9 %collective-permute-start = (bf16[112,1152]{1,0:T(8,128)(2,1)}, bf16[112,1152]{1,0:T(8,128)(2,1)S(1)}, u32[]{:S(2)}, u32[]{:S(2)}) collective-permute-start(bf16[112,1152]{1,0:T(8,128)(2,1)} %t0.1), channel_id=1, source_target_pairs={{0,8},{1,9},{2,10},{3,11},{4,12},{5,13},{6,14},{7,15},{8,0},{9,1},... | collective-permute-start | bytes 774152 | tf_op jit(solution)/shard_map/ppermute | solution.py:55
  9.4 3.8 %collective-permute-start.2 = (bf16[112,1152]{1,0:T(8,128)(2,1)}, bf16[112,1152]{1,0:T(8,128)(2,1)S(1)}, u32[]{:S(2)}, u32[]{:S(2)}) collective-permute-start(bf16[112,1152]{1,0:T(8,128)(2,1)} %t0.1), channel_id=1, source_target_pairs={{0,24},{1,25},{2,26},{3,27},{4,28},{5,29},{6,30},{7,31},{8,16},{9,... | collective-permute-start | bytes 774152 | tf_op jit(solution)/shard_map/ppermute | solution.py:65
  13.2 15.5 %all_gather.3.images = bf16[448,1152]{1,0:T(8,128)(2,1)S(1)} all-gather(bf16[112,1152]{1,0:T(8,128)(2,1)} %param.8), channel_id=1, replica_groups={{0,2,4,6},{1,3,5,7},{8,10,12,14},{9,11,13,15},{16,18,20,22},{17,19,21,2..., dimensions={0}, use_global_device_ids=true | all-gather | bytes 1290240 | tf_op jit(solution)/shard_map/all_gather | solution.py:70
  28.7 1.9 %collective-permute-start.3 = (bf16[448,1152]{1,0:T(8,128)(2,1)S(1)}, bf16[448,1152]{1,0:T(8,128)(2,1)S(1)}, u32[]{:S(2)}, u32[]{:S(2)}) collective-permute-start(bf16[448,1152]{1,0:T(8,128)(2,1)S(1)} %all_gather.3.images), channel_id=1, source_target_pairs={{0,1},{1,0},{2,3},{3,2},{4,5},{5,4},{6,7},{7,6},{8,9},{9,8},{10,11... | collective-permute-start | bytes 3096584 | tf_op jit(solution)/shard_map/ppermute | solution.py:55
  32.6 0.0 collective-permute-done.1.t2
  32.6 0.0 collective-permute-done.t1
  32.6 0.0 collective-permute-done.2.t3
  32.6 0.0 copy-start
  32.6 0.0 copy-start.1
  32.6 3.2 %shard_map.103 = (bf16[448,1152]{1,0:T(8,128)(2,1)S(1)}, bf16[448,448]{1,0:T(8,128)(2,1)S(1)}, f32[448,1152]{1,0:T(8,128)S(1)}, f32[448,1]{1,0:T(8,128)S(1)}) custom-call(s32[14,128]{1,0:T(8,128)} %bitcast.4, bf16[112,1152]{1,0:T(8,128)(2,1)} %t0.1, s32[1]{0:T(128)S(6)} %copy.11.step, f32[1]{0:T(128)S(6)} %copy.12.scale, f32[1]{0:T(128)S(6)} %copy.13.bias, ...), custom_call_target="tpu_custom_call" | custom-call | flops 18496880640 | bytes 5571340 | tf_op jit(solution)/shard_map/pallas_call | solution.py:84
  35.9 0.0 collective-permute-done.3.images
  35.9 2.3 %shard_map.104 = (bf16[448,448]{1,0:T(8,128)(2,1)S(1)}, bf16[240,1152]{1,0:T(8,128)(2,1)S(1)}, f32[8,128]{1,0:T(8,128)S(1)}) custom-call(s32[14,128]{1,0:T(8,128)} %bitcast.5, s32[1]{0:T(128)S(6)} %copy.11.step, f32[1]{0:T(128)S(6)} %copy.12.scale, f32[1]{0:T(128)S(6)} %copy.13.bias, bf16[448,1152]{1,0:T(8,128)(2,1)S(1)} %get-tuple-element.18.texts, ...), custom_call_target="tpu_custom_call" | custom-call | flops 924844032 | bytes 5612748 | tf_op jit(solution)/shard_map/pallas_call | solution.py:84
  38.2 0.8 %shard_map.106 = bf16[448,1152]{1,0:T(8,128)(2,1)S(1)} custom-call(f32[8,128]{1,0:T(8,128)S(1)} %get-tuple-element.21.late_rows, bf16[448,448]{1,0:T(8,128)(2,1)S(1)} %get-tuple-element.23.w_other.w, bf16[448,1152]{1,0:T(8,128)(2,1)S(1)} %get-tuple-element.18.texts), custom_call_target="tpu_custom_call" | custom-call | flops 9248440320 | bytes 2469888 | tf_op jit(solution)/shard_map/pallas_call | solution.py:84
  39.0 2.4 %collective-permute-start.4 = (bf16[448,1152]{1,0:T(8,128)(2,1)S(1)}, bf16[448,1152]{1,0:T(8,128)(2,1)S(1)}, u32[]{:S(2)}, u32[]{:S(2)}) collective-permute-start(bf16[448,1152]{1,0:T(8,128)(2,1)S(1)} %shard_map.106), channel_id=1, source_target_pairs={{0,1},{1,0},{2,3},{3,2},{4,5},{5,4},{6,7},{7,6},{8,9},{9,8},{10,11... | collective-permute-start | bytes 3096584 | tf_op jit(solution)/shard_map/ppermute | solution.py:55
  41.5 3.8 %collective-permute-start.8 = (bf16[240,1152]{1,0:T(8,128)(2,1)S(1)}, bf16[240,1152]{1,0:T(8,128)(2,1)S(1)}, u32[]{:S(2)}, u32[]{:S(2)}) collective-permute-start(bf16[240,1152]{1,0:T(8,128)(2,1)S(1)} %get-tuple-element.29), channel_id=1, source_target_pairs={{0,16},{1,17},{2,18},{3,19},{4,20},{5,21},{6,22},{7,23},{8,24},{9,... | collective-permute-start | bytes 1658888 | tf_op jit(solution)/shard_map/ppermute | solution.py:65
  45.3 1.1 %shard_map.105 = (f32[448,1152]{1,0:T(8,128)S(1)}, f32[224,1152]{1,0:T(8,128)S(1)}) custom-call(f32[8,128]{1,0:T(8,128)S(1)} %get-tuple-element.21.late_rows, bf16[448,448]{1,0:T(8,128)(2,1)S(1)} %get-tuple-element.22.w_own, bf16[448,448]{1,0:T(8,128)(2,1)S(1)} %get-tuple-element.23.w_other.w, bf16[448,1152]{1,0:T(8,128)(2,1)S(1)} %get-tuple-element.18.texts, ...), custom_call_target="tpu_custom_call" | custom-call | flops 9248440320 | bytes 8032256 | tf_op jit(solution)/shard_map/pallas_call | solution.py:84
  46.4 0.0 collective-permute-done.4.came
  46.4 0.1 shard_map.107.refs_0_
  46.5 0.1 shard_map.108.refs_0_
  46.6 0.1 shard_map.109
  46.7 4.0 %collective-permute-start.7 = (bf16[112,1152]{1,0:T(8,128)(2,1)S(1)}, bf16[112,1152]{1,0:T(8,128)(2,1)S(1)}, u32[]{:S(2)}, u32[]{:S(2)}) collective-permute-start(bf16[112,1152]{1,0:T(8,128)(2,1)S(1)} %get-tuple-element.26), channel_id=1, source_target_pairs={{0,4},{1,5},{2,6},{3,7},{4,0},{5,1},{6,2},{7,3},{8,12},{9,13},{10,... | collective-permute-start | bytes 774152 | tf_op jit(solution)/shard_map/ppermute | solution.py:55
  50.7 1.9 %collective-permute-start.6 = (bf16[112,1152]{1,0:T(8,128)(2,1)S(1)}, bf16[112,1152]{1,0:T(8,128)(2,1)S(1)}, u32[]{:S(2)}, u32[]{:S(2)}) collective-permute-start(bf16[112,1152]{1,0:T(8,128)(2,1)S(1)} %shard_map.108.refs_0_), channel_id=1, source_target_pairs={{0,6},{1,7},{2,0},{3,1},{4,2},{5,3},{6,4},{7,5},{8,14},{9,15},{10,... | collective-permute-start | bytes 774152 | tf_op jit(solution)/shard_map/ppermute | solution.py:55
  52.6 3.9 %collective-permute-start.5 = (bf16[112,1152]{1,0:T(8,128)(2,1)S(1)}, bf16[112,1152]{1,0:T(8,128)(2,1)S(1)}, u32[]{:S(2)}, u32[]{:S(2)}) collective-permute-start(bf16[112,1152]{1,0:T(8,128)(2,1)S(1)} %shard_map.107.refs_0_), channel_id=1, source_target_pairs={{0,2},{1,3},{2,4},{3,5},{4,6},{5,7},{6,0},{7,1},{8,10},{9,11},{10,... | collective-permute-start | bytes 774152 | tf_op jit(solution)/shard_map/ppermute | solution.py:55
  56.5 5.3 %collective-permute-done.8.came = bf16[240,1152]{1,0:T(8,128)(2,1)S(1)} collective-permute-done((bf16[240,1152]{1,0:T(8,128)(2,1)S(1)}, bf16[240,1152]{1,0:T(8,128)(2,1)S(1)}, u32[]{:S(2)}, u32[]{:S(2)}) %collective-permute-start.8) | collective-permute-done | bytes 552992 | tf_op jit(solution)/shard_map/ppermute | solution.py:65
  61.9 0.1 shard_map.111
  61.9 3.7 %collective-permute-start.9 = (bf16[128,1152]{1,0:T(8,128)(2,1)S(1)}, bf16[128,1152]{1,0:T(8,128)(2,1)S(1)}, u32[]{:S(2)}, u32[]{:S(2)}) collective-permute-start(bf16[128,1152]{1,0:T(8,128)(2,1)S(1)} %shard_map.111), channel_id=1, source_target_pairs={{0,8},{1,9},{2,10},{3,11},{4,12},{5,13},{6,14},{7,15},{8,0},{9,1},... | collective-permute-start | bytes 884744 | tf_op jit(solution)/shard_map/ppermute | solution.py:55
  65.6 0.0 collective-permute-done.7.three
  65.6 0.0 collective-permute-done.5.one
  65.7 0.9 %shard_map.110 = (f32[112,1152]{1,0:T(8,128)}, f32[8,128]{1,0:T(8,128)S(1)}) custom-call(f32[112,1152]{1,0:T(8,128)S(1)} %get-tuple-element.25.kept.token, bf16[112,1152]{1,0:T(8,128)(2,1)S(1)} %collective-permute-done.5.one, bf16[112,1152]{1,0:T(8,128)(2,1)S(1)} %collective-permute-done.6.two, bf16[112,1152]{1,0:T(8,128)(2,1)S(1)} %collective-permute-done.7.three), custom_call_target="tpu_custom_call" | custom-call | flops 18496880640 | bytes 1810432 | tf_op jit(solution)/shard_map/pallas_call | solution.py:84
  66.6 7.1 %collective-permute-done.9.crossed = bf16[128,1152]{1,0:T(8,128)(2,1)S(1)} collective-permute-done((bf16[128,1152]{1,0:T(8,128)(2,1)S(1)}, bf16[128,1152]{1,0:T(8,128)(2,1)S(1)}, u32[]{:S(2)}, u32[]{:S(2)}) %collective-permute-start.9) | collective-permute-done | bytes 294944 | tf_op jit(solution)/shard_map/ppermute | solution.py:55
  73.7 0.9 %shard_map.112 = (f32[112,1152]{1,0:T(8,128)}, f32[1,112]{1,0:T(1,128)}) custom-call(f32[224,1152]{1,0:T(8,128)S(1)} %get-tuple-element.28.late, f32[8,128]{1,0:T(8,128)S(1)} %get-tuple-element.21.late_rows, bf16[240,1152]{1,0:T(8,128)(2,1)S(1)} %collective-permute-done.8.came, bf16[128,1152]{1,0:T(8,128)(2,1)S(1)} %collective-permute-done.9.crossed, ...), custom_call_target="tpu_custom_call" | custom-call | flops 129024 | bytes 2404800 | tf_op jit(solution)/shard_map/pallas_call | solution.py:84
  (3 shorter events, 0.0 us)
Async XLA Ops:
  0.6 32.0 %collective-permute-start.1 = (bf16[112,1152]{1,0:T(8,128)(2,1)}, bf16[112,1152]{1,0:T(8,128)(2,1)S(1)}, u32[]{:S(2)}, u32[]{:S(2)}) collective-permute-start(bf16[112,1152]{1,0:T(8,128)(2,1)} %t0.1), channel_id=1, source_target_pairs={{0,16},{1,17},{2,18},{3,19},{4,20},{5,21},{6,22},{7,23},{8,24},{9,... | collective-permute-start | bytes 774152 | tf_op jit(solution)/shard_map/ppermute | solution.py:65
  4.5 28.1 %collective-permute-start = (bf16[112,1152]{1,0:T(8,128)(2,1)}, bf16[112,1152]{1,0:T(8,128)(2,1)S(1)}, u32[]{:S(2)}, u32[]{:S(2)}) collective-permute-start(bf16[112,1152]{1,0:T(8,128)(2,1)} %t0.1), channel_id=1, source_target_pairs={{0,8},{1,9},{2,10},{3,11},{4,12},{5,13},{6,14},{7,15},{8,0},{9,1},... | collective-permute-start | bytes 774152 | tf_op jit(solution)/shard_map/ppermute | solution.py:55
  9.4 23.2 %collective-permute-start.2 = (bf16[112,1152]{1,0:T(8,128)(2,1)}, bf16[112,1152]{1,0:T(8,128)(2,1)S(1)}, u32[]{:S(2)}, u32[]{:S(2)}) collective-permute-start(bf16[112,1152]{1,0:T(8,128)(2,1)} %t0.1), channel_id=1, source_target_pairs={{0,24},{1,25},{2,26},{3,27},{4,28},{5,29},{6,30},{7,31},{8,16},{9,... | collective-permute-start | bytes 774152 | tf_op jit(solution)/shard_map/ppermute | solution.py:65
  28.7 7.1 %collective-permute-start.3 = (bf16[448,1152]{1,0:T(8,128)(2,1)S(1)}, bf16[448,1152]{1,0:T(8,128)(2,1)S(1)}, u32[]{:S(2)}, u32[]{:S(2)}) collective-permute-start(bf16[448,1152]{1,0:T(8,128)(2,1)S(1)} %all_gather.3.images), channel_id=1, source_target_pairs={{0,1},{1,0},{2,3},{3,2},{4,5},{5,4},{6,7},{7,6},{8,9},{9,8},{10,11... | collective-permute-start | bytes 3096584 | tf_op jit(solution)/shard_map/ppermute | solution.py:55
  32.6 3.3 %copy-start = (f32[112,1152]{1,0:T(8,128)S(1)}, f32[112,1152]{1,0:T(8,128)}, u32[]{:S(2)}) copy-start(f32[112,1152]{1,0:T(8,128)} %acc.1) | copy-start | bytes 1548292
  32.6 3.3 %copy-start.1 = (f32[112]{0:T(128)S(1)}, f32[112]{0:T(128)}, u32[]{:S(2)}) copy-start(f32[112]{0:T(128)} %param.11) | copy-start | bytes 1348
  39.0 7.4 %collective-permute-start.4 = (bf16[448,1152]{1,0:T(8,128)(2,1)S(1)}, bf16[448,1152]{1,0:T(8,128)(2,1)S(1)}, u32[]{:S(2)}, u32[]{:S(2)}) collective-permute-start(bf16[448,1152]{1,0:T(8,128)(2,1)S(1)} %shard_map.106), channel_id=1, source_target_pairs={{0,1},{1,0},{2,3},{3,2},{4,5},{5,4},{6,7},{7,6},{8,9},{9,8},{10,11... | collective-permute-start | bytes 3096584 | tf_op jit(solution)/shard_map/ppermute | solution.py:55
  41.5 20.4 %collective-permute-start.8 = (bf16[240,1152]{1,0:T(8,128)(2,1)S(1)}, bf16[240,1152]{1,0:T(8,128)(2,1)S(1)}, u32[]{:S(2)}, u32[]{:S(2)}) collective-permute-start(bf16[240,1152]{1,0:T(8,128)(2,1)S(1)} %get-tuple-element.29), channel_id=1, source_target_pairs={{0,16},{1,17},{2,18},{3,19},{4,20},{5,21},{6,22},{7,23},{8,24},{9,... | collective-permute-start | bytes 1658888 | tf_op jit(solution)/shard_map/ppermute | solution.py:65
  46.7 18.9 %collective-permute-start.7 = (bf16[112,1152]{1,0:T(8,128)(2,1)S(1)}, bf16[112,1152]{1,0:T(8,128)(2,1)S(1)}, u32[]{:S(2)}, u32[]{:S(2)}) collective-permute-start(bf16[112,1152]{1,0:T(8,128)(2,1)S(1)} %get-tuple-element.26), channel_id=1, source_target_pairs={{0,4},{1,5},{2,6},{3,7},{4,0},{5,1},{6,2},{7,3},{8,12},{9,13},{10,... | collective-permute-start | bytes 774152 | tf_op jit(solution)/shard_map/ppermute | solution.py:55
  50.7 15.0 %collective-permute-start.6 = (bf16[112,1152]{1,0:T(8,128)(2,1)S(1)}, bf16[112,1152]{1,0:T(8,128)(2,1)S(1)}, u32[]{:S(2)}, u32[]{:S(2)}) collective-permute-start(bf16[112,1152]{1,0:T(8,128)(2,1)S(1)} %shard_map.108.refs_0_), channel_id=1, source_target_pairs={{0,6},{1,7},{2,0},{3,1},{4,2},{5,3},{6,4},{7,5},{8,14},{9,15},{10,... | collective-permute-start | bytes 774152 | tf_op jit(solution)/shard_map/ppermute | solution.py:55
  52.6 13.0 %collective-permute-start.5 = (bf16[112,1152]{1,0:T(8,128)(2,1)S(1)}, bf16[112,1152]{1,0:T(8,128)(2,1)S(1)}, u32[]{:S(2)}, u32[]{:S(2)}) collective-permute-start(bf16[112,1152]{1,0:T(8,128)(2,1)S(1)} %shard_map.107.refs_0_), channel_id=1, source_target_pairs={{0,2},{1,3},{2,4},{3,5},{4,6},{5,7},{6,0},{7,1},{8,10},{9,11},{10,... | collective-permute-start | bytes 774152 | tf_op jit(solution)/shard_map/ppermute | solution.py:55
  61.9 11.8 %collective-permute-start.9 = (bf16[128,1152]{1,0:T(8,128)(2,1)S(1)}, bf16[128,1152]{1,0:T(8,128)(2,1)S(1)}, u32[]{:S(2)}, u32[]{:S(2)}) collective-permute-start(bf16[128,1152]{1,0:T(8,128)(2,1)S(1)} %shard_map.111), channel_id=1, source_target_pairs={{0,8},{1,9},{2,10},{3,11},{4,12},{5,13},{6,14},{7,15},{8,0},{9,1},... | collective-permute-start | bytes 884744 | tf_op jit(solution)/shard_map/ppermute | solution.py:55

commit v4 on v3

v4 whole, which is shorter than its diff:
```python
import jax
import jax.numpy as jnp
from jax import lax
from jax.experimental import pallas as pl
from jax.experimental.pallas import tpu as pltpu
from jax.sharding import PartitionSpec as P


NBLK = 32
XH, Y, CORE = 2, 4, 2
ROWS = 112
SETS = Y * ROWS
LAG = XH * ROWS
SPAN = XH * Y * CORE * ROWS
TAIL = 16
LOG2E = 1.4426950408889634
LN2 = 0.6931471805599453
CHUNK = 32
F32 = jnp.float32
BF16 = jnp.bfloat16


def spot(xh, y, core):
    return (xh * Y + y) * CORE + core


def member_route(move):
    return [
        (spot(xh, y, c), spot(*move(xh, y, c)))
        for xh in range(XH)
        for y in range(Y)
        for c in range(CORE)
    ]


def across_x(xh, y, c):
    return (1 - xh, y, c)


def across_core(xh, y, c):
    return (xh, y, 1 - c)


def along_y(steps):
    return lambda xh, y, c: (xh, (y + steps) % Y, c)


def stay(xh, y, c):
    return (xh, y, c)


def to_member(block, move):
    return lax.ppermute(block, "grp", member_route(move))


def to_next_group(block, move):
    ngrp = XH * Y * CORE
    route = [
        (b * ngrp + s, ((b + 1) % NBLK) * ngrp + t)
        for b in range(NBLK)
        for s, t in member_route(move)
    ]
    return lax.ppermute(block, ("blk", "grp"), route)


def gather_y(block):
    groups = [[spot(xh, y, c) for y in range(Y)] for xh in range(XH) for c in range(CORE)]
    return lax.all_gather(block, "grp", axis_index_groups=groups, tiled=True)


VMEM = pl.BlockSpec(memory_space=pltpu.VMEM)
SMEM = pl.BlockSpec(memory_space=pltpu.SMEM)
HBM = pl.BlockSpec(memory_space=pltpu.HBM)


def call(body, outs, ins, flops, scratch=(), far=0):
    size = flops // 64
    ins = [
        pltpu.with_memory_space_constraint(x, pltpu.HBM) if i < far else x
        for i, x in enumerate(ins)
    ]
    return pl.pallas_call(
        body,
        out_shape=outs,
        in_specs=[HBM if i < far else SMEM if x.size == 1 else VMEM for i, x in enumerate(ins)],
        out_specs=[VMEM] * len(outs),
        scratch_shapes=list(scratch),
        cost_estimate=pl.CostEstimate(flops=flops, bytes_accessed=size, transcendentals=0),
        compiler_params=pltpu.CompilerParams(vmem_limit_bytes=12 * 1024 * 1024),
    )(*ins)


def shape(rows, cols, dtype):
    return jax.ShapeDtypeStruct((rows, cols), dtype)


def held(rows, cols, dtype):
    return pltpu.VMEM((rows, cols), dtype)


def labels_of(match_ref, member, other):
    core = (member ^ other) & (CORE - 1)
    xh = member // (Y * CORE)
    lane = lax.broadcasted_iota(jnp.int32, (8, 128), 1)
    last = match_ref.shape[0] - 1
    tiles = []
    for q in range(-(-SETS // 128)):
        tile = jnp.zeros((8, 128), jnp.int32)
        for y in range(q * 128 // ROWS, min(Y - 1, (q * 128 + 127) // ROWS) + 1):
            shift = ROWS * (xh * Y * CORE + core + y)
            row = q + shift // 128
            turn = shift % 128
            pieces = []
            for r in (row, row + 1):
                piece = match_ref[pl.ds(jnp.minimum(r, last), 1), :]
                piece = jnp.broadcast_to(piece, (8, 128))
                pieces.append(pltpu.roll(piece, (128 - turn) % 128, 1))
            found = jnp.where(lane < 128 - turn, pieces[0], pieces[1])
            here = q * 128 + lane
            tile = jnp.where((here >= y * ROWS) & (here < (y + 1) * ROWS), found, tile)
        tiles.append(tile)
    return jnp.concatenate(tiles, axis=1)[0:1, :SETS]


def weigh(lag, s_ref, labels, member, given, w_ref, lost_ref=None, first=True):
    factor, offset = given[0:1, 0:1] * LOG2E, given[0:1, 1:2] * LOG2E
    anchor = given[0:1, 2:3].astype(jnp.int32)
    turned = (anchor - lag) & (NBLK - 1)
    partner = member ^ (Y * CORE)
    bases = [turned * SPAN + member * ROWS, turned * SPAN + (partner - 1) * ROWS]

    def chunk(i, carry):
        start = pl.multiple_of(i * CHUNK, CHUNK)
        rows = start + lax.broadcasted_iota(jnp.int32, (CHUNK, 1), 0)
        base = jnp.where(rows < ROWS, bases[0], bases[1])
        logits = factor * s_ref[pl.ds(start, CHUNK), :] + offset
        paired = (rows + base) == labels
        t = jnp.where(paired, -logits, logits)
        e = jnp.exp2(-jnp.abs(t))
        more = jnp.where(e < 1e-4, LOG2E * e, jnp.log2(1.0 + e))
        lost = jnp.maximum(t, 0.0) + more
        sig = jnp.exp2(t - lost)
        w_ref[pl.ds(start, CHUNK), :] = jnp.where(paired, -sig, sig).astype(BF16)
        if lost_ref is not None:
            total = jnp.sum(lost, axis=1, keepdims=True)
            if not first:
                total = total + lost_ref[pl.ds(start, CHUNK), :]
            lost_ref[pl.ds(start, CHUNK), :] = total
        return carry

    lax.fori_loop(0, XH * ROWS // CHUNK, chunk, 0, unroll=True)


def logits_of(texts, images):
    return lax.dot_general(texts, images, (((1,), (1,)), ((), ())), preferred_element_type=F32)


def image_part(weights, texts):
    return lax.dot_general(weights, texts, (((0,), (0,)), ((), ())), preferred_element_type=F32)


def fetch(pairs, sems):
    copies = [pltpu.make_async_copy(a, b, sems.at[i]) for i, (a, b) in enumerate(pairs)]
    for copy in copies:
        copy.start()
    return copies


def own_logits(
    match, text, loss_hbm, given, t1, z, d, images, texts, s0, s1, labels, loss_acc, match_v, sems
):
    copies = fetch([(match, match_v), (text, texts.at[:ROWS, :]), (loss_hbm, loss_acc)], sems)
    for i, t in enumerate((t1, z, d)):
        texts[(i + 1) * ROWS : (i + 2) * ROWS, :] = t[...]
    s1[...] = logits_of(texts[LAG:, :], images[...])
    for copy in copies:
        copy.wait()
    s0[...] = logits_of(texts[:LAG, :], images[...])
    member = lax.axis_index("grp")
    at = lax.broadcasted_iota(jnp.int32, labels.shape, 0)
    labels[...] = jnp.where(at == 0, labels_of(match_v, member, 0), labels_of(match_v, member, 1))


def text_part(weights, halves):
    return sum(
        jnp.dot(w[...], x[...], preferred_element_type=F32) for w, x in zip(weights, halves)
    )


def row_of(column):
    r = lax.broadcasted_iota(jnp.int32, (ROWS, 128), 0)
    c = lax.broadcasted_iota(jnp.int32, (ROWS, 128), 1)
    return jnp.sum(jnp.where(r == c, column, 0.0), axis=0, keepdims=True)


def loss_rows(lost):
    rows = [row_of(lost[i * ROWS : (i + 1) * ROWS, :]) * (LN2 / SPAN) for i in range(XH)]
    at = lax.broadcasted_iota(jnp.int32, (TAIL, 128), 0)
    return jnp.where(at == 0, rows[0], jnp.where(at == 1, rows[1], 0.0))


def first_lag(
    given, labels, texts, s_own, own, other, acc, loss_acc, w_own, sent, s, w_other, lost
):
    member = lax.axis_index("grp")
    s[...] = logits_of(texts[:LAG, :], other[...])
    weigh(0, s_own, labels[0:1, :], member, given, w_own, lost, True)
    grad = jnp.dot(w_own[...], own[...], preferred_element_type=F32)
    weigh(0, s, labels[1:2, :], member, given, w_other, lost, False)
    grad = grad + jnp.dot(w_other[...], other[...], preferred_element_type=F32)
    grad = given[0:1, 0:1] * grad
    sent[:ROWS, :] = (acc[...] + grad[:ROWS]).astype(BF16)
    sent[ROWS : 2 * ROWS, :] = grad[ROWS:].astype(BF16)
    at = lax.broadcasted_iota(jnp.int32, (TAIL, ROWS), 0)
    tail = loss_rows(lost)[:, :ROWS] + jnp.where(at == 0, loss_acc[...], 0.0)
    sent[2 * ROWS :, :] = jnp.zeros((TAIL, sent.shape[1]), BF16)
    sent[2 * ROWS :, :ROWS] = tail.astype(BF16)


def image_parts(
    given, labels, w0, s1, texts, beside, own,
    w1, lost, kept, one, two, three, s_b, w, w_b, total,
):
    member = lax.axis_index("grp")
    there = member ^ 1
    row = labels[0:1, :]
    s_b[...] = logits_of(beside[...], own[...])
    weigh(1, s1, row, member, given, w1, lost, True)
    w[:LAG, :] = w0[...]
    w[LAG:, :] = w1[...]
    part = image_part(w[...], texts[...])
    weigh(0, s_b.at[:LAG, :], row, there, given, w_b.at[:LAG, :])
    weigh(1, s_b.at[LAG:, :], row, there, given, w_b.at[LAG:, :])
    part = part + image_part(w_b[...], beside[...])
    total[...] = given[0:1, 0:1] * part
    y = (member // CORE) & (Y - 1)
    for step, out in enumerate((kept, one, two, three)):
        start = pl.multiple_of(((y + step) & (Y - 1)) * ROWS, 16)
        out[...] = total[pl.ds(start, ROWS), :].astype(out.dtype)


def second_lag(
    given, labels, texts, w_own, lost_own, own, other, token, late, late_rows, s, w_other, lost
):
    member = lax.axis_index("grp")
    lost[...] = lost_own[...]
    s[...] = logits_of(texts[LAG:, :], other[...])
    weigh(1, s, labels[1:2, :], member, given, w_other, lost, False)
    late[...] = given[0:1, 0:1] * text_part((w_own, w_other), (own, other))
    late_rows[...] = loss_rows(lost)[:8, :]


def across(late, late_rows, came, sent):
    sent[:ROWS, :] = (late[ROWS:, :] + came[ROWS : 2 * ROWS, :].astype(F32)).astype(BF16)
    sent[ROWS:, :] = jnp.zeros((TAIL, sent.shape[1]), BF16)
    tail = came[2 * ROWS :, :128].astype(F32)
    sent[ROWS:, :128] = (tail[1:2, :] + late_rows[1:2, :] + jnp.zeros((TAIL, 128), F32)).astype(BF16)


def image_end(kept, one, two, three, out, token):
    token[...] = kept[:8, :128]
    out[...] = kept[...] + one[...].astype(F32) + two[...].astype(F32) + three[...].astype(F32)


def text_end(late, late_rows, came, crossed, token, grad, loss):
    grad[...] = late[:ROWS, :] + came[:ROWS, :].astype(F32) + crossed[:ROWS, :].astype(F32)
    ahead = came[2 * ROWS :, :128].astype(F32)
    beside = crossed[ROWS:, :128].astype(F32)
    loss[...] = (late_rows[0:1, :] + ahead[0:1, :] + beside[0:1, :])[:, :ROWS]


def on_device(image_emb, text_held, text_grad_acc, text_loss_acc, match, step, scale, bias):
    width = text_held.shape[1]

    text_z = to_next_group(text_held, stay)
    text_d = to_next_group(text_held, across_x)
    text_x = to_member(text_held, across_x)
    images = gather_y(image_emb)
    images_other = to_member(images, across_core)

    match = match.reshape(-1, 128)
    anchor = (lax.axis_index("blk").astype(jnp.int32) - step) & (NBLK - 1)
    given = jnp.concatenate([scale, bias, anchor.astype(F32), jnp.zeros((125,), F32)]).reshape(1, 128)

    big = 2 * LAG * SETS * width
    block = shape(ROWS, width, BF16)
    logits = held(LAG, SETS, F32)
    weights = held(LAG, SETS, BF16)
    texts, s0, s1, labels, loss_acc = call(
        own_logits,
        [shape(2 * LAG, width, BF16), logits, logits, held(8, SETS, jnp.int32), held(1, ROWS, F32)],
        [match, text_held, text_loss_acc.reshape(1, ROWS), given, text_x, text_z, text_d, images],
        2 * big,
        [pltpu.VMEM(match.shape, jnp.int32), pltpu.SemaphoreType.DMA((3,))],
        far=3,
    )
    texts_beside = to_member(texts, across_core)
    w0, ahead = call(
        first_lag,
        [weights, shape(LAG + TAIL, width, BF16)],
        [given, labels, texts, s0, images, images_other, text_grad_acc, loss_acc],
        3 * big,
        [logits, weights, held(LAG, 1, F32)],
    )
    came = to_next_group(ahead, stay)
    w1, lost1, kept, *sent = call(
        image_parts,
        [weights, held(LAG, 1, F32), held(ROWS, width, F32), block, block, block],
        [given, labels, w0, s1, texts, texts_beside, images],
        6 * big,
        [held(2 * LAG, SETS, F32), held(2 * LAG, SETS, BF16), held(2 * LAG, SETS, BF16), held(SETS, width, F32)],
    )
    arrived = [to_member(part, along_y(i + 1)) for i, part in enumerate(sent)]
    late, late_rows = call(
        second_lag,
        [held(LAG, width, F32), held(8, 128, F32)],
        [given, labels, texts, w1, lost1, images, images_other, kept],
        3 * big,
        [logits, weights, held(LAG, 1, F32)],
    )
    (crossing,) = call(across, [shape(ROWS + TAIL, width, BF16)], [late, late_rows, came], ROWS * width)
    crossed = to_member(crossing, across_x)
    image_grad, token = call(
        image_end, [shape(ROWS, width, F32), held(8, 128, F32)], [kept, *arrived], 40 * big
    )
    text_grad_out, loss = call(
        text_end,
        [shape(ROWS, width, F32), shape(1, ROWS, F32)],
        [late, late_rows, came, crossed, token],
        ROWS * width,
    )
    return (image_grad, text_grad_out, loss.reshape(ROWS))


def solution(mesh):
    placed = (
        P(("blk", "grp"), None),
        P(("blk", "grp"), None),
        P(("blk", "grp"), None),
        P(("blk", "grp")),
        P("blk"),
        P(),
        P(),
        P(),
    )
    return jax.shard_map(
        on_device,
        mesh=mesh,
        in_specs=placed,
        out_specs=(P(("blk", "grp"), None), P(("blk", "grp"), None), P(("blk", "grp"))),
        check_vma=False,
    )
```

time: 75.1 us -> 72 us (0.959)
  waiting for transfers between devices: 12.5 us -> 8.62 us
    ppermute x3, waiting for transfers between devices: 5.32 us -> 1.45 us  [to_next_group(): return lax.ppermute(block, ('blk', 'grp'), route)]
    pallas_call x10 -> x7, Pallas kernels: 9.58 us -> 9.8 us  [call(): pl.pallas_call(body, out_shape=outs, in_specs=[HBM if i < far else SMEM i...]
  transfers between devices with their start and end apart: 10 -> 10, of which waited for: 2 -> 3; matrix products, arithmetic and copies ran while one was open for 0% -> 0% of each run, Pallas kernels for 7% -> 12%
where the time goes in v4:
time: 72 us; the launch traced here: 71.6 us
  starting transfers between devices  34.8 us (48%)
  blocking collectives  15.5 us (22%)
  Pallas kernels  9.8 us (14%)
  waiting for transfers between devices  8.62 us (12%)
  between operations  2.74 us (4%)
    ppermute x7, starting transfers between devices, to_member(): return lax.ppermute(block, 'grp', member_route(move))  23.4 us
    all_gather x1, blocking collectives, gather_y(): return lax.all_gather(block, 'grp', axis_index_groups=groups, tiled=True)  15.5 us
    ppermute x3, starting transfers between devices, to_next_group(): return lax.ppermute(block, ('blk', 'grp'), route)  11.4 us
    pallas_call x7, Pallas kernels, call(): pl.pallas_call(body, out_shape=outs, in_specs=[HBM if i < far else SMEM i...  9.8 us
    ppermute x7, waiting for transfers between devices, to_member(): return lax.ppermute(block, 'grp', member_route(move))  7.17 us
    ppermute x3, waiting for transfers between devices, to_next_group(): return lax.ppermute(block, ('blk', 'grp'), route)  1.45 us
  transfers between devices with their start and end apart: 10, of which 3 were waited for; matrix products, arithmetic and copies ran while one was open for 0% of the time, Pallas kernels for 12%

profile of v4, /device:TPU:8, one launch (start us, length us, event | category | flops | bytes accessed | tf_op | source)
XLA Modules:
  0.0 71.6 jit_solution(4113871104111601308)
XLA Ops:
  0.6 3.8 %collective-permute-start.1 = (bf16[112,1152]{1,0:T(8,128)(2,1)}, bf16[112,1152]{1,0:T(8,128)(2,1)S(1)}, u32[]{:S(2)}, u32[]{:S(2)}) collective-permute-start(bf16[112,1152]{1,0:T(8,128)(2,1)} %text.1), channel_id=1, source_target_pairs={{0,16},{1,17},{2,18},{3,19},{4,20},{5,21},{6,22},{7,23},{8,24},{9,... | collective-permute-start | bytes 774152 | tf_op jit(solution)/shard_map/ppermute | solution.py:63
  4.5 4.9 %collective-permute-start = (bf16[112,1152]{1,0:T(8,128)(2,1)}, bf16[112,1152]{1,0:T(8,128)(2,1)S(1)}, u32[]{:S(2)}, u32[]{:S(2)}) collective-permute-start(bf16[112,1152]{1,0:T(8,128)(2,1)} %text.1), channel_id=1, source_target_pairs={{0,8},{1,9},{2,10},{3,11},{4,12},{5,13},{6,14},{7,15},{8,0},{9,1},... | collective-permute-start | bytes 774152 | tf_op jit(solution)/shard_map/ppermute | solution.py:53
  9.4 3.8 %collective-permute-start.2 = (bf16[112,1152]{1,0:T(8,128)(2,1)}, bf16[112,1152]{1,0:T(8,128)(2,1)S(1)}, u32[]{:S(2)}, u32[]{:S(2)}) collective-permute-start(bf16[112,1152]{1,0:T(8,128)(2,1)} %text.1), channel_id=1, source_target_pairs={{0,24},{1,25},{2,26},{3,27},{4,28},{5,29},{6,30},{7,31},{8,16},{9,... | collective-permute-start | bytes 774152 | tf_op jit(solution)/shard_map/ppermute | solution.py:63
  13.2 15.5 %all_gather.3.images.own = bf16[448,1152]{1,0:T(8,128)(2,1)S(1)} all-gather(bf16[112,1152]{1,0:T(8,128)(2,1)} %param.8), channel_id=1, replica_groups={{0,2,4,6},{1,3,5,7},{8,10,12,14},{9,11,13,15},{16,18,20,22},{17,19,21,2..., dimensions={0}, use_global_device_ids=true | all-gather | bytes 1290240 | tf_op jit(solution)/shard_map/all_gather | solution.py:68
  28.7 1.9 %collective-permute-start.3 = (bf16[448,1152]{1,0:T(8,128)(2,1)S(1)}, bf16[448,1152]{1,0:T(8,128)(2,1)S(1)}, u32[]{:S(2)}, u32[]{:S(2)}) collective-permute-start(bf16[448,1152]{1,0:T(8,128)(2,1)S(1)} %all_gather.3.images.own), channel_id=1, source_target_pairs={{0,1},{1,0},{2,3},{3,2},{4,5},{5,4},{6,7},{7,6},{8,9},{9,8},{10,11... | collective-permute-start | bytes 3096584 | tf_op jit(solution)/shard_map/ppermute | solution.py:53
  32.6 0.1 maximum_bitcast_fusion.given
  32.7 0.0 collective-permute-done.1.z
  32.7 0.0 collective-permute-done.t1
  32.7 0.0 collective-permute-done.2.d
  32.7 0.0 copy-start
  32.7 1.6 %shard_map.103 = (bf16[448,1152]{1,0:T(8,128)(2,1)S(1)}, f32[224,448]{1,0:T(8,128)S(1)}, f32[224,448]{1,0:T(8,128)S(1)}, s32[8,448]{1,0:T(8,128)S(1)}, f32[1,112]{1,0:T(1,128)S(1)}) custom-call(s32[14,128]{1,0:T(8,128)} %bitcast.6, bf16[112,1152]{1,0:T(8,128)(2,1)} %text.1, f32[1,112]{1,0:T(1,128)} %bitcast.7, f32[1,128]{1,0:T(1,128)S(1)} %maximum_bitcast_fusion.given, ...), custom_call_target="tpu_custom_call" | custom-call | flops 462422016 | bytes 7225344 | tf_op jit(solution)/shard_map/pallas_call | solution.py:82
  34.3 2.4 %collective-permute-start.4 = (bf16[448,1152]{1,0:T(8,128)(2,1)S(1)}, bf16[448,1152]{1,0:T(8,128)(2,1)S(1)}, u32[]{:S(2)}, u32[]{:S(2)}) collective-permute-start(bf16[448,1152]{1,0:T(8,128)(2,1)S(1)} %get-tuple-element.23.texts), channel_id=1, source_target_pairs={{0,1},{1,0},{2,3},{3,2},{4,5},{5,4},{6,7},{7,6},{8,9},{9,8},{10,11... | collective-permute-start | bytes 3096584 | tf_op jit(solution)/shard_map/ppermute | solution.py:53
  36.7 0.0 collective-permute-done.3.other
  36.7 0.0 copy-done
  36.7 1.7 %shard_map.104 = (bf16[224,448]{1,0:T(8,128)(2,1)S(1)}, bf16[240,1152]{1,0:T(8,128)(2,1)S(1)}) custom-call(f32[1,128]{1,0:T(1,128)S(1)} %maximum_bitcast_fusion.given, s32[8,448]{1,0:T(8,128)S(1)} %get-tuple-element.22.labels, bf16[448,1152]{1,0:T(8,128)(2,1)S(1)} %get-tuple-element.23.texts, f32[224,448]{1,0:T(8,128)S(1)} %get-tuple-element.24.s_own, ...), custom_call_target="tpu_custom_call" | custom-call | flops 693633024 | bytes 10838016 | tf_op jit(solution)/shard_map/pallas_call | solution.py:82
  38.4 3.8 %collective-permute-start.8 = (bf16[240,1152]{1,0:T(8,128)(2,1)S(1)}, bf16[240,1152]{1,0:T(8,128)(2,1)S(1)}, u32[]{:S(2)}, u32[]{:S(2)}) collective-permute-start(bf16[240,1152]{1,0:T(8,128)(2,1)S(1)} %get-tuple-element.37), channel_id=1, source_target_pairs={{0,16},{1,17},{2,18},{3,19},{4,20},{5,21},{6,22},{7,23},{8,24},{9,... | collective-permute-start | bytes 1658888 | tf_op jit(solution)/shard_map/ppermute | solution.py:63
  42.3 0.0 collective-permute-done.4.beside
  42.3 3.2 %shard_map.105 = (bf16[224,448]{1,0:T(8,128)(2,1)S(1)}, f32[224,1]{1,0:T(8,128)S(1)}, f32[112,1152]{1,0:T(8,128)S(1)}, bf16[112,1152]{1,0:T(8,128)(2,1)S(1)}, bf...) custom-call(f32[1,128]{1,0:T(1,128)S(1)} %maximum_bitcast_fusion.given, ...), custom_call_target="tpu_custom_call" | custom-call | flops 1387266048 | bytes 21676032 | tf_op jit(solution)/shard_map/pallas_call | solution.py:82
  45.5 1.9 %collective-permute-start.5 = (bf16[112,1152]{1,0:T(8,128)(2,1)S(1)}, bf16[112,1152]{1,0:T(8,128)(2,1)S(1)}, u32[]{:S(2)}, u32[]{:S(2)}) collective-permute-start(bf16[112,1152]{1,0:T(8,128)(2,1)S(1)} %get-tuple-element.29), channel_id=1, source_target_pairs={{0,2},{1,3},{2,4},{3,5},{4,6},{5,7},{6,0},{7,1},{8,10},{9,11},{10,... | collective-permute-start | bytes 774152 | tf_op jit(solution)/shard_map/ppermute | solution.py:53
  47.4 4.0 %collective-permute-start.6 = (bf16[112,1152]{1,0:T(8,128)(2,1)S(1)}, bf16[112,1152]{1,0:T(8,128)(2,1)S(1)}, u32[]{:S(2)}, u32[]{:S(2)}) collective-permute-start(bf16[112,1152]{1,0:T(8,128)(2,1)S(1)} %get-tuple-element.30), channel_id=1, source_target_pairs={{0,4},{1,5},{2,6},{3,7},{4,0},{5,1},{6,2},{7,3},{8,12},{9,13},{10,... | collective-permute-start | bytes 774152 | tf_op jit(solution)/shard_map/ppermute | solution.py:53
  51.5 4.5 %collective-permute-start.7 = (bf16[112,1152]{1,0:T(8,128)(2,1)S(1)}, bf16[112,1152]{1,0:T(8,128)(2,1)S(1)}, u32[]{:S(2)}, u32[]{:S(2)}) collective-permute-start(bf16[112,1152]{1,0:T(8,128)(2,1)S(1)} %get-tuple-element.31), channel_id=1, source_target_pairs={{0,6},{1,7},{2,0},{3,1},{4,2},{5,3},{6,4},{7,5},{8,14},{9,15},{10,... | collective-permute-start | bytes 774152 | tf_op jit(solution)/shard_map/ppermute | solution.py:53
  55.9 1.5 %shard_map.107 = (f32[224,1152]{1,0:T(8,128)S(1)}, f32[8,128]{1,0:T(8,128)S(1)}) custom-call(f32[1,128]{1,0:T(1,128)S(1)} %maximum_bitcast_fusion.given, s32[8,448]{1,0:T(8,128)S(1)} %get-tuple-element.22.labels, bf16[448,1152]{1,0:T(8,128)(2,1)S(1)} %get-tuple-element.23.texts, bf16[224,448]{1,0:T(8,128)(2,1)S(1)} %get-tuple-element.33.w_own, ...), custom_call_target="tpu_custom_call" | custom-call | flops 693633024 | bytes 10838016 | tf_op jit(solution)/shard_map/pallas_call | solution.py:82
  57.4 1.4 %collective-permute-done.8.came = bf16[240,1152]{1,0:T(8,128)(2,1)S(1)} collective-permute-done((bf16[240,1152]{1,0:T(8,128)(2,1)S(1)}, bf16[240,1152]{1,0:T(8,128)(2,1)S(1)}, u32[]{:S(2)}, u32[]{:S(2)}) %collective-permute-start.8) | collective-permute-done | bytes 552992 | tf_op jit(solution)/shard_map/ppermute | solution.py:63
  58.9 0.1 shard_map.108
  58.9 3.7 %collective-permute-start.9 = (bf16[128,1152]{1,0:T(8,128)(2,1)S(1)}, bf16[128,1152]{1,0:T(8,128)(2,1)S(1)}, u32[]{:S(2)}, u32[]{:S(2)}) collective-permute-start(bf16[128,1152]{1,0:T(8,128)(2,1)S(1)} %shard_map.108), channel_id=1, source_target_pairs={{0,8},{1,9},{2,10},{3,11},{4,12},{5,13},{6,14},{7,15},{8,0},{9,1},... | collective-permute-start | bytes 884744 | tf_op jit(solution)/shard_map/ppermute | solution.py:53
  62.6 0.0 collective-permute-done.5.one
  62.6 0.0 collective-permute-done.6.two
  62.6 1.6 %collective-permute-done.7.three = bf16[112,1152]{1,0:T(8,128)(2,1)S(1)} collective-permute-done((bf16[112,1152]{1,0:T(8,128)(2,1)S(1)}, bf16[112,1152]{1,0:T(8,128)(2,1)S(1)}, u32[]{:S(2)}, u32[]{:S(2)}) %collective-permute-start.7) | collective-permute-done | bytes 258080 | tf_op jit(solution)/shard_map/ppermute | solution.py:53
  64.2 0.9 %shard_map.106 = (f32[112,1152]{1,0:T(8,128)}, f32[8,128]{1,0:T(8,128)S(1)}) custom-call(f32[112,1152]{1,0:T(8,128)S(1)} %get-tuple-element.28.kept.token, bf16[112,1152]{1,0:T(8,128)(2,1)S(1)} %collective-permute-done.5.one, bf16[112,1152]{1,0:T(8,128)(2,1)S(1)} %collective-permute-done.6.two, bf16[112,1152]{1,0:T(8,128)(2,1)S(1)} %collective-permute-done.7.three), custom_call_target="tpu_custom_call" | custom-call | flops 9248440320 | bytes 144506880 | tf_op jit(solution)/shard_map/pallas_call | solution.py:82
  65.1 5.6 %collective-permute-done.9.crossed = bf16[128,1152]{1,0:T(8,128)(2,1)S(1)} collective-permute-done((bf16[128,1152]{1,0:T(8,128)(2,1)S(1)}, bf16[128,1152]{1,0:T(8,128)(2,1)S(1)}, u32[]{:S(2)}, u32[]{:S(2)}) %collective-permute-start.9) | collective-permute-done | bytes 294944 | tf_op jit(solution)/shard_map/ppermute | solution.py:53
  70.7 0.9 %shard_map.109 = (f32[112,1152]{1,0:T(8,128)}, f32[1,112]{1,0:T(1,128)}) custom-call(f32[224,1152]{1,0:T(8,128)S(1)} %get-tuple-element.35.late, f32[8,128]{1,0:T(8,128)S(1)} %get-tuple-element.36.late_rows, bf16[240,1152]{1,0:T(8,128)(2,1)S(1)} %collective-permute-done.8.came, bf16[128,1152]{1,0:T(8,128)(2,1)S(1)} %collective-permute-done.9.crossed, ...), custom_call_target="tpu_custom_call" | custom-call | flops 129024 | bytes 2016 | tf_op jit(solution)/shard_map/pallas_call | solution.py:82
  (1 shorter events, 0.0 us)
Async XLA Ops:
  0.6 32.1 %collective-permute-start.1 = (bf16[112,1152]{1,0:T(8,128)(2,1)}, bf16[112,1152]{1,0:T(8,128)(2,1)S(1)}, u32[]{:S(2)}, u32[]{:S(2)}) collective-permute-start(bf16[112,1152]{1,0:T(8,128)(2,1)} %text.1), channel_id=1, source_target_pairs={{0,16},{1,17},{2,18},{3,19},{4,20},{5,21},{6,22},{7,23},{8,24},{9,... | collective-permute-start | bytes 774152 | tf_op jit(solution)/shard_map/ppermute | solution.py:63
  4.5 28.2 %collective-permute-start = (bf16[112,1152]{1,0:T(8,128)(2,1)}, bf16[112,1152]{1,0:T(8,128)(2,1)S(1)}, u32[]{:S(2)}, u32[]{:S(2)}) collective-permute-start(bf16[112,1152]{1,0:T(8,128)(2,1)} %text.1), channel_id=1, source_target_pairs={{0,8},{1,9},{2,10},{3,11},{4,12},{5,13},{6,14},{7,15},{8,0},{9,1},... | collective-permute-start | bytes 774152 | tf_op jit(solution)/shard_map/ppermute | solution.py:53
  9.4 23.3 %collective-permute-start.2 = (bf16[112,1152]{1,0:T(8,128)(2,1)}, bf16[112,1152]{1,0:T(8,128)(2,1)S(1)}, u32[]{:S(2)}, u32[]{:S(2)}) collective-permute-start(bf16[112,1152]{1,0:T(8,128)(2,1)} %text.1), channel_id=1, source_target_pairs={{0,24},{1,25},{2,26},{3,27},{4,28},{5,29},{6,30},{7,31},{8,16},{9,... | collective-permute-start | bytes 774152 | tf_op jit(solution)/shard_map/ppermute | solution.py:63
  28.7 8.0 %collective-permute-start.3 = (bf16[448,1152]{1,0:T(8,128)(2,1)S(1)}, bf16[448,1152]{1,0:T(8,128)(2,1)S(1)}, u32[]{:S(2)}, u32[]{:S(2)}) collective-permute-start(bf16[448,1152]{1,0:T(8,128)(2,1)S(1)} %all_gather.3.images.own), channel_id=1, source_target_pairs={{0,1},{1,0},{2,3},{3,2},{4,5},{5,4},{6,7},{7,6},{8,9},{9,8},{10,11... | collective-permute-start | bytes 3096584 | tf_op jit(solution)/shard_map/ppermute | solution.py:53
  32.7 4.0 %copy-start = (f32[112,1152]{1,0:T(8,128)S(1)}, f32[112,1152]{1,0:T(8,128)}, u32[]{:S(2)}) copy-start(f32[112,1152]{1,0:T(8,128)} %acc.1) | copy-start | bytes 1548292
  34.3 8.0 %collective-permute-start.4 = (bf16[448,1152]{1,0:T(8,128)(2,1)S(1)}, bf16[448,1152]{1,0:T(8,128)(2,1)S(1)}, u32[]{:S(2)}, u32[]{:S(2)}) collective-permute-start(bf16[448,1152]{1,0:T(8,128)(2,1)S(1)} %get-tuple-element.23.texts), channel_id=1, source_target_pairs={{0,1},{1,0},{2,3},{3,2},{4,5},{5,4},{6,7},{7,6},{8,9},{9,8},{10,11... | collective-permute-start | bytes 3096584 | tf_op jit(solution)/shard_map/ppermute | solution.py:53
  38.4 20.4 %collective-permute-start.8 = (bf16[240,1152]{1,0:T(8,128)(2,1)S(1)}, bf16[240,1152]{1,0:T(8,128)(2,1)S(1)}, u32[]{:S(2)}, u32[]{:S(2)}) collective-permute-start(bf16[240,1152]{1,0:T(8,128)(2,1)S(1)} %get-tuple-element.37), channel_id=1, source_target_pairs={{0,16},{1,17},{2,18},{3,19},{4,20},{5,21},{6,22},{7,23},{8,24},{9,... | collective-permute-start | bytes 1658888 | tf_op jit(solution)/shard_map/ppermute | solution.py:63
  45.5 17.1 %collective-permute-start.5 = (bf16[112,1152]{1,0:T(8,128)(2,1)S(1)}, bf16[112,1152]{1,0:T(8,128)(2,1)S(1)}, u32[]{:S(2)}, u32[]{:S(2)}) collective-permute-start(bf16[112,1152]{1,0:T(8,128)(2,1)S(1)} %get-tuple-element.29), channel_id=1, source_target_pairs={{0,2},{1,3},{2,4},{3,5},{4,6},{5,7},{6,0},{7,1},{8,10},{9,11},{10,... | collective-permute-start | bytes 774152 | tf_op jit(solution)/shard_map/ppermute | solution.py:53
  47.4 15.2 %collective-permute-start.6 = (bf16[112,1152]{1,0:T(8,128)(2,1)S(1)}, bf16[112,1152]{1,0:T(8,128)(2,1)S(1)}, u32[]{:S(2)}, u32[]{:S(2)}) collective-permute-start(bf16[112,1152]{1,0:T(8,128)(2,1)S(1)} %get-tuple-element.30), channel_id=1, source_target_pairs={{0,4},{1,5},{2,6},{3,7},{4,0},{5,1},{6,2},{7,3},{8,12},{9,13},{10,... | collective-permute-start | bytes 774152 | tf_op jit(solution)/shard_map/ppermute | solution.py:53
  51.5 12.7 %collective-permute-start.7 = (bf16[112,1152]{1,0:T(8,128)(2,1)S(1)}, bf16[112,1152]{1,0:T(8,128)(2,1)S(1)}, u32[]{:S(2)}, u32[]{:S(2)}) collective-permute-start(bf16[112,1152]{1,0:T(8,128)(2,1)S(1)} %get-tuple-element.31), channel_id=1, source_target_pairs={{0,6},{1,7},{2,0},{3,1},{4,2},{5,3},{6,4},{7,5},{8,14},{9,15},{10,... | collective-permute-start | bytes 774152 | tf_op jit(solution)/shard_map/ppermute | solution.py:53
  58.9 11.8 %collective-permute-start.9 = (bf16[128,1152]{1,0:T(8,128)(2,1)S(1)}, bf16[128,1152]{1,0:T(8,128)(2,1)S(1)}, u32[]{:S(2)}, u32[]{:S(2)}) collective-permute-start(bf16[128,1152]{1,0:T(8,128)(2,1)S(1)} %shard_map.108), channel_id=1, source_target_pairs={{0,8},{1,9},{2,10},{3,11},{4,12},{5,13},{6,14},{7,15},{8,0},{9,1},... | collective-permute-start | bytes 884744 | tf_op jit(solution)/shard_map/ppermute | solution.py:53

commit v5 on v4

--- a/solution.py
+++ b/solution.py
@@ -167,24 +167,22 @@
 
 
 def own_logits(
-    match, text, loss_hbm, given, t1, z, d, images, texts, s0, s1, labels, loss_acc, match_v, sems
+    match, text, loss_hbm, given, t1, images, texts, s0, labels, loss_acc, match_v, sems
 ):
     copies = fetch([(match, match_v), (text, texts.at[:ROWS, :]), (loss_hbm, loss_acc)], sems)
-    for i, t in enumerate((t1, z, d)):
-        texts[(i + 1) * ROWS : (i + 2) * ROWS, :] = t[...]
-    s1[...] = logits_of(texts[LAG:, :], images[...])
+    texts[ROWS:, :] = t1[...]
     for copy in copies:
         copy.wait()
-    s0[...] = logits_of(texts[:LAG, :], images[...])
+    s0[...] = logits_of(texts[...], images[...])
     member = lax.axis_index("grp")
     at = lax.broadcasted_iota(jnp.int32, labels.shape, 0)
     labels[...] = jnp.where(at == 0, labels_of(match_v, member, 0), labels_of(match_v, member, 1))
 
 
-def text_part(weights, halves):
-    return sum(
-        jnp.dot(w[...], x[...], preferred_element_type=F32) for w, x in zip(weights, halves)
-    )
+def late_texts(texts0, z, d, texts):
+    texts[:LAG, :] = texts0[...]
+    texts[LAG : LAG + ROWS, :] = z[...]
+    texts[LAG + ROWS :, :] = d[...]
 
 
 def row_of(column):
@@ -203,7 +201,7 @@
     given, labels, texts, s_own, own, other, acc, loss_acc, w_own, sent, s, w_other, lost
 ):
     member = lax.axis_index("grp")
-    s[...] = logits_of(texts[:LAG, :], other[...])
+    s[...] = logits_of(texts[...], other[...])
     weigh(0, s_own, labels[0:1, :], member, given, w_own, lost, True)
     grad = jnp.dot(w_own[...], own[...], preferred_element_type=F32)
     weigh(0, s, labels[1:2, :], member, given, w_other, lost, False)
@@ -217,21 +215,32 @@
     sent[2 * ROWS :, :ROWS] = tail.astype(BF16)
 
 
+def second_lag(
+    given, labels, texts, own, other, w_own, late, late_rows, s_own, s, w_other, lost
+):
+    member = lax.axis_index("grp")
+    s_own[...] = logits_of(texts[LAG:, :], own[...])
+    s[...] = logits_of(texts[LAG:, :], other[...])
+    weigh(1, s_own, labels[0:1, :], member, given, w_own, lost, True)
+    grad = jnp.dot(w_own[...], own[...], preferred_element_type=F32)
+    weigh(1, s, labels[1:2, :], member, given, w_other, lost, False)
+    grad = grad + jnp.dot(w_other[...], other[...], preferred_element_type=F32)
+    late[...] = given[0:1, 0:1] * grad
+    late_rows[...] = loss_rows(lost)[:8, :]
+
+
 def image_parts(
-    given, labels, w0, s1, texts, beside, own,
-    w1, lost, kept, one, two, three, s_b, w, w_b, total,
+    given, labels, w0, w1, texts, beside, own, token, kept, one, two, three, s_b, w, w_b, total
 ):
     member = lax.axis_index("grp")
     there = member ^ 1
     row = labels[0:1, :]
     s_b[...] = logits_of(beside[...], own[...])
-    weigh(1, s1, row, member, given, w1, lost, True)
     w[:LAG, :] = w0[...]
     w[LAG:, :] = w1[...]
-    part = image_part(w[...], texts[...])
     weigh(0, s_b.at[:LAG, :], row, there, given, w_b.at[:LAG, :])
     weigh(1, s_b.at[LAG:, :], row, there, given, w_b.at[LAG:, :])
-    part = part + image_part(w_b[...], beside[...])
+    part = image_part(w[...], texts[...]) + image_part(w_b[...], beside[...])
     total[...] = given[0:1, 0:1] * part
     y = (member // CORE) & (Y - 1)
     for step, out in enumerate((kept, one, two, three)):
@@ -239,17 +248,6 @@
         out[...] = total[pl.ds(start, ROWS), :].astype(out.dtype)
 
 
-def second_lag(
-    given, labels, texts, w_own, lost_own, own, other, token, late, late_rows, s, w_other, lost
-):
-    member = lax.axis_index("grp")
-    lost[...] = lost_own[...]
-    s[...] = logits_of(texts[LAG:, :], other[...])
-    weigh(1, s, labels[1:2, :], member, given, w_other, lost, False)
-    late[...] = given[0:1, 0:1] * text_part((w_own, w_other), (own, other))
-    late_rows[...] = loss_rows(lost)[:8, :]
-
-
 def across(late, late_rows, came, sent):
     sent[:ROWS, :] = (late[ROWS:, :] + came[ROWS : 2 * ROWS, :].astype(F32)).astype(BF16)
     sent[ROWS:, :] = jnp.zeros((TAIL, sent.shape[1]), BF16)
@@ -286,38 +284,39 @@
     block = shape(ROWS, width, BF16)
     logits = held(LAG, SETS, F32)
     weights = held(LAG, SETS, BF16)
-    texts, s0, s1, labels, loss_acc = call(
+    texts0, s0, labels, loss_acc = call(
         own_logits,
-        [shape(2 * LAG, width, BF16), logits, logits, held(8, SETS, jnp.int32), held(1, ROWS, F32)],
-        [match, text_held, text_loss_acc.reshape(1, ROWS), given, text_x, text_z, text_d, images],
+        [shape(LAG, width, BF16), logits, held(8, SETS, jnp.int32), held(1, ROWS, F32)],
+        [match, text_held, text_loss_acc.reshape(1, ROWS), given, text_x, images],
         2 * big,
         [pltpu.VMEM(match.shape, jnp.int32), pltpu.SemaphoreType.DMA((3,))],
         far=3,
     )
-    texts_beside = to_member(texts, across_core)
     w0, ahead = call(
         first_lag,
         [weights, shape(LAG + TAIL, width, BF16)],
-        [given, labels, texts, s0, images, images_other, text_grad_acc, loss_acc],
+        [given, labels, texts0, s0, images, images_other, text_grad_acc, loss_acc],
         3 * big,
         [logits, weights, held(LAG, 1, F32)],
     )
     came = to_next_group(ahead, stay)
-    w1, lost1, kept, *sent = call(
+    (texts,) = call(late_texts, [shape(2 * LAG, width, BF16)], [texts0, text_z, text_d], big // 8)
+    texts_beside = to_member(texts, across_core)
+    w1, late, late_rows = call(
+        second_lag,
+        [weights, held(LAG, width, F32), held(8, 128, F32)],
+        [given, labels, texts, images, images_other],
+        4 * big,
+        [logits, logits, weights, held(LAG, 1, F32)],
+    )
+    kept, *sent = call(
         image_parts,
-        [weights, held(LAG, 1, F32), held(ROWS, width, F32), block, block, block],
-        [given, labels, w0, s1, texts, texts_beside, images],
+        [held(ROWS, width, F32), block, block, block],
+        [given, labels, w0, w1, texts, texts_beside, images, late_rows],
         6 * big,
         [held(2 * LAG, SETS, F32), held(2 * LAG, SETS, BF16), held(2 * LAG, SETS, BF16), held(SETS, width, F32)],
     )
     arrived = [to_member(part, along_y(i + 1)) for i, part in enumerate(sent)]
-    late, late_rows = call(
-        second_lag,
-        [held(LAG, width, F32), held(8, 128, F32)],
-        [given, labels, texts, w1, lost1, images, images_other, kept],
-        3 * big,
-        [logits, weights, held(LAG, 1, F32)],
-    )
     (crossing,) = call(across, [shape(ROWS + TAIL, width, BF16)], [late, late_rows, came], ROWS * width)
     crossed = to_member(crossing, across_x)
     image_grad, token = call(

time: 72 us -> 72 us (level)
  waiting for transfers between devices: 8.62 us -> 7.74 us
    pallas_call x7 -> x8, Pallas kernels: 9.8 us -> 10.1 us  [call(): pl.pallas_call(body, out_shape=outs, in_specs=[HBM if i < far else SMEM i...]
  transfers between devices with their start and end apart: 10 -> 10, of which waited for: 3 -> 3; matrix products, arithmetic and copies ran while one was open for 0% -> 0% of each run, Pallas kernels for 12% -> 13%
where the time goes in v5:
time: 72 us; the launch traced here: 71.5 us
  starting transfers between devices  35.4 us (49%)
  blocking collectives  15.4 us (21%)
  Pallas kernels  10.1 us (14%)
  waiting for transfers between devices  7.74 us (11%)
  between operations  2.76 us (4%)
    ppermute x7, starting transfers between devices, to_member(): return lax.ppermute(block, 'grp', member_route(move))  23.9 us
    all_gather x1, blocking collectives, gather_y(): return lax.all_gather(block, 'grp', axis_index_groups=groups, tiled=True)  15.4 us
    ppermute x3, starting transfers between devices, to_next_group(): return lax.ppermute(block, ('blk', 'grp'), route)  11.6 us
    pallas_call x8, Pallas kernels, call(): pl.pallas_call(body, out_shape=outs, in_specs=[HBM if i < far else SMEM i...  10.1 us
    ppermute x7, waiting for transfers between devices, to_member(): return lax.ppermute(block, 'grp', member_route(move))  6.8 us
  transfers between devices with their start and end apart: 10, of which 3 were waited for; matrix products, arithmetic and copies ran while one was open for 0% of the time, Pallas kernels for 13%

profile of v5, /device:TPU:8, one launch (start us, length us, event | category | flops | bytes accessed | tf_op | source)
XLA Modules:
  0.0 71.5 jit_solution(7646241019672782687)
XLA Ops:
  0.6 4.9 %collective-permute-start = (bf16[112,1152]{1,0:T(8,128)(2,1)}, bf16[112,1152]{1,0:T(8,128)(2,1)S(1)}, u32[]{:S(2)}, u32[]{:S(2)}) collective-permute-start(bf16[112,1152]{1,0:T(8,128)(2,1)} %text.1), channel_id=1, source_target_pairs={{0,8},{1,9},{2,10},{3,11},{4,12},{5,13},{6,14},{7,15},{8,0},{9,1},... | collective-permute-start | bytes 774152 | tf_op jit(solution)/shard_map/ppermute | solution.py:53
  5.6 3.8 %collective-permute-start.3 = (bf16[112,1152]{1,0:T(8,128)(2,1)}, bf16[112,1152]{1,0:T(8,128)(2,1)S(1)}, u32[]{:S(2)}, u32[]{:S(2)}) collective-permute-start(bf16[112,1152]{1,0:T(8,128)(2,1)} %text.1), channel_id=1, source_target_pairs={{0,24},{1,25},{2,26},{3,27},{4,28},{5,29},{6,30},{7,31},{8,16},{9,... | collective-permute-start | bytes 774152 | tf_op jit(solution)/shard_map/ppermute | solution.py:63
  9.3 3.8 %collective-permute-start.2 = (bf16[112,1152]{1,0:T(8,128)(2,1)}, bf16[112,1152]{1,0:T(8,128)(2,1)S(1)}, u32[]{:S(2)}, u32[]{:S(2)}) collective-permute-start(bf16[112,1152]{1,0:T(8,128)(2,1)} %text.1), channel_id=1, source_target_pairs={{0,16},{1,17},{2,18},{3,19},{4,20},{5,21},{6,22},{7,23},{8,24},{9,... | collective-permute-start | bytes 774152 | tf_op jit(solution)/shard_map/ppermute | solution.py:63
  13.2 15.4 %all_gather.3.images.own = bf16[448,1152]{1,0:T(8,128)(2,1)S(1)} all-gather(bf16[112,1152]{1,0:T(8,128)(2,1)} %param.8), channel_id=1, replica_groups={{0,2,4,6},{1,3,5,7},{8,10,12,14},{9,11,13,15},{16,18,20,22},{17,19,21,2..., dimensions={0}, use_global_device_ids=true | all-gather | bytes 1290240 | tf_op jit(solution)/shard_map/all_gather | solution.py:68
  28.6 1.9 %collective-permute-start.1 = (bf16[448,1152]{1,0:T(8,128)(2,1)S(1)}, bf16[448,1152]{1,0:T(8,128)(2,1)S(1)}, u32[]{:S(2)}, u32[]{:S(2)}) collective-permute-start(bf16[448,1152]{1,0:T(8,128)(2,1)S(1)} %all_gather.3.images.own), channel_id=1, source_target_pairs={{0,1},{1,0},{2,3},{3,2},{4,5},{5,4},{6,7},{7,6},{8,9},{9,8},{10,11... | collective-permute-start | bytes 3096584 | tf_op jit(solution)/shard_map/ppermute | solution.py:53
  32.5 0.1 maximum_bitcast_fusion.given
  32.5 0.0 collective-permute-done.t1
  32.6 1.5 %shard_map.103 = (bf16[224,1152]{1,0:T(8,128)(2,1)S(1)}, f32[224,448]{1,0:T(8,128)S(1)}, s32[8,448]{1,0:T(8,128)S(1)}, f32[1,112]{1,0:T(1,128)S(1)}) custom-call(s32[14,128]{1,0:T(8,128)} %bitcast.6, bf16[112,1152]{1,0:T(8,128)(2,1)} %text.1, f32[1,112]{1,0:T(1,128)} %bitcast.7, f32[1,128]{1,0:T(1,128)S(1)} %maximum_bitcast_fusion.given, ...), custom_call_target="tpu_custom_call" | custom-call | flops 462422016 | bytes 7225344 | tf_op jit(solution)/shard_map/pallas_call | solution.py:82
  34.1 0.0 collective-permute-done.3.d
  34.1 0.0 collective-permute-done.2.z
  34.1 0.0 copy-start
  34.1 0.1 shard_map.105.texts
  34.2 2.5 %collective-permute-start.4 = (bf16[448,1152]{1,0:T(8,128)(2,1)S(1)}, bf16[448,1152]{1,0:T(8,128)(2,1)S(1)}, u32[]{:S(2)}, u32[]{:S(2)}) collective-permute-start(bf16[448,1152]{1,0:T(8,128)(2,1)S(1)} %shard_map.105.texts), channel_id=1, source_target_pairs={{0,1},{1,0},{2,3},{3,2},{4,5},{5,4},{6,7},{7,6},{8,9},{9,8},{10,11... | collective-permute-start | bytes 3096584 | tf_op jit(solution)/shard_map/ppermute | solution.py:53
  36.7 0.0 collective-permute-done.1.other
  36.7 0.0 copy-done
  36.7 1.7 %shard_map.104 = (bf16[224,448]{1,0:T(8,128)(2,1)S(1)}, bf16[240,1152]{1,0:T(8,128)(2,1)S(1)}) custom-call(f32[1,128]{1,0:T(1,128)S(1)} %maximum_bitcast_fusion.given, s32[8,448]{1,0:T(8,128)S(1)} %get-tuple-element.20.labels, bf16[224,1152]{1,0:T(8,128)(2,1)S(1)} %get-tuple-element.21.texts.texts0, f32[224,448]{1,0:T(8,128)S(1)} %get-tuple-element.22.s_own, ...), custom_call_target="tpu_custom_call" | custom-call | flops 693633024 | bytes 10838016 | tf_op jit(solution)/shard_map/pallas_call | solution.py:82
  38.5 4.0 %collective-permute-start.8 = (bf16[240,1152]{1,0:T(8,128)(2,1)S(1)}, bf16[240,1152]{1,0:T(8,128)(2,1)S(1)}, u32[]{:S(2)}, u32[]{:S(2)}) collective-permute-start(bf16[240,1152]{1,0:T(8,128)(2,1)S(1)} %get-tuple-element.33), channel_id=1, source_target_pairs={{0,16},{1,17},{2,18},{3,19},{4,20},{5,21},{6,22},{7,23},{8,24},{9,... | collective-permute-start | bytes 1658888 | tf_op jit(solution)/shard_map/ppermute | solution.py:63
  42.4 1.9 %shard_map.106 = (bf16[224,448]{1,0:T(8,128)(2,1)S(1)}, f32[224,1152]{1,0:T(8,128)S(1)}, f32[8,128]{1,0:T(8,128)S(1)}) custom-call(f32[1,128]{1,0:T(1,128)S(1)} %maximum_bitcast_fusion.given, s32[8,448]{1,0:T(8,128)S(1)} %get-tuple-element.20.labels, bf16[448,1152]{1,0:T(8,128)(2,1)S(1)} %shard_map.105.texts, bf16[448,1152]{1,0:T(8,128)(2,1)S(1)} %all_gather.3.images.own, ...), custom_call_target="tpu_custom_call" | custom-call | flops 924844032 | bytes 14450688 | tf_op jit(solution)/shard_map/pallas_call | solution.py:82
  44.4 0.0 collective-permute-done.4.beside
  44.4 3.0 %shard_map.107 = (f32[112,1152]{1,0:T(8,128)S(1)}, bf16[112,1152]{1,0:T(8,128)(2,1)S(1)}, bf16[112,1152]{1,0:T(8,128)(2,1)S(1)}, bf16[112,1152]{1,0:T(8,128)(2,1)S(1)}) custom-call(f32[1,128]{1,0:T(1,128)S(1)} %maximum_bitcast_fusion.given, s32[8,448]{1,0:T(8,128)S(1)} %get-tuple-element.20.labels, bf16[224,448]{1,0:T(8,128)(2,1)S(1)} %get-tuple-element.24.w0, ...), custom_call_target="tpu_custom_call" | custom-call | flops 1387266048 | bytes 21676032 | tf_op jit(solution)/shard_map/pallas_call | solution.py:82
  47.4 1.9 %collective-permute-start.5 = (bf16[112,1152]{1,0:T(8,128)(2,1)S(1)}, bf16[112,1152]{1,0:T(8,128)(2,1)S(1)}, u32[]{:S(2)}, u32[]{:S(2)}) collective-permute-start(bf16[112,1152]{1,0:T(8,128)(2,1)S(1)} %get-tuple-element.28), channel_id=1, source_target_pairs={{0,2},{1,3},{2,4},{3,5},{4,6},{5,7},{6,0},{7,1},{8,10},{9,11},{10,... | collective-permute-start | bytes 774152 | tf_op jit(solution)/shard_map/ppermute | solution.py:53
  49.3 4.0 %collective-permute-start.6 = (bf16[112,1152]{1,0:T(8,128)(2,1)S(1)}, bf16[112,1152]{1,0:T(8,128)(2,1)S(1)}, u32[]{:S(2)}, u32[]{:S(2)}) collective-permute-start(bf16[112,1152]{1,0:T(8,128)(2,1)S(1)} %get-tuple-element.29), channel_id=1, source_target_pairs={{0,4},{1,5},{2,6},{3,7},{4,0},{5,1},{6,2},{7,3},{8,12},{9,13},{10,... | collective-permute-start | bytes 774152 | tf_op jit(solution)/shard_map/ppermute | solution.py:53
  53.4 4.5 %collective-permute-start.7 = (bf16[112,1152]{1,0:T(8,128)(2,1)S(1)}, bf16[112,1152]{1,0:T(8,128)(2,1)S(1)}, u32[]{:S(2)}, u32[]{:S(2)}) collective-permute-start(bf16[112,1152]{1,0:T(8,128)(2,1)S(1)} %get-tuple-element.30), channel_id=1, source_target_pairs={{0,6},{1,7},{2,0},{3,1},{4,2},{5,3},{6,4},{7,5},{8,14},{9,15},{10,... | collective-permute-start | bytes 774152 | tf_op jit(solution)/shard_map/ppermute | solution.py:53
  57.9 0.9 %collective-permute-done.8.came = bf16[240,1152]{1,0:T(8,128)(2,1)S(1)} collective-permute-done((bf16[240,1152]{1,0:T(8,128)(2,1)S(1)}, bf16[240,1152]{1,0:T(8,128)(2,1)S(1)}, u32[]{:S(2)}, u32[]{:S(2)}) %collective-permute-start.8) | collective-permute-done | bytes 552992 | tf_op jit(solution)/shard_map/ppermute | solution.py:63
  58.8 4.1 %collective-permute-start.9 = (bf16[128,1152]{1,0:T(8,128)(2,1)S(1)}, bf16[128,1152]{1,0:T(8,128)(2,1)S(1)}, u32[]{:S(2)}, u32[]{:S(2)}) collective-permute-start(bf16[128,1152]{1,0:T(8,128)(2,1)S(1)} %shard_map.109), channel_id=1, source_target_pairs={{0,8},{1,9},{2,10},{3,11},{4,12},{5,13},{6,14},{7,15},{8,0},{9,1},... | collective-permute-start | bytes 884744 | tf_op jit(solution)/shard_map/ppermute | solution.py:53
  62.9 0.0 collective-permute-done.5.one
  62.9 0.0 collective-permute-done.6.two
  62.9 3.2 %collective-permute-done.7.three = bf16[112,1152]{1,0:T(8,128)(2,1)S(1)} collective-permute-done((bf16[112,1152]{1,0:T(8,128)(2,1)S(1)}, bf16[112,1152]{1,0:T(8,128)(2,1)S(1)}, u32[]{:S(2)}, u32[]{:S(2)}) %collective-permute-start.7) | collective-permute-done | bytes 258080 | tf_op jit(solution)/shard_map/ppermute | solution.py:53
  66.1 0.9 %shard_map.108 = (f32[112,1152]{1,0:T(8,128)}, f32[8,128]{1,0:T(8,128)S(1)}) custom-call(f32[112,1152]{1,0:T(8,128)S(1)} %get-tuple-element.27.kept, bf16[112,1152]{1,0:T(8,128)(2,1)S(1)} %collective-permute-done.5.one, bf16[112,1152]{1,0:T(8,128)(2,1)S(1)} %collective-permute-done.6.two, bf16[112,1152]{1,0:T(8,128)(2,1)S(1)} %collective-permute-done.7.three), custom_call_target="tpu_custom_call" | custom-call | flops 9248440320 | bytes 144506880 | tf_op jit(solution)/shard_map/pallas_call | solution.py:82
  67.0 3.6 %collective-permute-done.9.crossed = bf16[128,1152]{1,0:T(8,128)(2,1)S(1)} collective-permute-done((bf16[128,1152]{1,0:T(8,128)(2,1)S(1)}, bf16[128,1152]{1,0:T(8,128)(2,1)S(1)}, u32[]{:S(2)}, u32[]{:S(2)}) %collective-permute-start.9) | collective-permute-done | bytes 294944 | tf_op jit(solution)/shard_map/ppermute | solution.py:53
  70.6 0.9 %shard_map.110 = (f32[112,1152]{1,0:T(8,128)}, f32[1,112]{1,0:T(1,128)}) custom-call(f32[224,1152]{1,0:T(8,128)S(1)} %get-tuple-element.32.late, f32[8,128]{1,0:T(8,128)S(1)} %get-tuple-element.26.token.late_rows, bf16[240,1152]{1,0:T(8,128)(2,1)S(1)} %collective-permute-done.8.came, bf16[128,1152]{1,0:T(8,128)(2,1)S(1)} %collective-permute-done.9.crossed, ...), custom_call_target="tpu_custom_call" | custom-call | flops 129024 | bytes 2016 | tf_op jit(solution)/shard_map/pallas_call | solution.py:82
  (2 shorter events, 0.1 us)
Async XLA Ops:
  0.6 31.9 %collective-permute-start = (bf16[112,1152]{1,0:T(8,128)(2,1)}, bf16[112,1152]{1,0:T(8,128)(2,1)S(1)}, u32[]{:S(2)}, u32[]{:S(2)}) collective-permute-start(bf16[112,1152]{1,0:T(8,128)(2,1)} %text.1), channel_id=1, source_target_pairs={{0,8},{1,9},{2,10},{3,11},{4,12},{5,13},{6,14},{7,15},{8,0},{9,1},... | collective-permute-start | bytes 774152 | tf_op jit(solution)/shard_map/ppermute | solution.py:53
  5.6 28.5 %collective-permute-start.3 = (bf16[112,1152]{1,0:T(8,128)(2,1)}, bf16[112,1152]{1,0:T(8,128)(2,1)S(1)}, u32[]{:S(2)}, u32[]{:S(2)}) collective-permute-start(bf16[112,1152]{1,0:T(8,128)(2,1)} %text.1), channel_id=1, source_target_pairs={{0,24},{1,25},{2,26},{3,27},{4,28},{5,29},{6,30},{7,31},{8,16},{9,... | collective-permute-start | bytes 774152 | tf_op jit(solution)/shard_map/ppermute | solution.py:63
  9.3 24.7 %collective-permute-start.2 = (bf16[112,1152]{1,0:T(8,128)(2,1)}, bf16[112,1152]{1,0:T(8,128)(2,1)S(1)}, u32[]{:S(2)}, u32[]{:S(2)}) collective-permute-start(bf16[112,1152]{1,0:T(8,128)(2,1)} %text.1), channel_id=1, source_target_pairs={{0,16},{1,17},{2,18},{3,19},{4,20},{5,21},{6,22},{7,23},{8,24},{9,... | collective-permute-start | bytes 774152 | tf_op jit(solution)/shard_map/ppermute | solution.py:63
  28.6 8.1 %collective-permute-start.1 = (bf16[448,1152]{1,0:T(8,128)(2,1)S(1)}, bf16[448,1152]{1,0:T(8,128)(2,1)S(1)}, u32[]{:S(2)}, u32[]{:S(2)}) collective-permute-start(bf16[448,1152]{1,0:T(8,128)(2,1)S(1)} %all_gather.3.images.own), channel_id=1, source_target_pairs={{0,1},{1,0},{2,3},{3,2},{4,5},{5,4},{6,7},{7,6},{8,9},{9,8},{10,11... | collective-permute-start | bytes 3096584 | tf_op jit(solution)/shard_map/ppermute | solution.py:53
  34.1 2.7 %copy-start = (f32[112,1152]{1,0:T(8,128)S(1)}, f32[112,1152]{1,0:T(8,128)}, u32[]{:S(2)}) copy-start(f32[112,1152]{1,0:T(8,128)} %acc.1) | copy-start | bytes 1548292
  34.2 10.2 %collective-permute-start.4 = (bf16[448,1152]{1,0:T(8,128)(2,1)S(1)}, bf16[448,1152]{1,0:T(8,128)(2,1)S(1)}, u32[]{:S(2)}, u32[]{:S(2)}) collective-permute-start(bf16[448,1152]{1,0:T(8,128)(2,1)S(1)} %shard_map.105.texts), channel_id=1, source_target_pairs={{0,1},{1,0},{2,3},{3,2},{4,5},{5,4},{6,7},{7,6},{8,9},{9,8},{10,11... | collective-permute-start | bytes 3096584 | tf_op jit(solution)/shard_map/ppermute | solution.py:53
  38.5 20.3 %collective-permute-start.8 = (bf16[240,1152]{1,0:T(8,128)(2,1)S(1)}, bf16[240,1152]{1,0:T(8,128)(2,1)S(1)}, u32[]{:S(2)}, u32[]{:S(2)}) collective-permute-start(bf16[240,1152]{1,0:T(8,128)(2,1)S(1)} %get-tuple-element.33), channel_id=1, source_target_pairs={{0,16},{1,17},{2,18},{3,19},{4,20},{5,21},{6,22},{7,23},{8,24},{9,... | collective-permute-start | bytes 1658888 | tf_op jit(solution)/shard_map/ppermute | solution.py:63
  47.4 15.5 %collective-permute-start.5 = (bf16[112,1152]{1,0:T(8,128)(2,1)S(1)}, bf16[112,1152]{1,0:T(8,128)(2,1)S(1)}, u32[]{:S(2)}, u32[]{:S(2)}) collective-permute-start(bf16[112,1152]{1,0:T(8,128)(2,1)S(1)} %get-tuple-element.28), channel_id=1, source_target_pairs={{0,2},{1,3},{2,4},{3,5},{4,6},{5,7},{6,0},{7,1},{8,10},{9,11},{10,... | collective-permute-start | bytes 774152 | tf_op jit(solution)/shard_map/ppermute | solution.py:53
  49.3 13.6 %collective-permute-start.6 = (bf16[112,1152]{1,0:T(8,128)(2,1)S(1)}, bf16[112,1152]{1,0:T(8,128)(2,1)S(1)}, u32[]{:S(2)}, u32[]{:S(2)}) collective-permute-start(bf16[112,1152]{1,0:T(8,128)(2,1)S(1)} %get-tuple-element.29), channel_id=1, source_target_pairs={{0,4},{1,5},{2,6},{3,7},{4,0},{5,1},{6,2},{7,3},{8,12},{9,13},{10,... | collective-permute-start | bytes 774152 | tf_op jit(solution)/shard_map/ppermute | solution.py:53
  53.4 12.7 %collective-permute-start.7 = (bf16[112,1152]{1,0:T(8,128)(2,1)S(1)}, bf16[112,1152]{1,0:T(8,128)(2,1)S(1)}, u32[]{:S(2)}, u32[]{:S(2)}) collective-permute-start(bf16[112,1152]{1,0:T(8,128)(2,1)S(1)} %get-tuple-element.30), channel_id=1, source_target_pairs={{0,6},{1,7},{2,0},{3,1},{4,2},{5,3},{6,4},{7,5},{8,14},{9,15},{10,... | collective-permute-start | bytes 774152 | tf_op jit(solution)/shard_map/ppermute | solution.py:53
  58.8 11.8 %collective-permute-start.9 = (bf16[128,1152]{1,0:T(8,128)(2,1)S(1)}, bf16[128,1152]{1,0:T(8,128)(2,1)S(1)}, u32[]{:S(2)}, u32[]{:S(2)}) collective-permute-start(bf16[128,1152]{1,0:T(8,128)(2,1)S(1)} %shard_map.109), channel_id=1, source_target_pairs={{0,8},{1,9},{2,10},{3,11},{4,12},{5,13},{6,14},{7,15},{8,0},{9,1},... | collective-permute-start | bytes 884744 | tf_op jit(solution)/shard_map/ppermute | solution.py:53

commit v6 on v5

--- a/solution.py
+++ b/solution.py
@@ -137,7 +137,7 @@
         paired = (rows + base) == labels
         t = jnp.where(paired, -logits, logits)
         e = jnp.exp2(-jnp.abs(t))
-        more = jnp.where(e < 1e-4, LOG2E * e, jnp.log2(1.0 + e))
+        more = jnp.where(e < 1e-4, LOG2E * e * (1.0 - 0.5 * e), jnp.log2(1.0 + e))
         lost = jnp.maximum(t, 0.0) + more
         sig = jnp.exp2(t - lost)
         w_ref[pl.ds(start, CHUNK), :] = jnp.where(paired, -sig, sig).astype(BF16)
@@ -238,14 +238,15 @@
     s_b[...] = logits_of(beside[...], own[...])
     w[:LAG, :] = w0[...]
     w[LAG:, :] = w1[...]
+    total[...] = image_part(w[...], texts[...])
     weigh(0, s_b.at[:LAG, :], row, there, given, w_b.at[:LAG, :])
     weigh(1, s_b.at[LAG:, :], row, there, given, w_b.at[LAG:, :])
-    part = image_part(w[...], texts[...]) + image_part(w_b[...], beside[...])
-    total[...] = given[0:1, 0:1] * part
+    total[...] += image_part(w_b[...], beside[...])
+    factor = given[0:1, 0:1]
     y = (member // CORE) & (Y - 1)
     for step, out in enumerate((kept, one, two, three)):
         start = pl.multiple_of(((y + step) & (Y - 1)) * ROWS, 16)
-        out[...] = total[pl.ds(start, ROWS), :].astype(out.dtype)
+        out[...] = (factor * total[pl.ds(start, ROWS), :]).astype(out.dtype)
 
 
 def across(late, late_rows, came, sent):

time: 72 us -> 72.1 us (level)
  no operation moved by 1% of the time
where the time goes in v6:
time: 72.1 us; the launch traced here: 71.6 us
  starting transfers between devices  35.4 us (49%)
  blocking collectives  15.4 us (21%)
  Pallas kernels  10.1 us (14%)
  waiting for transfers between devices  7.89 us (11%)
  between operations  2.76 us (4%)
    ppermute x7, starting transfers between devices, to_member(): return lax.ppermute(block, 'grp', member_route(move))  23.8 us
    all_gather x1, blocking collectives, gather_y(): return lax.all_gather(block, 'grp', axis_index_groups=groups, tiled=True)  15.4 us
    ppermute x3, starting transfers between devices, to_next_group(): return lax.ppermute(block, ('blk', 'grp'), route)  11.6 us
    pallas_call x8, Pallas kernels, call(): pl.pallas_call(body, out_shape=outs, in_specs=[HBM if i < far else SMEM i...  10.1 us
    ppermute x7, waiting for transfers between devices, to_member(): return lax.ppermute(block, 'grp', member_route(move))  6.87 us
  transfers between devices with their start and end apart: 10, of which 3 were waited for; matrix products, arithmetic and copies ran while one was open for 0% of the time, Pallas kernels for 13%

profile of v6, /device:TPU:8, one launch (start us, length us, event | category | flops | bytes accessed | tf_op | source)
XLA Modules:
  0.0 71.6 jit_solution(14270441615555021919)
XLA Ops:
  0.6 4.9 %collective-permute-start = (bf16[112,1152]{1,0:T(8,128)(2,1)}, bf16[112,1152]{1,0:T(8,128)(2,1)S(1)}, u32[]{:S(2)}, u32[]{:S(2)}) collective-permute-start(bf16[112,1152]{1,0:T(8,128)(2,1)} %text.1), channel_id=1, source_target_pairs={{0,8},{1,9},{2,10},{3,11},{4,12},{5,13},{6,14},{7,15},{8,0},{9,1},... | collective-permute-start | bytes 774152 | tf_op jit(solution)/shard_map/ppermute | solution.py:53
  5.6 3.8 %collective-permute-start.3 = (bf16[112,1152]{1,0:T(8,128)(2,1)}, bf16[112,1152]{1,0:T(8,128)(2,1)S(1)}, u32[]{:S(2)}, u32[]{:S(2)}) collective-permute-start(bf16[112,1152]{1,0:T(8,128)(2,1)} %text.1), channel_id=1, source_target_pairs={{0,24},{1,25},{2,26},{3,27},{4,28},{5,29},{6,30},{7,31},{8,16},{9,... | collective-permute-start | bytes 774152 | tf_op jit(solution)/shard_map/ppermute | solution.py:63
  9.3 3.8 %collective-permute-start.2 = (bf16[112,1152]{1,0:T(8,128)(2,1)}, bf16[112,1152]{1,0:T(8,128)(2,1)S(1)}, u32[]{:S(2)}, u32[]{:S(2)}) collective-permute-start(bf16[112,1152]{1,0:T(8,128)(2,1)} %text.1), channel_id=1, source_target_pairs={{0,16},{1,17},{2,18},{3,19},{4,20},{5,21},{6,22},{7,23},{8,24},{9,... | collective-permute-start | bytes 774152 | tf_op jit(solution)/shard_map/ppermute | solution.py:63
  13.2 15.4 %all_gather.3.images.own = bf16[448,1152]{1,0:T(8,128)(2,1)S(1)} all-gather(bf16[112,1152]{1,0:T(8,128)(2,1)} %param.8), channel_id=1, replica_groups={{0,2,4,6},{1,3,5,7},{8,10,12,14},{9,11,13,15},{16,18,20,22},{17,19,21,2..., dimensions={0}, use_global_device_ids=true | all-gather | bytes 1290240 | tf_op jit(solution)/shard_map/all_gather | solution.py:68
  28.6 1.9 %collective-permute-start.1 = (bf16[448,1152]{1,0:T(8,128)(2,1)S(1)}, bf16[448,1152]{1,0:T(8,128)(2,1)S(1)}, u32[]{:S(2)}, u32[]{:S(2)}) collective-permute-start(bf16[448,1152]{1,0:T(8,128)(2,1)S(1)} %all_gather.3.images.own), channel_id=1, source_target_pairs={{0,1},{1,0},{2,3},{3,2},{4,5},{5,4},{6,7},{7,6},{8,9},{9,8},{10,11... | collective-permute-start | bytes 3096584 | tf_op jit(solution)/shard_map/ppermute | solution.py:53
  32.5 0.1 maximum_bitcast_fusion.given
  32.5 0.0 collective-permute-done.t1
  32.6 1.5 %shard_map.103 = (bf16[224,1152]{1,0:T(8,128)(2,1)S(1)}, f32[224,448]{1,0:T(8,128)S(1)}, s32[8,448]{1,0:T(8,128)S(1)}, f32[1,112]{1,0:T(1,128)S(1)}) custom-call(s32[14,128]{1,0:T(8,128)} %bitcast.6, bf16[112,1152]{1,0:T(8,128)(2,1)} %text.1, f32[1,112]{1,0:T(1,128)} %bitcast.7, f32[1,128]{1,0:T(1,128)S(1)} %maximum_bitcast_fusion.given, ...), custom_call_target="tpu_custom_call" | custom-call | flops 462422016 | bytes 7225344 | tf_op jit(solution)/shard_map/pallas_call | solution.py:82
  34.1 0.0 collective-permute-done.3.d
  34.1 0.0 collective-permute-done.2.z
  34.1 0.0 copy-start
  34.1 0.1 shard_map.105.texts
  34.2 2.5 %collective-permute-start.4 = (bf16[448,1152]{1,0:T(8,128)(2,1)S(1)}, bf16[448,1152]{1,0:T(8,128)(2,1)S(1)}, u32[]{:S(2)}, u32[]{:S(2)}) collective-permute-start(bf16[448,1152]{1,0:T(8,128)(2,1)S(1)} %shard_map.105.texts), channel_id=1, source_target_pairs={{0,1},{1,0},{2,3},{3,2},{4,5},{5,4},{6,7},{7,6},{8,9},{9,8},{10,11... | collective-permute-start | bytes 3096584 | tf_op jit(solution)/shard_map/ppermute | solution.py:53
  36.7 0.0 collective-permute-done.1.other
  36.7 0.0 copy-done
  36.7 1.8 %shard_map.104 = (bf16[224,448]{1,0:T(8,128)(2,1)S(1)}, bf16[240,1152]{1,0:T(8,128)(2,1)S(1)}) custom-call(f32[1,128]{1,0:T(1,128)S(1)} %maximum_bitcast_fusion.given, s32[8,448]{1,0:T(8,128)S(1)} %get-tuple-element.20.labels, bf16[224,1152]{1,0:T(8,128)(2,1)S(1)} %get-tuple-element.21.texts.texts0, f32[224,448]{1,0:T(8,128)S(1)} %get-tuple-element.22.s_own, ...), custom_call_target="tpu_custom_call" | custom-call | flops 693633024 | bytes 10838016 | tf_op jit(solution)/shard_map/pallas_call | solution.py:82
  38.6 4.0 %collective-permute-start.8 = (bf16[240,1152]{1,0:T(8,128)(2,1)S(1)}, bf16[240,1152]{1,0:T(8,128)(2,1)S(1)}, u32[]{:S(2)}, u32[]{:S(2)}) collective-permute-start(bf16[240,1152]{1,0:T(8,128)(2,1)S(1)} %get-tuple-element.33), channel_id=1, source_target_pairs={{0,16},{1,17},{2,18},{3,19},{4,20},{5,21},{6,22},{7,23},{8,24},{9,... | collective-permute-start | bytes 1658888 | tf_op jit(solution)/shard_map/ppermute | solution.py:63
  42.5 2.0 %shard_map.106 = (bf16[224,448]{1,0:T(8,128)(2,1)S(1)}, f32[224,1152]{1,0:T(8,128)S(1)}, f32[8,128]{1,0:T(8,128)S(1)}) custom-call(f32[1,128]{1,0:T(1,128)S(1)} %maximum_bitcast_fusion.given, s32[8,448]{1,0:T(8,128)S(1)} %get-tuple-element.20.labels, bf16[448,1152]{1,0:T(8,128)(2,1)S(1)} %shard_map.105.texts, bf16[448,1152]{1,0:T(8,128)(2,1)S(1)} %all_gather.3.images.own, ...), custom_call_target="tpu_custom_call" | custom-call | flops 924844032 | bytes 14450688 | tf_op jit(solution)/shard_map/pallas_call | solution.py:82
  44.6 0.0 collective-permute-done.4.beside
  44.6 2.8 %shard_map.107 = (f32[112,1152]{1,0:T(8,128)S(1)}, bf16[112,1152]{1,0:T(8,128)(2,1)S(1)}, bf16[112,1152]{1,0:T(8,128)(2,1)S(1)}, bf16[112,1152]{1,0:T(8,128)(2,1)S(1)}) custom-call(f32[1,128]{1,0:T(1,128)S(1)} %maximum_bitcast_fusion.given, s32[8,448]{1,0:T(8,128)S(1)} %get-tuple-element.20.labels, bf16[224,448]{1,0:T(8,128)(2,1)S(1)} %get-tuple-element.24.w0, ...), custom_call_target="tpu_custom_call" | custom-call | flops 1387266048 | bytes 21676032 | tf_op jit(solution)/shard_map/pallas_call | solution.py:82
  47.4 1.9 %collective-permute-start.5 = (bf16[112,1152]{1,0:T(8,128)(2,1)S(1)}, bf16[112,1152]{1,0:T(8,128)(2,1)S(1)}, u32[]{:S(2)}, u32[]{:S(2)}) collective-permute-start(bf16[112,1152]{1,0:T(8,128)(2,1)S(1)} %get-tuple-element.28), channel_id=1, source_target_pairs={{0,2},{1,3},{2,4},{3,5},{4,6},{5,7},{6,0},{7,1},{8,10},{9,11},{10,... | collective-permute-start | bytes 774152 | tf_op jit(solution)/shard_map/ppermute | solution.py:53
  49.4 4.1 %collective-permute-start.6 = (bf16[112,1152]{1,0:T(8,128)(2,1)S(1)}, bf16[112,1152]{1,0:T(8,128)(2,1)S(1)}, u32[]{:S(2)}, u32[]{:S(2)}) collective-permute-start(bf16[112,1152]{1,0:T(8,128)(2,1)S(1)} %get-tuple-element.29), channel_id=1, source_target_pairs={{0,4},{1,5},{2,6},{3,7},{4,0},{5,1},{6,2},{7,3},{8,12},{9,13},{10,... | collective-permute-start | bytes 774152 | tf_op jit(solution)/shard_map/ppermute | solution.py:53
  53.4 4.5 %collective-permute-start.7 = (bf16[112,1152]{1,0:T(8,128)(2,1)S(1)}, bf16[112,1152]{1,0:T(8,128)(2,1)S(1)}, u32[]{:S(2)}, u32[]{:S(2)}) collective-permute-start(bf16[112,1152]{1,0:T(8,128)(2,1)S(1)} %get-tuple-element.30), channel_id=1, source_target_pairs={{0,6},{1,7},{2,0},{3,1},{4,2},{5,3},{6,4},{7,5},{8,14},{9,15},{10,... | collective-permute-start | bytes 774152 | tf_op jit(solution)/shard_map/ppermute | solution.py:53
  57.9 1.0 %collective-permute-done.8.came = bf16[240,1152]{1,0:T(8,128)(2,1)S(1)} collective-permute-done((bf16[240,1152]{1,0:T(8,128)(2,1)S(1)}, bf16[240,1152]{1,0:T(8,128)(2,1)S(1)}, u32[]{:S(2)}, u32[]{:S(2)}) %collective-permute-start.8) | collective-permute-done | bytes 552992 | tf_op jit(solution)/shard_map/ppermute | solution.py:63
  58.9 4.0 %collective-permute-start.9 = (bf16[128,1152]{1,0:T(8,128)(2,1)S(1)}, bf16[128,1152]{1,0:T(8,128)(2,1)S(1)}, u32[]{:S(2)}, u32[]{:S(2)}) collective-permute-start(bf16[128,1152]{1,0:T(8,128)(2,1)S(1)} %shard_map.109), channel_id=1, source_target_pairs={{0,8},{1,9},{2,10},{3,11},{4,12},{5,13},{6,14},{7,15},{8,0},{9,1},... | collective-permute-start | bytes 884744 | tf_op jit(solution)/shard_map/ppermute | solution.py:53
  62.9 0.0 collective-permute-done.5.one
  62.9 0.0 collective-permute-done.6.two
  63.0 3.2 %collective-permute-done.7.three = bf16[112,1152]{1,0:T(8,128)(2,1)S(1)} collective-permute-done((bf16[112,1152]{1,0:T(8,128)(2,1)S(1)}, bf16[112,1152]{1,0:T(8,128)(2,1)S(1)}, u32[]{:S(2)}, u32[]{:S(2)}) %collective-permute-start.7) | collective-permute-done | bytes 258080 | tf_op jit(solution)/shard_map/ppermute | solution.py:53
  66.1 0.9 %shard_map.108 = (f32[112,1152]{1,0:T(8,128)}, f32[8,128]{1,0:T(8,128)S(1)}) custom-call(f32[112,1152]{1,0:T(8,128)S(1)} %get-tuple-element.27.kept, bf16[112,1152]{1,0:T(8,128)(2,1)S(1)} %collective-permute-done.5.one, bf16[112,1152]{1,0:T(8,128)(2,1)S(1)} %collective-permute-done.6.two, bf16[112,1152]{1,0:T(8,128)(2,1)S(1)} %collective-permute-done.7.three), custom_call_target="tpu_custom_call" | custom-call | flops 9248440320 | bytes 144506880 | tf_op jit(solution)/shard_map/pallas_call | solution.py:82
  67.1 3.7 %collective-permute-done.9.crossed = bf16[128,1152]{1,0:T(8,128)(2,1)S(1)} collective-permute-done((bf16[128,1152]{1,0:T(8,128)(2,1)S(1)}, bf16[128,1152]{1,0:T(8,128)(2,1)S(1)}, u32[]{:S(2)}, u32[]{:S(2)}) %collective-permute-start.9) | collective-permute-done | bytes 294944 | tf_op jit(solution)/shard_map/ppermute | solution.py:53
  70.7 0.9 %shard_map.110 = (f32[112,1152]{1,0:T(8,128)}, f32[1,112]{1,0:T(1,128)}) custom-call(f32[224,1152]{1,0:T(8,128)S(1)} %get-tuple-element.32.late, f32[8,128]{1,0:T(8,128)S(1)} %get-tuple-element.26.token.late_rows, bf16[240,1152]{1,0:T(8,128)(2,1)S(1)} %collective-permute-done.8.came, bf16[128,1152]{1,0:T(8,128)(2,1)S(1)} %collective-permute-done.9.crossed, ...), custom_call_target="tpu_custom_call" | custom-call | flops 129024 | bytes 2016 | tf_op jit(solution)/shard_map/pallas_call | solution.py:82
  (2 shorter events, 0.1 us)
Async XLA Ops:
  0.6 31.9 %collective-permute-start = (bf16[112,1152]{1,0:T(8,128)(2,1)}, bf16[112,1152]{1,0:T(8,128)(2,1)S(1)}, u32[]{:S(2)}, u32[]{:S(2)}) collective-permute-start(bf16[112,1152]{1,0:T(8,128)(2,1)} %text.1), channel_id=1, source_target_pairs={{0,8},{1,9},{2,10},{3,11},{4,12},{5,13},{6,14},{7,15},{8,0},{9,1},... | collective-permute-start | bytes 774152 | tf_op jit(solution)/shard_map/ppermute | solution.py:53
  5.6 28.5 %collective-permute-start.3 = (bf16[112,1152]{1,0:T(8,128)(2,1)}, bf16[112,1152]{1,0:T(8,128)(2,1)S(1)}, u32[]{:S(2)}, u32[]{:S(2)}) collective-permute-start(bf16[112,1152]{1,0:T(8,128)(2,1)} %text.1), channel_id=1, source_target_pairs={{0,24},{1,25},{2,26},{3,27},{4,28},{5,29},{6,30},{7,31},{8,16},{9,... | collective-permute-start | bytes 774152 | tf_op jit(solution)/shard_map/ppermute | solution.py:63
  9.3 24.7 %collective-permute-start.2 = (bf16[112,1152]{1,0:T(8,128)(2,1)}, bf16[112,1152]{1,0:T(8,128)(2,1)S(1)}, u32[]{:S(2)}, u32[]{:S(2)}) collective-permute-start(bf16[112,1152]{1,0:T(8,128)(2,1)} %text.1), channel_id=1, source_target_pairs={{0,16},{1,17},{2,18},{3,19},{4,20},{5,21},{6,22},{7,23},{8,24},{9,... | collective-permute-start | bytes 774152 | tf_op jit(solution)/shard_map/ppermute | solution.py:63
  28.6 8.1 %collective-permute-start.1 = (bf16[448,1152]{1,0:T(8,128)(2,1)S(1)}, bf16[448,1152]{1,0:T(8,128)(2,1)S(1)}, u32[]{:S(2)}, u32[]{:S(2)}) collective-permute-start(bf16[448,1152]{1,0:T(8,128)(2,1)S(1)} %all_gather.3.images.own), channel_id=1, source_target_pairs={{0,1},{1,0},{2,3},{3,2},{4,5},{5,4},{6,7},{7,6},{8,9},{9,8},{10,11... | collective-permute-start | bytes 3096584 | tf_op jit(solution)/shard_map/ppermute | solution.py:53
  34.1 2.7 %copy-start = (f32[112,1152]{1,0:T(8,128)S(1)}, f32[112,1152]{1,0:T(8,128)}, u32[]{:S(2)}) copy-start(f32[112,1152]{1,0:T(8,128)} %acc.1) | copy-start | bytes 1548292
  34.2 10.4 %collective-permute-start.4 = (bf16[448,1152]{1,0:T(8,128)(2,1)S(1)}, bf16[448,1152]{1,0:T(8,128)(2,1)S(1)}, u32[]{:S(2)}, u32[]{:S(2)}) collective-permute-start(bf16[448,1152]{1,0:T(8,128)(2,1)S(1)} %shard_map.105.texts), channel_id=1, source_target_pairs={{0,1},{1,0},{2,3},{3,2},{4,5},{5,4},{6,7},{7,6},{8,9},{9,8},{10,11... | collective-permute-start | bytes 3096584 | tf_op jit(solution)/shard_map/ppermute | solution.py:53
  38.6 20.3 %collective-permute-start.8 = (bf16[240,1152]{1,0:T(8,128)(2,1)S(1)}, bf16[240,1152]{1,0:T(8,128)(2,1)S(1)}, u32[]{:S(2)}, u32[]{:S(2)}) collective-permute-start(bf16[240,1152]{1,0:T(8,128)(2,1)S(1)} %get-tuple-element.33), channel_id=1, source_target_pairs={{0,16},{1,17},{2,18},{3,19},{4,20},{5,21},{6,22},{7,23},{8,24},{9,... | collective-permute-start | bytes 1658888 | tf_op jit(solution)/shard_map/ppermute | solution.py:63
  47.4 15.5 %collective-permute-start.5 = (bf16[112,1152]{1,0:T(8,128)(2,1)S(1)}, bf16[112,1152]{1,0:T(8,128)(2,1)S(1)}, u32[]{:S(2)}, u32[]{:S(2)}) collective-permute-start(bf16[112,1152]{1,0:T(8,128)(2,1)S(1)} %get-tuple-element.28), channel_id=1, source_target_pairs={{0,2},{1,3},{2,4},{3,5},{4,6},{5,7},{6,0},{7,1},{8,10},{9,11},{10,... | collective-permute-start | bytes 774152 | tf_op jit(solution)/shard_map/ppermute | solution.py:53
  49.4 13.6 %collective-permute-start.6 = (bf16[112,1152]{1,0:T(8,128)(2,1)S(1)}, bf16[112,1152]{1,0:T(8,128)(2,1)S(1)}, u32[]{:S(2)}, u32[]{:S(2)}) collective-permute-start(bf16[112,1152]{1,0:T(8,128)(2,1)S(1)} %get-tuple-element.29), channel_id=1, source_target_pairs={{0,4},{1,5},{2,6},{3,7},{4,0},{5,1},{6,2},{7,3},{8,12},{9,13},{10,... | collective-permute-start | bytes 774152 | tf_op jit(solution)/shard_map/ppermute | solution.py:53
  53.4 12.7 %collective-permute-start.7 = (bf16[112,1152]{1,0:T(8,128)(2,1)S(1)}, bf16[112,1152]{1,0:T(8,128)(2,1)S(1)}, u32[]{:S(2)}, u32[]{:S(2)}) collective-permute-start(bf16[112,1152]{1,0:T(8,128)(2,1)S(1)} %get-tuple-element.30), channel_id=1, source_target_pairs={{0,6},{1,7},{2,0},{3,1},{4,2},{5,3},{6,4},{7,5},{8,14},{9,15},{10,... | collective-permute-start | bytes 774152 | tf_op jit(solution)/shard_map/ppermute | solution.py:53
  58.9 11.8 %collective-permute-start.9 = (bf16[128,1152]{1,0:T(8,128)(2,1)S(1)}, bf16[128,1152]{1,0:T(8,128)(2,1)S(1)}, u32[]{:S(2)}, u32[]{:S(2)}) collective-permute-start(bf16[128,1152]{1,0:T(8,128)(2,1)S(1)} %shard_map.109), channel_id=1, source_target_pairs={{0,8},{1,9},{2,10},{3,11},{4,12},{5,13},{6,14},{7,15},{8,0},{9,1},... | collective-permute-start | bytes 884744 | tf_op jit(solution)/shard_map/ppermute | solution.py:53

commit v7 on v6

--- a/solution.py
+++ b/solution.py
@@ -13,6 +13,7 @@
 LAG = XH * ROWS
 SPAN = XH * Y * CORE * ROWS
 TAIL = 16
+STEPS = (0, 2, 1, 3)
 LOG2E = 1.4426950408889634
 LN2 = 0.6931471805599453
 CHUNK = 32
@@ -244,7 +245,7 @@
     total[...] += image_part(w_b[...], beside[...])
     factor = given[0:1, 0:1]
     y = (member // CORE) & (Y - 1)
-    for step, out in enumerate((kept, one, two, three)):
+    for step, out in zip(STEPS, (kept, one, two, three)):
         start = pl.multiple_of(((y + step) & (Y - 1)) * ROWS, 16)
         out[...] = (factor * total[pl.ds(start, ROWS), :]).astype(out.dtype)
 
@@ -317,7 +318,7 @@
         6 * big,
         [held(2 * LAG, SETS, F32), held(2 * LAG, SETS, BF16), held(2 * LAG, SETS, BF16), held(SETS, width, F32)],
     )
-    arrived = [to_member(part, along_y(i + 1)) for i, part in enumerate(sent)]
+    arrived = [to_member(part, along_y(i)) for i, part in zip(STEPS[1:], sent)]
     (crossing,) = call(across, [shape(ROWS + TAIL, width, BF16)], [late, late_rows, came], ROWS * width)
     crossed = to_member(crossing, across_x)
     image_grad, token = call(

time: 72.1 us -> 72.1 us (level)
  no operation moved by 1% of the time
where the time goes in v7:
time: 72.1 us; the launch traced here: 71.6 us
  starting transfers between devices  34.7 us (48%)
  blocking collectives  15.4 us (21%)
  Pallas kernels  10.1 us (14%)
  waiting for transfers between devices  8.57 us (12%)
  between operations  2.76 us (4%)
    ppermute x7, starting transfers between devices, to_member(): return lax.ppermute(block, 'grp', member_route(move))  23.1 us
    all_gather x1, blocking collectives, gather_y(): return lax.all_gather(block, 'grp', axis_index_groups=groups, tiled=True)  15.4 us
    ppermute x3, starting transfers between devices, to_next_group(): return lax.ppermute(block, ('blk', 'grp'), route)  11.6 us
    pallas_call x8, Pallas kernels, call(): pl.pallas_call(body, out_shape=outs, in_specs=[HBM if i < far else SMEM i...  10.1 us
    ppermute x7, waiting for transfers between devices, to_member(): return lax.ppermute(block, 'grp', member_route(move))  6.94 us
    ppermute x3, waiting for transfers between devices, to_next_group(): return lax.ppermute(block, ('blk', 'grp'), route)  1.63 us
  transfers between devices with their start and end apart: 10, of which 3 were waited for; matrix products, arithmetic and copies ran while one was open for 0% of the time, Pallas kernels for 13%

profile of v7, /device:TPU:8, one launch (start us, length us, event | category | flops | bytes accessed | tf_op | source)
XLA Modules:
  0.0 71.6 jit_solution(10723165994453893297)
XLA Ops:
  0.6 4.9 %collective-permute-start = (bf16[112,1152]{1,0:T(8,128)(2,1)}, bf16[112,1152]{1,0:T(8,128)(2,1)S(1)}, u32[]{:S(2)}, u32[]{:S(2)}) collective-permute-start(bf16[112,1152]{1,0:T(8,128)(2,1)} %text.1), channel_id=1, source_target_pairs={{0,8},{1,9},{2,10},{3,11},{4,12},{5,13},{6,14},{7,15},{8,0},{9,1},... | collective-permute-start | bytes 774152 | tf_op jit(solution)/shard_map/ppermute | solution.py:54
  5.6 3.8 %collective-permute-start.3 = (bf16[112,1152]{1,0:T(8,128)(2,1)}, bf16[112,1152]{1,0:T(8,128)(2,1)S(1)}, u32[]{:S(2)}, u32[]{:S(2)}) collective-permute-start(bf16[112,1152]{1,0:T(8,128)(2,1)} %text.1), channel_id=1, source_target_pairs={{0,24},{1,25},{2,26},{3,27},{4,28},{5,29},{6,30},{7,31},{8,16},{9,... | collective-permute-start | bytes 774152 | tf_op jit(solution)/shard_map/ppermute | solution.py:64
  9.3 3.8 %collective-permute-start.2 = (bf16[112,1152]{1,0:T(8,128)(2,1)}, bf16[112,1152]{1,0:T(8,128)(2,1)S(1)}, u32[]{:S(2)}, u32[]{:S(2)}) collective-permute-start(bf16[112,1152]{1,0:T(8,128)(2,1)} %text.1), channel_id=1, source_target_pairs={{0,16},{1,17},{2,18},{3,19},{4,20},{5,21},{6,22},{7,23},{8,24},{9,... | collective-permute-start | bytes 774152 | tf_op jit(solution)/shard_map/ppermute | solution.py:64
  13.2 15.4 %all_gather.3.images.own = bf16[448,1152]{1,0:T(8,128)(2,1)S(1)} all-gather(bf16[112,1152]{1,0:T(8,128)(2,1)} %param.8), channel_id=1, replica_groups={{0,2,4,6},{1,3,5,7},{8,10,12,14},{9,11,13,15},{16,18,20,22},{17,19,21,2..., dimensions={0}, use_global_device_ids=true | all-gather | bytes 1290240 | tf_op jit(solution)/shard_map/all_gather | solution.py:69
  28.6 1.9 %collective-permute-start.1 = (bf16[448,1152]{1,0:T(8,128)(2,1)S(1)}, bf16[448,1152]{1,0:T(8,128)(2,1)S(1)}, u32[]{:S(2)}, u32[]{:S(2)}) collective-permute-start(bf16[448,1152]{1,0:T(8,128)(2,1)S(1)} %all_gather.3.images.own), channel_id=1, source_target_pairs={{0,1},{1,0},{2,3},{3,2},{4,5},{5,4},{6,7},{7,6},{8,9},{9,8},{10,11... | collective-permute-start | bytes 3096584 | tf_op jit(solution)/shard_map/ppermute | solution.py:54
  32.5 0.1 maximum_bitcast_fusion.given
  32.5 0.0 collective-permute-done.t1
  32.6 1.5 %shard_map.103 = (bf16[224,1152]{1,0:T(8,128)(2,1)S(1)}, f32[224,448]{1,0:T(8,128)S(1)}, s32[8,448]{1,0:T(8,128)S(1)}, f32[1,112]{1,0:T(1,128)S(1)}) custom-call(s32[14,128]{1,0:T(8,128)} %bitcast.6, bf16[112,1152]{1,0:T(8,128)(2,1)} %text.1, f32[1,112]{1,0:T(1,128)} %bitcast.7, f32[1,128]{1,0:T(1,128)S(1)} %maximum_bitcast_fusion.given, ...), custom_call_target="tpu_custom_call" | custom-call | flops 462422016 | bytes 7225344 | tf_op jit(solution)/shard_map/pallas_call | solution.py:83
  34.1 0.0 collective-permute-done.3.d
  34.1 0.0 collective-permute-done.2.z
  34.1 0.0 copy-start
  34.1 0.1 shard_map.105.texts
  34.2 2.5 %collective-permute-start.4 = (bf16[448,1152]{1,0:T(8,128)(2,1)S(1)}, bf16[448,1152]{1,0:T(8,128)(2,1)S(1)}, u32[]{:S(2)}, u32[]{:S(2)}) collective-permute-start(bf16[448,1152]{1,0:T(8,128)(2,1)S(1)} %shard_map.105.texts), channel_id=1, source_target_pairs={{0,1},{1,0},{2,3},{3,2},{4,5},{5,4},{6,7},{7,6},{8,9},{9,8},{10,11... | collective-permute-start | bytes 3096584 | tf_op jit(solution)/shard_map/ppermute | solution.py:54
  36.7 0.0 collective-permute-done.1.other
  36.7 0.0 copy-done
  36.7 1.8 %shard_map.104 = (bf16[224,448]{1,0:T(8,128)(2,1)S(1)}, bf16[240,1152]{1,0:T(8,128)(2,1)S(1)}) custom-call(f32[1,128]{1,0:T(1,128)S(1)} %maximum_bitcast_fusion.given, s32[8,448]{1,0:T(8,128)S(1)} %get-tuple-element.20.labels, bf16[224,1152]{1,0:T(8,128)(2,1)S(1)} %get-tuple-element.21.texts.texts0, f32[224,448]{1,0:T(8,128)S(1)} %get-tuple-element.22.s_own, ...), custom_call_target="tpu_custom_call" | custom-call | flops 693633024 | bytes 10838016 | tf_op jit(solution)/shard_map/pallas_call | solution.py:83
  38.6 4.0 %collective-permute-start.8 = (bf16[240,1152]{1,0:T(8,128)(2,1)S(1)}, bf16[240,1152]{1,0:T(8,128)(2,1)S(1)}, u32[]{:S(2)}, u32[]{:S(2)}) collective-permute-start(bf16[240,1152]{1,0:T(8,128)(2,1)S(1)} %get-tuple-element.33), channel_id=1, source_target_pairs={{0,16},{1,17},{2,18},{3,19},{4,20},{5,21},{6,22},{7,23},{8,24},{9,... | collective-permute-start | bytes 1658888 | tf_op jit(solution)/shard_map/ppermute | solution.py:64
  42.5 2.0 %shard_map.106 = (bf16[224,448]{1,0:T(8,128)(2,1)S(1)}, f32[224,1152]{1,0:T(8,128)S(1)}, f32[8,128]{1,0:T(8,128)S(1)}) custom-call(f32[1,128]{1,0:T(1,128)S(1)} %maximum_bitcast_fusion.given, s32[8,448]{1,0:T(8,128)S(1)} %get-tuple-element.20.labels, bf16[448,1152]{1,0:T(8,128)(2,1)S(1)} %shard_map.105.texts, bf16[448,1152]{1,0:T(8,128)(2,1)S(1)} %all_gather.3.images.own, ...), custom_call_target="tpu_custom_call" | custom-call | flops 924844032 | bytes 14450688 | tf_op jit(solution)/shard_map/pallas_call | solution.py:83
  44.6 0.0 collective-permute-done.4.beside
  44.6 2.8 %shard_map.107 = (f32[112,1152]{1,0:T(8,128)S(1)}, bf16[112,1152]{1,0:T(8,128)(2,1)S(1)}, bf16[112,1152]{1,0:T(8,128)(2,1)S(1)}, bf16[112,1152]{1,0:T(8,128)(2,1)S(1)}) custom-call(f32[1,128]{1,0:T(1,128)S(1)} %maximum_bitcast_fusion.given, s32[8,448]{1,0:T(8,128)S(1)} %get-tuple-element.20.labels, bf16[224,448]{1,0:T(8,128)(2,1)S(1)} %get-tuple-element.24.w0, ...), custom_call_target="tpu_custom_call" | custom-call | flops 1387266048 | bytes 21676032 | tf_op jit(solution)/shard_map/pallas_call | solution.py:83
  47.4 4.0 %collective-permute-start.5 = (bf16[112,1152]{1,0:T(8,128)(2,1)S(1)}, bf16[112,1152]{1,0:T(8,128)(2,1)S(1)}, u32[]{:S(2)}, u32[]{:S(2)}) collective-permute-start(bf16[112,1152]{1,0:T(8,128)(2,1)S(1)} %get-tuple-element.28), channel_id=1, source_target_pairs={{0,4},{1,5},{2,6},{3,7},{4,0},{5,1},{6,2},{7,3},{8,12},{9,13},{10,... | collective-permute-start | bytes 774152 | tf_op jit(solution)/shard_map/ppermute | solution.py:54
  51.4 1.9 %collective-permute-start.6 = (bf16[112,1152]{1,0:T(8,128)(2,1)S(1)}, bf16[112,1152]{1,0:T(8,128)(2,1)S(1)}, u32[]{:S(2)}, u32[]{:S(2)}) collective-permute-start(bf16[112,1152]{1,0:T(8,128)(2,1)S(1)} %get-tuple-element.29), channel_id=1, source_target_pairs={{0,2},{1,3},{2,4},{3,5},{4,6},{5,7},{6,0},{7,1},{8,10},{9,11},{10,... | collective-permute-start | bytes 774152 | tf_op jit(solution)/shard_map/ppermute | solution.py:54
  53.3 3.9 %collective-permute-start.7 = (bf16[112,1152]{1,0:T(8,128)(2,1)S(1)}, bf16[112,1152]{1,0:T(8,128)(2,1)S(1)}, u32[]{:S(2)}, u32[]{:S(2)}) collective-permute-start(bf16[112,1152]{1,0:T(8,128)(2,1)S(1)} %get-tuple-element.30), channel_id=1, source_target_pairs={{0,6},{1,7},{2,0},{3,1},{4,2},{5,3},{6,4},{7,5},{8,14},{9,15},{10,... | collective-permute-start | bytes 774152 | tf_op jit(solution)/shard_map/ppermute | solution.py:54
  57.3 1.6 %collective-permute-done.8.came = bf16[240,1152]{1,0:T(8,128)(2,1)S(1)} collective-permute-done((bf16[240,1152]{1,0:T(8,128)(2,1)S(1)}, bf16[240,1152]{1,0:T(8,128)(2,1)S(1)}, u32[]{:S(2)}, u32[]{:S(2)}) %collective-permute-start.8) | collective-permute-done | bytes 552992 | tf_op jit(solution)/shard_map/ppermute | solution.py:64
  58.9 3.9 %collective-permute-start.9 = (bf16[128,1152]{1,0:T(8,128)(2,1)S(1)}, bf16[128,1152]{1,0:T(8,128)(2,1)S(1)}, u32[]{:S(2)}, u32[]{:S(2)}) collective-permute-start(bf16[128,1152]{1,0:T(8,128)(2,1)S(1)} %shard_map.109), channel_id=1, source_target_pairs={{0,8},{1,9},{2,10},{3,11},{4,12},{5,13},{6,14},{7,15},{8,0},{9,1},... | collective-permute-start | bytes 884744 | tf_op jit(solution)/shard_map/ppermute | solution.py:54
  62.9 0.0 collective-permute-done.5.one
  62.9 0.0 collective-permute-done.6.two
  62.9 1.3 %collective-permute-done.7.three = bf16[112,1152]{1,0:T(8,128)(2,1)S(1)} collective-permute-done((bf16[112,1152]{1,0:T(8,128)(2,1)S(1)}, bf16[112,1152]{1,0:T(8,128)(2,1)S(1)}, u32[]{:S(2)}, u32[]{:S(2)}) %collective-permute-start.7) | collective-permute-done | bytes 258080 | tf_op jit(solution)/shard_map/ppermute | solution.py:54
  64.2 0.9 %shard_map.108 = (f32[112,1152]{1,0:T(8,128)}, f32[8,128]{1,0:T(8,128)S(1)}) custom-call(f32[112,1152]{1,0:T(8,128)S(1)} %get-tuple-element.27.kept, bf16[112,1152]{1,0:T(8,128)(2,1)S(1)} %collective-permute-done.5.one, bf16[112,1152]{1,0:T(8,128)(2,1)S(1)} %collective-permute-done.6.two, bf16[112,1152]{1,0:T(8,128)(2,1)S(1)} %collective-permute-done.7.three), custom_call_target="tpu_custom_call" | custom-call | flops 9248440320 | bytes 144506880 | tf_op jit(solution)/shard_map/pallas_call | solution.py:83
  65.1 5.6 %collective-permute-done.9.crossed = bf16[128,1152]{1,0:T(8,128)(2,1)S(1)} collective-permute-done((bf16[128,1152]{1,0:T(8,128)(2,1)S(1)}, bf16[128,1152]{1,0:T(8,128)(2,1)S(1)}, u32[]{:S(2)}, u32[]{:S(2)}) %collective-permute-start.9) | collective-permute-done | bytes 294944 | tf_op jit(solution)/shard_map/ppermute | solution.py:54
  70.7 0.9 %shard_map.110 = (f32[112,1152]{1,0:T(8,128)}, f32[1,112]{1,0:T(1,128)}) custom-call(f32[224,1152]{1,0:T(8,128)S(1)} %get-tuple-element.32.late, f32[8,128]{1,0:T(8,128)S(1)} %get-tuple-element.26.token.late_rows, bf16[240,1152]{1,0:T(8,128)(2,1)S(1)} %collective-permute-done.8.came, bf16[128,1152]{1,0:T(8,128)(2,1)S(1)} %collective-permute-done.9.crossed, ...), custom_call_target="tpu_custom_call" | custom-call | flops 129024 | bytes 2016 | tf_op jit(solution)/shard_map/pallas_call | solution.py:83
  (2 shorter events, 0.1 us)
Async XLA Ops:
  0.6 31.9 %collective-permute-start = (bf16[112,1152]{1,0:T(8,128)(2,1)}, bf16[112,1152]{1,0:T(8,128)(2,1)S(1)}, u32[]{:S(2)}, u32[]{:S(2)}) collective-permute-start(bf16[112,1152]{1,0:T(8,128)(2,1)} %text.1), channel_id=1, source_target_pairs={{0,8},{1,9},{2,10},{3,11},{4,12},{5,13},{6,14},{7,15},{8,0},{9,1},... | collective-permute-start | bytes 774152 | tf_op jit(solution)/shard_map/ppermute | solution.py:54
  5.6 28.5 %collective-permute-start.3 = (bf16[112,1152]{1,0:T(8,128)(2,1)}, bf16[112,1152]{1,0:T(8,128)(2,1)S(1)}, u32[]{:S(2)}, u32[]{:S(2)}) collective-permute-start(bf16[112,1152]{1,0:T(8,128)(2,1)} %text.1), channel_id=1, source_target_pairs={{0,24},{1,25},{2,26},{3,27},{4,28},{5,29},{6,30},{7,31},{8,16},{9,... | collective-permute-start | bytes 774152 | tf_op jit(solution)/shard_map/ppermute | solution.py:64
  9.3 24.7 %collective-permute-start.2 = (bf16[112,1152]{1,0:T(8,128)(2,1)}, bf16[112,1152]{1,0:T(8,128)(2,1)S(1)}, u32[]{:S(2)}, u32[]{:S(2)}) collective-permute-start(bf16[112,1152]{1,0:T(8,128)(2,1)} %text.1), channel_id=1, source_target_pairs={{0,16},{1,17},{2,18},{3,19},{4,20},{5,21},{6,22},{7,23},{8,24},{9,... | collective-permute-start | bytes 774152 | tf_op jit(solution)/shard_map/ppermute | solution.py:64
  28.6 8.1 %collective-permute-start.1 = (bf16[448,1152]{1,0:T(8,128)(2,1)S(1)}, bf16[448,1152]{1,0:T(8,128)(2,1)S(1)}, u32[]{:S(2)}, u32[]{:S(2)}) collective-permute-start(bf16[448,1152]{1,0:T(8,128)(2,1)S(1)} %all_gather.3.images.own), channel_id=1, source_target_pairs={{0,1},{1,0},{2,3},{3,2},{4,5},{5,4},{6,7},{7,6},{8,9},{9,8},{10,11... | collective-permute-start | bytes 3096584 | tf_op jit(solution)/shard_map/ppermute | solution.py:54
  34.1 2.7 %copy-start = (f32[112,1152]{1,0:T(8,128)S(1)}, f32[112,1152]{1,0:T(8,128)}, u32[]{:S(2)}) copy-start(f32[112,1152]{1,0:T(8,128)} %acc.1) | copy-start | bytes 1548292
  34.2 10.4 %collective-permute-start.4 = (bf16[448,1152]{1,0:T(8,128)(2,1)S(1)}, bf16[448,1152]{1,0:T(8,128)(2,1)S(1)}, u32[]{:S(2)}, u32[]{:S(2)}) collective-permute-start(bf16[448,1152]{1,0:T(8,128)(2,1)S(1)} %shard_map.105.texts), channel_id=1, source_target_pairs={{0,1},{1,0},{2,3},{3,2},{4,5},{5,4},{6,7},{7,6},{8,9},{9,8},{10,11... | collective-permute-start | bytes 3096584 | tf_op jit(solution)/shard_map/ppermute | solution.py:54
  38.6 20.3 %collective-permute-start.8 = (bf16[240,1152]{1,0:T(8,128)(2,1)S(1)}, bf16[240,1152]{1,0:T(8,128)(2,1)S(1)}, u32[]{:S(2)}, u32[]{:S(2)}) collective-permute-start(bf16[240,1152]{1,0:T(8,128)(2,1)S(1)} %get-tuple-element.33), channel_id=1, source_target_pairs={{0,16},{1,17},{2,18},{3,19},{4,20},{5,21},{6,22},{7,23},{8,24},{9,... | collective-permute-start | bytes 1658888 | tf_op jit(solution)/shard_map/ppermute | solution.py:64
  47.4 15.4 %collective-permute-start.5 = (bf16[112,1152]{1,0:T(8,128)(2,1)S(1)}, bf16[112,1152]{1,0:T(8,128)(2,1)S(1)}, u32[]{:S(2)}, u32[]{:S(2)}) collective-permute-start(bf16[112,1152]{1,0:T(8,128)(2,1)S(1)} %get-tuple-element.28), channel_id=1, source_target_pairs={{0,4},{1,5},{2,6},{3,7},{4,0},{5,1},{6,2},{7,3},{8,12},{9,13},{10,... | collective-permute-start | bytes 774152 | tf_op jit(solution)/shard_map/ppermute | solution.py:54
  51.4 11.5 %collective-permute-start.6 = (bf16[112,1152]{1,0:T(8,128)(2,1)S(1)}, bf16[112,1152]{1,0:T(8,128)(2,1)S(1)}, u32[]{:S(2)}, u32[]{:S(2)}) collective-permute-start(bf16[112,1152]{1,0:T(8,128)(2,1)S(1)} %get-tuple-element.29), channel_id=1, source_target_pairs={{0,2},{1,3},{2,4},{3,5},{4,6},{5,7},{6,0},{7,1},{8,10},{9,11},{10,... | collective-permute-start | bytes 774152 | tf_op jit(solution)/shard_map/ppermute | solution.py:54
  53.3 10.9 %collective-permute-start.7 = (bf16[112,1152]{1,0:T(8,128)(2,1)S(1)}, bf16[112,1152]{1,0:T(8,128)(2,1)S(1)}, u32[]{:S(2)}, u32[]{:S(2)}) collective-permute-start(bf16[112,1152]{1,0:T(8,128)(2,1)S(1)} %get-tuple-element.30), channel_id=1, source_target_pairs={{0,6},{1,7},{2,0},{3,1},{4,2},{5,3},{6,4},{7,5},{8,14},{9,15},{10,... | collective-permute-start | bytes 774152 | tf_op jit(solution)/shard_map/ppermute | solution.py:54
  58.9 11.8 %collective-permute-start.9 = (bf16[128,1152]{1,0:T(8,128)(2,1)S(1)}, bf16[128,1152]{1,0:T(8,128)(2,1)S(1)}, u32[]{:S(2)}, u32[]{:S(2)}) collective-permute-start(bf16[128,1152]{1,0:T(8,128)(2,1)S(1)} %shard_map.109), channel_id=1, source_target_pairs={{0,8},{1,9},{2,10},{3,11},{4,12},{5,13},{6,14},{7,15},{8,0},{9,1},... | collective-permute-start | bytes 884744 | tf_op jit(solution)/shard_map/ppermute | solution.py:54
